TPU v7x, 32 devices: a whole 2x2x4 slice. The times are simulated.
32 devices in a mesh: stream: 2 (over x), expert: 16 (over z, y, core).
Axes of the slice: x: 2, y: 2, z: 4, core: 2. Of those that a mesh axis runs over, the one named last changes fastest.
Arguments:
- tokens: bfloat16 [2048, 2048], P(('stream', 'expert')), may hold values from -6 to 6
- route_gates: float32 [2048, 8], P(('stream', 'expert')), may hold values from 0.1 to 1
- expert_ids: int32 [2048, 8], P(('stream', 'expert')), may hold values from 0 to 15, as said below
- slot_index: int32 [2048, 8], P(('stream', 'expert')), may hold values from -1 to 31, as said below
- gate_quant: bfloat16 [16, 2048, 1024], P('expert', None, 'stream'), may hold values from -0.125 to 0.125
- up_quant: bfloat16 [16, 2048, 1024], P('expert', None, 'stream'), may hold values from -0.125 to 0.125
- down_quant: bfloat16 [16, 2048, 1024], P('expert', None, 'stream'), may hold values from -0.1875 to 0.1875
- gate_scale: float32 [16, 16, 8], P('expert', None, 'stream'), may hold values from 0.5 to 2
- up_scale: float32 [16, 16, 8], P('expert', None, 'stream'), may hold values from 0.5 to 2
- down_scale: float32 [16, 16, 8], P('expert', None, 'stream'), may hold values from 0.5 to 2
Outputs:
- mixed: bfloat16 [2048, 2048], P(('stream', 'expert'))
Inputs may be any that keep to these rules, and one draw needn't show every extreme that they name: `expert_ids`: the 8 ids of one token differ. `slot_index`: among the choices of one device's 64 tokens that name one expert, taken in token order, the first 32 get places 0, 1, ... and the rest get -1. In every draw some expert gets all 32 places from every device.
All inputs are finite; a program needn't handle non-finite values.
Results may differ from a plain program's by a relative error of at most 0.0076.
Values may be sent and summed in bfloat16 or wider, within the bound.
No kernel may reach another device: no remote copies, remote signals or barrier semaphores. Data moves between devices by JAX's collectives and lax.ppermute only.
A program may use at most 64 MiB of HBM per device.

v0:
```python
import jax
import jax.numpy as jnp
from jax import lax
from jax.sharding import PartitionSpec as P

QB = 128


def dequantize(quant, scales):
    expanded = jnp.repeat(jnp.repeat(scales, QB, axis=0), QB, axis=1)
    return (quant.astype(jnp.float32) * expanded).astype(jnp.bfloat16)


def local(
    tokens,
    route_gates,
    expert_ids,
    slot_index,
    gate_quant,
    up_quant,
    down_quant,
    gate_scale,
    up_scale,
    down_scale,
):
    experts = lax.axis_size("expert")
    tok_rows = tokens.shape[0]
    top_count = expert_ids.shape[1]
    width = tokens.shape[1]
    capacity = max(2, tok_rows * top_count // experts)
    row_count = experts * capacity
    is_kept = slot_index >= 0
    position = jnp.where(is_kept, expert_ids * capacity + slot_index, -1)
    selector = jnp.any(
        position[None, :, :] == jnp.arange(row_count, dtype=jnp.int32)[:, None, None], axis=2
    )
    outgoing = jnp.dot(selector.astype(jnp.bfloat16), tokens, preferred_element_type=jnp.float32)
    outgoing = outgoing.astype(jnp.bfloat16).reshape(experts, capacity, width)
    incoming = lax.all_to_all(outgoing, "expert", split_axis=0, concat_axis=0, tiled=True).reshape(
        row_count, width
    )
    w_gate = dequantize(gate_quant[0], gate_scale[0])
    w_up = dequantize(up_quant[0], up_scale[0])
    w_down = dequantize(down_quant[0], down_scale[0])
    gate_piece = lax.all_gather(w_gate, "stream", axis=1, tiled=True)
    up_piece = lax.all_gather(w_up, "stream", axis=1, tiled=True)
    down_piece = lax.all_gather(w_down, "stream", axis=1, tiled=True)
    gate_act = jnp.dot(incoming, gate_piece, preferred_element_type=jnp.float32)
    up_act = jnp.dot(incoming, up_piece, preferred_element_type=jnp.float32)
    hidden = (jax.nn.silu(gate_act) * up_act).astype(jnp.bfloat16)
    running = jnp.einsum("rf,df->rd", hidden, down_piece, preferred_element_type=jnp.float32)
    expert_out = running.astype(jnp.bfloat16).reshape(experts, capacity, width)
    returned = lax.all_to_all(
        expert_out, "expert", split_axis=0, concat_axis=0, tiled=True
    ).reshape(row_count, width)
    gather_at = jnp.where(is_kept, position, 0).reshape(-1)
    picked = jnp.take(returned, gather_at, axis=0).reshape(tok_rows, top_count, width)
    weighting = jnp.where(is_kept, route_gates, jnp.float32(0.0))
    mixed_out = jnp.sum(weighting[:, :, None] * picked.astype(jnp.float32), axis=1)
    return mixed_out.astype(jnp.bfloat16)


def solution(mesh):
    return jax.shard_map(
        local,
        mesh=mesh,
        in_specs=(
            P(("stream", "expert"), None),
            P(("stream", "expert"), None),
            P(("stream", "expert"), None),
            P(("stream", "expert"), None),
            P("expert", None, "stream"),
            P("expert", None, "stream"),
            P("expert", None, "stream"),
            P("expert", None, "stream"),
            P("expert", None, "stream"),
            P("expert", None, "stream"),
        ),
        out_specs=P(("stream", "expert"), None),
        check_vma=False,
    )
```

profile of v0, /device:TPU:13, one launch (start us, length us, event | category | flops | bytes accessed | tf_op | source)
XLA Modules:
  0.0 267.4 jit_solution(11418379356204455910)
XLA Ops:
  6.5 0.0 copy-start
  6.5 0.0 all-gather.4.cloned.1.call-start
  6.5 0.8 copy.27
  7.3 0.1 broadcast_in_dim.43
  7.4 0.0 copy-start.1
  7.4 4.7 %broadcast_in_dim.44 = f32[2048,4,128]{2,1,0:T(4,128)S(1)} broadcast(f32[2048,4]{1,0:T(8,128)S(1)} %bitcast.50), dimensions={0,1} | broadcast | bytes 4227072 | tf_op jit(solution)/shard_map/broadcast_in_dim | solution.py:10
  12.1 0.0 copy-done.1
  12.1 2.2 fusion.2
  14.3 0.0 copy-start.7
  14.3 0.0 all-gather.4.cloned.1.call-update
  14.3 0.0 all-gather.6.cloned.1.call-start
  14.3 0.6 copy-done.7
  15.0 0.1 copy.28
  15.0 0.1 broadcast_in_dim.45
  15.1 0.0 copy-start.2
  15.1 4.7 %broadcast_in_dim.46 = f32[2048,4,128]{2,1,0:T(4,128)S(1)} broadcast(f32[2048,4]{1,0:T(8,128)S(1)} %bitcast.51), dimensions={0,1} | broadcast | bytes 4227072 | tf_op jit(solution)/shard_map/broadcast_in_dim | solution.py:10
  19.8 0.0 copy-done.2
  19.8 2.2 fusion.1
  22.0 0.0 copy-start.4
  22.0 0.0 copy-start.5
  22.0 0.0 all-gather.6.cloned.1.call-update
  22.0 0.7 copy-done.4
  22.7 0.0 copy-done.5
  22.7 0.1 copy.26
  22.8 0.4 fusion.3
  23.2 0.0 copy-done
  23.2 2.1 convolution_convert_fusion.1
  25.3 0.0 copy-start.8
  25.3 6.7 %all-to-all-start = ((bf16[16,32,2048]{2,1,0:T(8,128)(2,1)}), bf16[16,32,2048]{2,1,0:T(8,128)(2,1)S(1)}, u32[]{:S(2)}, u32[]{:S(2)}) async-start(bf16[16,32,2048]{2,1,0:T(8,128)(2,1)} %bitcast), calls=%async_computation | async-start | bytes 4194304 | tf_op jit(solution)/shard_map/all_to_all | solution.py:39
  32.0 0.2 all-gather.8.cloned.1.call-start
  32.2 0.0 copy-done.8
  32.2 0.1 copy.29
  32.3 0.1 broadcast_in_dim.47
  32.4 0.0 copy-start.3
  32.4 4.7 %broadcast_in_dim.48 = f32[2048,4,128]{2,1,0:T(4,128)S(1)} broadcast(f32[2048,4]{1,0:T(8,128)S(1)} %bitcast.52), dimensions={0,1} | broadcast | bytes 4227072 | tf_op jit(solution)/shard_map/broadcast_in_dim | solution.py:10
  37.1 0.0 copy-done.3
  37.1 2.2 fusion
  39.3 0.0 all-gather.8.cloned.1.call-update
  39.3 40.1 %all-to-all-done = bf16[16,32,2048]{2,1,0:T(8,128)(2,1)S(1)} async-done(((bf16[16,32,2048]{2,1,0:T(8,128)(2,1)}), bf16[16,32,2048]{2,1,0:T(8,128)(2,1)S(1)}, u32[]{:S(2)}, u32[]{:S(2)}) %all-to-all-start) | async-done | bytes 2097184 | tf_op jit(solution)/shard_map/all_to_all | solution.py:39
  79.4 0.0 all-gather.4.cloned.1.call-done
  79.4 6.4 %fusion.5 = f32[512,1024]{1,0:T(8,128)} fusion(bf16[512,2048]{1,0:T(8,128)(2,1)S(1)} %bitcast.53, bf16[2048,1024]{1,0:T(8,128)(2,1)} %all-gather.4.cloned.1.call-done), kind=kOutput, calls=%fused_computation.23 | convolution fusion | flops 2147483648 | bytes 8388608 | tf_op jit(solution)/shard_map/dot_general | solution.py:48
  85.8 44.8 %all-gather.6.cloned.1.call-done = bf16[2048,1024]{1,0:T(8,128)(2,1)} async-done(((bf16[2048,512]{1,0:T(8,128)(2,1)}), bf16[2048,1024]{1,0:T(8,128)(2,1)}) %all-gather.6.cloned.1.call-update) | async-done | bytes 4194320 | tf_op jit(solution)/shard_map/all_gather | solution.py:46
  130.6 58.3 %all-gather.8.cloned.1.call-done = bf16[2048,1024]{1,0:T(8,128)(2,1)} async-done(((bf16[2048,512]{1,0:T(8,128)(2,1)}), bf16[2048,1024]{1,0:T(8,128)(2,1)}) %all-gather.8.cloned.1.call-update) | async-done | bytes 4194320 | tf_op jit(solution)/shard_map/all_gather | solution.py:47
  189.0 10.0 %convolution_convert_fusion = bf16[512,2048]{1,0:T(8,128)(2,1)} fusion(bf16[2048,1024]{1,0:T(8,128)(2,1)} %all-gather.8.cloned.1.call-done, f32[512,1024]{1,0:T(8,128)} %fusion.5, bf16[512,2048]{1,0:T(8,128)(2,1)S(1)} %bitcast.54, bf16[2048,1024]{1,0:T(8,128)(2,1)} %all-gather.6.cloned.1.call-done), kind=kOutput, calls=%fused_computation.8 | convolution fusion | flops 4299161600 | bytes 14680064 | tf_op jit(solution)/shard_map/rf,df->rd/dot_general | solution.py:51
  199.0 0.0 copy-start.6
  199.0 6.5 %all-to-all-start.1 = ((bf16[16,32,2048]{2,1,0:T(8,128)(2,1)}), bf16[16,32,2048]{2,1,0:T(8,128)(2,1)S(1)}, u32[]{:S(2)}, u32[]{:S(2)}) async-start(bf16[16,32,2048]{2,1,0:T(8,128)(2,1)} %bitcast.55), calls=%async_computation.1 | async-start | bytes 4194304 | tf_op jit(solution)/shard_map/all_to_all | solution.py:53
  205.5 0.1 copy.30
  205.6 0.1 reshape.91
  205.7 0.1 copy.25
  205.8 0.0 copy-done.6
  205.8 0.1 copy.24
  205.9 47.0 %all-to-all-done.1 = bf16[16,32,2048]{2,1,0:T(8,128)(2,1)S(1)} async-done(((bf16[16,32,2048]{2,1,0:T(8,128)(2,1)}), bf16[16,32,2048]{2,1,0:T(8,128)(2,1)S(1)}, u32[]{:S(2)}, u32[]{:S(2)}) %all-to-all-start.1) | async-done | bytes 2097184 | tf_op jit(solution)/shard_map/all_to_all | solution.py:53
  252.9 3.3 %gather_fusion = bf16[512,2048]{1,0:T(8,128)(2,1)} fusion(bf16[512,2048]{1,0:T(8,128)(2,1)S(1)} %bitcast.46, s32[1024]{0:T(1024)S(1)} %pad_clamp_fusion), kind=kCustom, calls=%fused_computation | custom fusion | bytes 4196352 | tf_op jit(solution)/shard_map/jit(_take)/gather | solution.py:57
  256.2 4.7 %multiply_reduce_fusion = bf16[64,2048]{1,0:T(8,128)(2,1)} fusion(bf16[512,2048]{1,0:T(8,128)(2,1)} %gather_fusion, f32[64,8]{1,0:T(8,128)S(1)} %copy.24, pred[64,8]{1,0:T(8,128)(4,1)S(1)} %copy.25), kind=kLoop, calls=%fused_computation.7 | loop fusion | flops 4063232 | bytes 2361856 | tf_op jit(solution)/shard_map/reduce_sum | solution.py:59
  (5 shorter events, 0.0 us)
Async XLA Ops:
  6.5 16.7 %copy-start = (bf16[64,2048]{1,0:T(8,128)(2,1)S(1)}, bf16[64,2048]{1,0:T(8,128)(2,1)}, u32[]{:S(2)}) copy-start(bf16[64,2048]{1,0:T(8,128)(2,1)} %param.10) | copy-start | bytes 786436
  6.5 72.9 %all-gather.4.cloned.1.call-start = ((), (), s32[]{:S(2)}) async-start(), calls=%async_computation.2 | async-start | bytes 6291456 | tf_op jit(solution)/shard_map/all_gather | solution.py:45
  7.4 4.7 %copy-start.1 = (bf16[1,2048,512]{2,1,0:T(8,128)(2,1)S(1)}, bf16[1,2048,512]{2,1,0:T(8,128)(2,1)}, u32[]{:S(2)}) copy-start(bf16[1,2048,512]{2,1,0:T(8,128)(2,1)} %param.14) | copy-start | bytes 6291460
  14.3 0.7 copy-start.7
  14.3 116.3 %all-gather.6.cloned.1.call-start = ((), (), s32[]{:S(2)}) async-start(), calls=%async_computation.3 | async-start | bytes 6291456 | tf_op jit(solution)/shard_map/all_gather | solution.py:46
  15.1 4.7 %copy-start.2 = (bf16[1,2048,512]{2,1,0:T(8,128)(2,1)S(1)}, bf16[1,2048,512]{2,1,0:T(8,128)(2,1)}, u32[]{:S(2)}) copy-start(bf16[1,2048,512]{2,1,0:T(8,128)(2,1)} %param.15) | copy-start | bytes 6291460
  22.0 0.7 copy-start.4
  22.0 0.7 copy-start.5
  25.3 6.9 %copy-start.8 = (f32[1,16,4]{1,2,0:T(4,128)S(1)}, f32[1,16,4]{1,2,0:T(4,128)}, u32[]{:S(2)}) copy-start(f32[1,16,4]{1,2,0:T(4,128)} %param.19) | copy-start | bytes 772
  25.3 54.1 %all-to-all-start = ((bf16[16,32,2048]{2,1,0:T(8,128)(2,1)}), bf16[16,32,2048]{2,1,0:T(8,128)(2,1)S(1)}, u32[]{:S(2)}, u32[]{:S(2)}) async-start(bf16[16,32,2048]{2,1,0:T(8,128)(2,1)} %bitcast), calls=%async_computation | async-start | bytes 4194304 | tf_op jit(solution)/shard_map/all_to_all | solution.py:39
  32.0 157.0 %all-gather.8.cloned.1.call-start = ((), (), s32[]{:S(2)}) async-start(), calls=%async_computation.4 | async-start | bytes 6291456 | tf_op jit(solution)/shard_map/all_gather | solution.py:47
  32.4 4.7 %copy-start.3 = (bf16[1,2048,512]{2,1,0:T(8,128)(2,1)S(1)}, bf16[1,2048,512]{2,1,0:T(8,128)(2,1)}, u32[]{:S(2)}) copy-start(bf16[1,2048,512]{2,1,0:T(8,128)(2,1)} %param.16) | copy-start | bytes 6291460
  199.0 6.8 %copy-start.6 = (f32[64,8]{0,1:T(8,128)S(1)}, f32[64,8]{0,1:T(8,128)}, u32[]{:S(2)}) copy-start(f32[64,8]{0,1:T(8,128)} %param.11) | copy-start | bytes 6148
  199.0 53.9 %all-to-all-start.1 = ((bf16[16,32,2048]{2,1,0:T(8,128)(2,1)}), bf16[16,32,2048]{2,1,0:T(8,128)(2,1)S(1)}, u32[]{:S(2)}, u32[]{:S(2)}) async-start(bf16[16,32,2048]{2,1,0:T(8,128)(2,1)} %bitcast.55), calls=%async_computation.1 | async-start | bytes 4194304 | tf_op jit(solution)/shard_map/all_to_all | solution.py:53
Sparse Core Ops, SparseCore 0:
  14.4 57.8 all-gather.3
  73.9 56.7 all-gather.5
  132.2 56.7 all-gather.7
where the time goes:
time: 268 us; the launch traced here: 267 us
  waiting for transfers between devices  190 us (71%)
  local copies, waits for them, and re-layouts  20.3 us (8%)
  matrix products  18.5 us (7%)
  starting transfers between devices  13.4 us (5%)
  between operations  13.2 us (5%)
  other arithmetic  11.6 us (4%)
    all_gather x1, waiting for transfers between devices, local(): down_piece = lax.all_gather(w_down, 'stream', axis=1, tiled=True)  58.3 us
    all_to_all x1, waiting for transfers between devices, local(): lax.all_to_all(expert_out, 'expert', split_axis=0, concat_axis=0, tiled=T...  47 us
    all_gather x1, waiting for transfers between devices, local(): up_piece = lax.all_gather(w_up, 'stream', axis=1, tiled=True)  44.8 us
    all_to_all x1, waiting for transfers between devices, local(): lax.all_to_all(outgoing, 'expert', split_axis=0, concat_axis=0, tiled=True)  40.1 us
    broadcast_in_dim x6, local copies, waits for them, and re-layouts, dequantize(): expanded = jnp.repeat(jnp.repeat(scales, QB, axis=0), QB, axis=1)  14.2 us
    dot_general x1, matrix products, local(): jnp.einsum('rf,df->rd', hidden, down_piece, preferred_element_type=jnp.fl...  10 us
    all_to_all x1, starting transfers between devices, local(): lax.all_to_all(outgoing, 'expert', split_axis=0, concat_axis=0, tiled=True)  6.69 us
    convert_element_type x3, other arithmetic, dequantize(): return (quant.astype(jnp.float32) * expanded).astype(jnp.bfloat16)  6.54 us
  transfers between devices with their start and end apart: 5, of which 4 were waited for; matrix products, arithmetic and copies ran while one was open for 9% of the time, Pallas kernels for 0%

commit v1 on v0

--- a/solution.py
+++ b/solution.py
@@ -1,6 +1,10 @@
+import functools
+
 import jax
 import jax.numpy as jnp
 from jax import lax
+from jax.experimental import pallas as pl
+from jax.experimental.pallas import tpu as pltpu
 from jax.sharding import PartitionSpec as P
 
 QB = 128
@@ -11,7 +15,7 @@
     return (quant.astype(jnp.float32) * expanded).astype(jnp.bfloat16)
 
 
-def local(
+def exchange_rows(
     tokens,
     route_gates,
     expert_ids,
@@ -60,7 +64,317 @@
     return mixed_out.astype(jnp.bfloat16)
 
 
+AXES = ("stream", "expert")
+LANES = 128
+
+
+def pack_kernel(gates_ref, ids_ref, slots_ref, tokens_ref, out_ref):
+    width = tokens_ref.shape[1]
+    rows = tokens_ref.shape[0]
+    columns = LANES // 2
+    weighting = jnp.where(slots_ref[...] >= 0, gates_ref[...], jnp.float32(0.0))
+    ids = ids_ref[...]
+    column = lax.broadcasted_iota(jnp.int32, (columns, rows), 0)
+    spread = jnp.zeros((columns, rows), jnp.float32)
+    for k in range(ids.shape[0]):
+        spread += jnp.where(ids[k : k + 1] == column, weighting[k : k + 1], jnp.float32(0.0))
+    high = spread.astype(jnp.bfloat16).astype(jnp.float32)
+    both = jnp.concatenate([high, spread - high], axis=0)
+    out_ref[:, :width] = tokens_ref[...]
+    out_ref[:, width:] = both.T.astype(jnp.bfloat16)
+
+
+def pack(tokens, route_gates, expert_ids, slot_index):
+    rows, width = tokens.shape
+    return pl.pallas_call(
+        pack_kernel,
+        out_shape=jax.ShapeDtypeStruct((rows, width + LANES), jnp.bfloat16),
+        cost_estimate=pl.CostEstimate(
+            flops=rows * width, bytes_accessed=4 * rows * width, transcendentals=0
+        ),
+        name="pack",
+    )(route_gates.T, expert_ids.T, slot_index.T, tokens)
+
+
+def scale_kernel(*refs, pieces):
+    scales, quants, out_ref = refs[:3], refs[3:6], refs[6]
+    factors, held = refs[7:10], refs[10:13]
+    factor_sems, sems = refs[13:]
+    width, half = held[0].shape
+    rows = width // pieces
+
+    def fetch(which, piece):
+        at = pl.ds(piece * rows, rows)
+        return pltpu.make_async_copy(
+            quants[which].at[0, at], held[which].at[at], sems.at[which, piece]
+        )
+
+    factor_copies = [
+        pltpu.make_async_copy(scales[i], factors[i], factor_sems.at[i]) for i in range(3)
+    ]
+    for copy in factor_copies:
+        copy.start()
+    for piece in range(pieces):
+        for which in range(3):
+            fetch(which, piece).start()
+    for copy in factor_copies:
+        copy.wait()
+
+    def work(piece, carry):
+        for which in range(3):
+            fetch(which, piece).wait()
+            for i in range(rows // QB):
+                for j in range(half // QB):
+                    at = piece * (rows // QB) + i
+                    row = pl.ds(pl.multiple_of(at * QB, QB), QB)
+                    block = held[which][row, pl.ds(j * QB, QB)].astype(jnp.float32)
+                    block = (block * factors[which][j, at]).astype(out_ref.dtype)
+                    out_ref[row, pl.ds(which * half + j * QB, QB)] = block
+        return carry
+
+    lax.fori_loop(0, pieces, work, 0)
+
+
+def scale_weights(quants, scales):
+    _, width, half = quants[0].shape
+    pieces = 8
+    scales = [scale[0].T for scale in scales]
+    return pl.pallas_call(
+        functools.partial(scale_kernel, pieces=pieces),
+        in_specs=[pl.BlockSpec(memory_space=pl.ANY)] * 6,
+        out_specs=pl.BlockSpec(memory_space=pltpu.VMEM),
+        out_shape=pltpu.VMEM((width, 3 * half), jnp.bfloat16),
+        scratch_shapes=[pltpu.SMEM(scales[0].shape, jnp.float32)] * 3
+        + [pltpu.VMEM((width, half), jnp.bfloat16)] * 3
+        + [pltpu.SemaphoreType.DMA((3,)), pltpu.SemaphoreType.DMA((3, pieces))],
+        cost_estimate=pl.CostEstimate(
+            flops=3 * width * half, bytes_accessed=12 * width * half, transcendentals=0
+        ),
+        compiler_params=pltpu.CompilerParams(vmem_limit_bytes=52 * 2**20),
+        name="scale_weights",
+    )(*scales, *quants)
+
+
+def contract_last(a, b):
+    return lax.dot_general(a, b, (((1,), (1,)), ((), ())), preferred_element_type=jnp.float32)
+
+
+def hidden_units(me, which, rows_ref, weight, width, half):
+    columns = rows_ref[:, width:].astype(jnp.float32)
+    rank = lax.rem(lax.broadcasted_iota(jnp.int32, columns.shape, 1), LANES // 2)
+    gates = jnp.sum(
+        jnp.where(rank == me[which], columns, jnp.float32(0.0)), axis=1, keepdims=True
+    )
+    gate_act = jnp.dot(rows_ref[:, :width], weight[:, :half], preferred_element_type=jnp.float32)
+    up_act = jnp.dot(
+        rows_ref[:, :width], weight[:, half : 2 * half], preferred_element_type=jnp.float32
+    )
+    return (gate_act / (1.0 + jnp.exp(-gate_act)) * up_act * gates).astype(jnp.bfloat16)
+
+
+def hidden_kernel(me_ref, *refs):
+    *messages, weight, out_ref, rows_ref = refs
+    rows = messages[0].shape[0]
+    for i, message in enumerate(messages):
+        rows_ref[pl.ds(i * rows, rows), :] = message[...]
+    width, half = rows_ref.shape[1] - LANES, out_ref.shape[1]
+    out_ref[...] = hidden_units(me_ref, 0, rows_ref, weight, width, half)
+
+
+def own_hidden(me, messages, weight):
+    rows, columns = messages[0].shape
+    total = len(messages) * rows
+    width, half = columns - LANES, weight.shape[1] // 3
+    vmem = pl.BlockSpec(memory_space=pltpu.VMEM)
+    return pl.pallas_call(
+        hidden_kernel,
+        in_specs=[pl.BlockSpec(memory_space=pltpu.SMEM)] + [vmem] * (len(messages) + 1),
+        out_specs=vmem,
+        out_shape=pltpu.VMEM((total, half), jnp.bfloat16),
+        scratch_shapes=[pltpu.VMEM((total, columns), jnp.bfloat16)],
+        cost_estimate=pl.CostEstimate(
+            flops=4 * total * width * half,
+            bytes_accessed=4 * width * half + 2 * total * width,
+            transcendentals=total * half,
+        ),
+        compiler_params=pltpu.CompilerParams(vmem_limit_bytes=20 * 2**20),
+        name="own_hidden",
+    )(me, *messages, weight)
+
+
+def expert_kernel(me_ref, *refs, blocks, fetch, begun):
+    refs = list(refs)
+
+    def take(count):
+        taken = refs[:count]
+        del refs[:count]
+        return taken
+
+    messages = take(blocks)
+    mine, other = take(2)
+    before = take(1) if begun else []
+    outs = take(blocks)
+    kept = take(1) if fetch else []
+    rows_ref, *sems = refs
+    rows, width = outs[0].shape
+    half = mine.shape[1] // 3
+    copies = []
+    if fetch:
+        for part in range(3):
+            at = pl.ds(part * half, half)
+            source, target = other.at[:, at], kept[0].at[:, at]
+            copies.append(pltpu.make_async_copy(source, target, sems[0].at[part]))
+        other = kept[0]
+    for copy in copies:
+        copy.start()
+    for i, message in enumerate(messages):
+        rows_ref[pl.ds(i * rows, rows), :] = message[...]
+    if begun:
+        first = before[0][...]
+    else:
+        first = hidden_units(me_ref, 0, rows_ref, mine, width, half)
+    for copy in copies:
+        copy.wait()
+    second = hidden_units(me_ref, 1, rows_ref, other, width, half)
+    for j in range(width // half):
+        at = pl.ds(j * half, half)
+        answer = contract_last(first, mine[at, 2 * half :])
+        answer += contract_last(second, other[at, 2 * half :])
+        for i in range(blocks):
+            outs[i][:, at] = answer[i * rows : (i + 1) * rows].astype(outs[i].dtype)
+
+
+def run_experts(me, messages, mine, other, before=None, fetch=False):
+    rows, columns = messages[0].shape
+    width, half = columns - LANES, mine.shape[1] // 3
+    blocks = len(messages)
+    total = blocks * rows
+    vmem = pl.BlockSpec(memory_space=pltpu.VMEM)
+    out_shape = [jax.ShapeDtypeStruct((rows, width), jnp.bfloat16)] * blocks
+    scratch_shapes = [pltpu.VMEM((total, columns), jnp.bfloat16)]
+    if fetch:
+        out_shape.append(pltpu.VMEM(other.shape, jnp.bfloat16))
+        scratch_shapes.append(pltpu.SemaphoreType.DMA((3,)))
+    others = [] if before is None else [before]
+    return list(
+        pl.pallas_call(
+            functools.partial(
+                expert_kernel, blocks=blocks, fetch=fetch, begun=before is not None
+            ),
+            in_specs=[pl.BlockSpec(memory_space=pltpu.SMEM)]
+            + [vmem] * (blocks + 1)
+            + [pl.BlockSpec(memory_space=pl.ANY) if fetch else vmem]
+            + [vmem] * len(others),
+            out_specs=[vmem] * len(out_shape),
+            out_shape=out_shape,
+            scratch_shapes=scratch_shapes,
+            cost_estimate=pl.CostEstimate(
+                flops=12 * total * width * half,
+                bytes_accessed=12 * width * half + 4 * total * width,
+                transcendentals=2 * total * half,
+            ),
+            compiler_params=pltpu.CompilerParams(vmem_limit_bytes=20 * 2**20),
+            name="run_experts",
+        )(me, *messages, mine, other, *others)
+    )
+
+
+def hop(value, bit, devices):
+    return lax.ppermute(value, AXES, [(i, i ^ bit) for i in range(devices)])
+
+
+def after(value, *others):
+    return lax.optimization_barrier((value, *others))[0]
+
+
+def add(*terms):
+    total = terms[0].astype(jnp.float32)
+    for term in terms[1:]:
+        total = total + term.astype(jnp.float32)
+    return total.astype(jnp.bfloat16)
+
+
+def gather_tokens(
+    tokens,
+    route_gates,
+    expert_ids,
+    slot_index,
+    gate_quant,
+    up_quant,
+    down_quant,
+    gate_scale,
+    up_scale,
+    down_scale,
+):
+    experts = lax.axis_size("expert")
+    devices = experts * lax.axis_size("stream")
+
+    def send(value, bit):
+        return hop(value, bit, devices)
+
+    core, y, z1, z2, z3, x = 1, 2, 4, 8, 12, experts
+    me = lax.axis_index("expert")
+    pair = jnp.stack([me, me ^ 1]).astype(jnp.int32)
+    s0 = pack(tokens, route_gates, expert_ids, slot_index)
+    s2 = send(s0, z2)
+    s1 = send(s0, z1)
+    x0 = send(s0, x)
+    y0 = send(s0, y)
+    mine = scale_weights(
+        (gate_quant, up_quant, down_quant), (gate_scale, up_scale, down_scale)
+    )
+    swapped = send(after(mine, s2, s1, x0, y0), core)
+    s3 = send(s2, z1)
+    y2 = send(after(s2, y0), y)
+    x2 = send(after(s2, x0), x)
+    begun = own_hidden(pair, (s0, x0, y0, s1), mine)
+    d0 = send(after(x0, y2, s3, begun), y)
+    d2 = send(after(y2, x2, s3, begun), x)
+    x3 = send(after(s3, x2), x)
+    y3 = send(after(s3, y2), y)
+    last = (s0, x0, y0, s1)
+    s2, s3, x2, y2, swapped = run_experts(pair, (s2, s3, x2, y2), mine, swapped, fetch=True)
+
+    def work(*messages):
+        return run_experts(pair, messages, mine, swapped)
+
+    d3 = send(after(x3, s2), y)
+    x1 = send(after(s1, x3, d0, s2), x)
+    d1 = send(after(d0, s2), z1)
+    y1 = send(after(s1, d0, s2), y)
+    d2, x3, y3, d0 = work(after(d2, s2), x3, y3, d0)
+    bx2 = send(after(x2, d3, x1, d2), x)
+    by2 = send(after(y2, d3, x1, d2), y)
+    bd2 = send(after(d2, d3, x1, d1), z1)
+    d3, x1, y1, d1 = work(after(d3, d2), x1, y1, d1)
+    bd3 = send(after(add(d3, bd2), bx2, by2), x)
+    bd1 = send(after(d1, bd2, bx2, by2), z1)
+    by1 = send(after(y1, bd2, bx2, by2), y)
+    bx3 = send(after(x3, bd2, bx2, by2, d3), x)
+    bs2 = send(after(add(s2, bx2, by2), bd2, d3), z2)
+    by3 = send(add(y3, bd3), y)
+    bd0 = send(after(add(d0, bd1), by1), y)
+    bx1 = send(after(x1, bd3, by1), x)
+    s0, x0, y0, s1 = run_experts(
+        pair, (after(last[0], d3, bd3, bd1), *last[1:]), mine, swapped, before=begun
+    )
+    by0 = send(y0, y)
+    bs3 = send(add(s3, bx3, by3), z3)
+    bs1 = send(add(s1, bx1, by1), z1)
+    bx0 = send(add(x0, bd0), x)
+    return add(s0, bx0, by0, bs1, bs2, bs3)
+
+
 def solution(mesh):
+    streams = mesh.shape["stream"]
+    experts = mesh.shape["expert"]
+
+    def local(tokens, *rest):
+        all_tokens = tokens.size * streams * experts
+        weights = 3 * rest[3].size * streams
+        move_tokens = (streams, experts) == (2, 16) and all_tokens < weights
+        return (gather_tokens if move_tokens else exchange_rows)(tokens, *rest)
+
     return jax.shard_map(
         local,
         mesh=mesh,

time: 268 us -> 103 us (0.38)
  the two profiles are of different devices: /device:TPU:13 before, /device:TPU:0 now
where the time goes in v1:
time: 103 us
  starting transfers between devices  38.3 us (37%)
  Pallas kernels  37.6 us (37%)
  waiting for transfers between devices  25.4 us (25%)
  other arithmetic  1.55 us (2%)
    ppermute x31, starting transfers between devices, hop(): return lax.ppermute(value, AXES, [(i, i ^ bit) for i in range(devices)])  38.3 us
    pallas_call x4, Pallas kernels, run_experts(): pl.pallas_call(functools.partial(expert_kernel, blocks=blocks, fetch=fetc...  26 us
    ppermute x31, waiting for transfers between devices, hop(): return lax.ppermute(value, AXES, [(i, i ^ bit) for i in range(devices)])  25.4 us
    pallas_call x1, Pallas kernels, scale_weights(): pl.pallas_call(functools.partial(scale_kernel, pieces=pieces), in_specs=[...  5.71 us
    pallas_call x1, Pallas kernels, own_hidden(): pl.pallas_call(hidden_kernel, in_specs=[pl.BlockSpec(memory_space=pltpu.S...  4.05 us
  transfers between devices with their start and end apart: 31, of which 11 were waited for; matrix products, arithmetic and copies ran while one was open for 1% of the time, Pallas kernels for 35%

profile of v1, /device:TPU:0, one launch (start us, length us, event | category | flops | bytes accessed | tf_op | source)
XLA Modules:
  0.0 103.0 jit_solution(6992941689418081241)
XLA Ops:
  0.0 1.8 %pack.1.refs_0_ = bf16[64,2176]{1,0:T(8,128)(2,1)} custom-call(f32[8,64]{1,0:T(8,128)} %bitcast.14, s32[8,64]{1,0:T(8,128)} %bitcast.15, s32[8,64]{1,0:T(8,128)} %bitcast.16, bf16[64,2048]{1,0:T(8,128)(2,1)} %tokens_ref.1), custom_call_target="tpu_custom_call" | custom-call | flops 131072 | bytes 524288 | tf_op jit(solution)/shard_map/pack/pallas_call | solution.py:89
  1.8 4.0 %collective-permute-start = (bf16[64,2176]{1,0:T(8,128)(2,1)}, bf16[64,2176]{1,0:T(8,128)(2,1)S(1)}, u32[]{:S(2)}, u32[]{:S(2)}) collective-permute-start(bf16[64,2176]{1,0:T(8,128)(2,1)} %pack.1.refs_0_), channel_id=1, source_target_pairs={{0,8},{1,9},{2,10},{3,11},{4,12},{5,13},{6,14},{7,15},{8,0},{9,1},... | collective-permute-start | bytes 835592 | tf_op jit(solution)/shard_map/ppermute | solution.py:283
  5.9 1.5 %collective-permute-start.2 = (bf16[64,2176]{1,0:T(8,128)(2,1)}, bf16[64,2176]{1,0:T(8,128)(2,1)S(1)}, u32[]{:S(2)}, u32[]{:S(2)}) collective-permute-start(bf16[64,2176]{1,0:T(8,128)(2,1)} %pack.1.refs_0_), channel_id=1, source_target_pairs={{0,16},{1,17},{2,18},{3,19},{4,20},{5,21},{6,22},{7,23},{8,24},{9,... | collective-permute-start | bytes 835592 | tf_op jit(solution)/shard_map/ppermute | solution.py:283
  7.4 1.6 %collective-permute-start.7 = (bf16[64,2176]{1,0:T(8,128)(2,1)}, bf16[64,2176]{1,0:T(8,128)(2,1)S(1)}, u32[]{:S(2)}, u32[]{:S(2)}) collective-permute-start(bf16[64,2176]{1,0:T(8,128)(2,1)} %pack.1.refs_0_), channel_id=1, source_target_pairs={{0,4},{1,5},{2,6},{3,7},{4,0},{5,1},{6,2},{7,3},{8,12},{9,13},{10,... | collective-permute-start | bytes 835592 | tf_op jit(solution)/shard_map/ppermute | solution.py:283
  8.9 1.5 %collective-permute-start.5 = (bf16[64,2176]{1,0:T(8,128)(2,1)}, bf16[64,2176]{1,0:T(8,128)(2,1)S(1)}, u32[]{:S(2)}, u32[]{:S(2)}) collective-permute-start(bf16[64,2176]{1,0:T(8,128)(2,1)} %pack.1.refs_0_), channel_id=1, source_target_pairs={{0,2},{1,3},{2,0},{3,1},{4,6},{5,7},{6,4},{7,5},{8,10},{9,11},{10,... | collective-permute-start | bytes 835592 | tf_op jit(solution)/shard_map/ppermute | solution.py:283
  10.5 5.7 %scale_weights.1.refs_4_ = bf16[2048,1536]{1,0:T(8,128)(2,1)} custom-call(f32[4,16]{1,0:T(4,128)} %bitcast.17, f32[4,16]{1,0:T(4,128)} %bitcast.18, f32[4,16]{1,0:T(4,128)} %bitcast.19, bf16[1,2048,512]{2,1,0:T(8,128)(2,1)} %refs_3_.1, bf16[1,2048,512]{2,1,0:T(8,128)(2,1)} %refs_4_.1, bf16[1,2048,512]{2,1,0:T(8,128)(2,1)} %refs_5_.1), custom_call_target="tpu_custom_call" | custom-call | flops 3145728 | bytes 12582912 | tf_op jit(solution)/shard_map/scale_weights/pallas_call | solution.py:142
  16.2 2.6 %collective-permute-done.refs_0_ = bf16[64,2176]{1,0:T(8,128)(2,1)S(1)} collective-permute-done((bf16[64,2176]{1,0:T(8,128)(2,1)}, bf16[64,2176]{1,0:T(8,128)(2,1)S(1)}, u32[]{:S(2)}, u32[]{:S(2)}) %collective-permute-start) | collective-permute-done | bytes 278560 | tf_op jit(solution)/shard_map/ppermute | solution.py:283
  18.8 0.0 collective-permute-done.2.refs_1_
  18.8 1.4 %collective-permute-done.7.refs_3_ = bf16[64,2176]{1,0:T(8,128)(2,1)S(1)} collective-permute-done((bf16[64,2176]{1,0:T(8,128)(2,1)}, bf16[64,2176]{1,0:T(8,128)(2,1)S(1)}, u32[]{:S(2)}, u32[]{:S(2)}) %collective-permute-start.7) | collective-permute-done | bytes 278560 | tf_op jit(solution)/shard_map/ppermute | solution.py:283
  20.2 0.0 collective-permute-done.5.refs_2_
  20.2 0.0 collective-permute-start.8
  20.2 1.6 %collective-permute-start.6 = (bf16[64,2176]{1,0:T(8,128)(2,1)S(1)}, bf16[64,2176]{1,0:T(8,128)(2,1)S(1)}, u32[]{:S(2)}, u32[]{:S(2)}) collective-permute-start(bf16[64,2176]{1,0:T(8,128)(2,1)S(1)} %collective-permute-done.refs_0_), channel_id=1, source_target_pairs={{0,2},{1,3},{2,0},{3,1},{4,6},{5,7},{6,4},{7,5},{8,10},{9,11},{10,... | collective-permute-start | bytes 835592 | tf_op jit(solution)/shard_map/ppermute | solution.py:283
  21.8 0.2 collective-permute-start.1
  22.0 1.5 %collective-permute-start.3 = (bf16[64,2176]{1,0:T(8,128)(2,1)S(1)}, bf16[64,2176]{1,0:T(8,128)(2,1)S(1)}, u32[]{:S(2)}, u32[]{:S(2)}) collective-permute-start(bf16[64,2176]{1,0:T(8,128)(2,1)S(1)} %collective-permute-done.refs_0_), channel_id=1, source_target_pairs={{0,16},{1,17},{2,18},{3,19},{4,20},{5,21},{6,22},{7,23},{8,24},{9,... | collective-permute-start | bytes 835592 | tf_op jit(solution)/shard_map/ppermute | solution.py:283
  23.5 0.1 pad_add_fusion.me_ref
  23.6 4.1 %own_hidden.1.refs_6_ = bf16[256,512]{1,0:T(8,128)(2,1)S(1)} custom-call(s32[2]{0:T(128)S(1)} %pad_add_fusion.me_ref, bf16[64,2176]{1,0:T(8,128)(2,1)S(1)} %copy-done, bf16[64,2176]{1,0:T(8,128)(2,1)S(1)} %collective-permute-done.2.refs_1_, bf16[64,2176]{1,0:T(8,128)(2,1)S(1)} %collective-permute-done.5.refs_2_, ...), custom_call_target="tpu_custom_call" | custom-call | flops 1073741824 | bytes 5242880 | tf_op jit(solution)/shard_map/own_hidden/pallas_call | solution.py:189
  27.6 1.6 %collective-permute-done.6.refs_3_ = bf16[64,2176]{1,0:T(8,128)(2,1)S(1)} collective-permute-done((bf16[64,2176]{1,0:T(8,128)(2,1)S(1)}, bf16[64,2176]{1,0:T(8,128)(2,1)S(1)}, u32[]{:S(2)}, u32[]{:S(2)}) %collective-permute-start.6) | collective-permute-done | bytes 278560 | tf_op jit(solution)/shard_map/ppermute | solution.py:283
  29.3 1.3 %collective-permute-done.1.refs_1_ = bf16[64,2176]{1,0:T(8,128)(2,1)S(1)} collective-permute-done((bf16[64,2176]{1,0:T(8,128)(2,1)S(1)}, bf16[64,2176]{1,0:T(8,128)(2,1)S(1)}, u32[]{:S(2)}, u32[]{:S(2)}) %collective-permute-start.1) | collective-permute-done | bytes 278560 | tf_op jit(solution)/shard_map/ppermute | solution.py:283
  30.6 0.5 collective-permute-start.12
  31.0 0.0 collective-permute-done.3.refs_2_
  31.0 1.0 collective-permute-start.4
  32.0 1.0 %collective-permute-start.10 = (bf16[64,2176]{1,0:T(8,128)(2,1)S(1)}, bf16[64,2176]{1,0:T(8,128)(2,1)S(1)}, u32[]{:S(2)}, u32[]{:S(2)}) collective-permute-start(bf16[64,2176]{1,0:T(8,128)(2,1)S(1)} %collective-permute-done.6.refs_3_), channel_id=1, source_target_pairs={{0,16},{1,17},{2,18},{3,19},{4,20},{5,21},{6,22},{7,23},{8,24},{9,... | collective-permute-start | bytes 835592 | tf_op jit(solution)/shard_map/ppermute | solution.py:283
  33.1 1.6 %collective-permute-start.11 = (bf16[64,2176]{1,0:T(8,128)(2,1)S(1)}, bf16[64,2176]{1,0:T(8,128)(2,1)S(1)}, u32[]{:S(2)}, u32[]{:S(2)}) collective-permute-start(bf16[64,2176]{1,0:T(8,128)(2,1)S(1)} %collective-permute-done.1.refs_1_), channel_id=1, source_target_pairs={{0,2},{1,3},{2,0},{3,1},{4,6},{5,7},{6,4},{7,5},{8,10},{9,11},{10,... | collective-permute-start | bytes 835592 | tf_op jit(solution)/shard_map/ppermute | solution.py:283
  34.6 0.0 collective-permute-done.8.refs_5_
  34.6 8.1 %run_experts.4 = (bf16[64,2048]{1,0:T(8,128)(2,1)S(1)}, bf16[64,2048]{1,0:T(8,128)(2,1)S(1)}, bf16[64,2048]{1,0:T(8,128)(2,1)S(1)}, bf16[64,2048]{1,0:T(8,128)(2,1)S(1)}, bf16[2048,1536]{1,0:T(8,128)(2,1)S(1)}) custom-call(s32[2]{0:T(128)S(1)} %pad_add_fusion.me_ref, bf16[64,2176]{1,0:T(8,128)(2,1)S(1)} %collective-permute-done.refs_0_, ...), custom_call_target="tpu_custom_call" | custom-call | flops 3221225472 | bytes 14680064 | tf_op jit(solution)/shard_map/run_experts/pallas_call | solution.py:260
  42.8 0.0 collective-permute-done.12.refs_3_
  42.8 0.6 collective-permute-start.13
  43.4 2.5 %collective-permute-done.10.refs_0_ = bf16[64,2176]{1,0:T(8,128)(2,1)S(1)} collective-permute-done((bf16[64,2176]{1,0:T(8,128)(2,1)S(1)}, bf16[64,2176]{1,0:T(8,128)(2,1)S(1)}, u32[]{:S(2)}, u32[]{:S(2)}) %collective-permute-start.10) | collective-permute-done | bytes 278560 | tf_op jit(solution)/shard_map/ppermute | solution.py:283
  45.9 2.3 %collective-permute-start.9 = (bf16[64,2176]{1,0:T(8,128)(2,1)S(1)}, bf16[64,2176]{1,0:T(8,128)(2,1)S(1)}, u32[]{:S(2)}, u32[]{:S(2)}) collective-permute-start(bf16[64,2176]{1,0:T(8,128)(2,1)S(1)} %collective-permute-done.4.refs_1_), channel_id=1, source_target_pairs={{0,2},{1,3},{2,0},{3,1},{4,6},{5,7},{6,4},{7,5},{8,10},{9,11},{10,... | collective-permute-start | bytes 835592 | tf_op jit(solution)/shard_map/ppermute | solution.py:283
  48.2 0.0 collective-permute-start.14
  48.2 1.5 %collective-permute-start.15 = (bf16[64,2176]{1,0:T(8,128)(2,1)S(1)}, bf16[64,2176]{1,0:T(8,128)(2,1)S(1)}, u32[]{:S(2)}, u32[]{:S(2)}) collective-permute-start(bf16[64,2176]{1,0:T(8,128)(2,1)S(1)} %collective-permute-done.12.refs_3_), channel_id=1, source_target_pairs={{0,4},{1,5},{2,6},{3,7},{4,0},{5,1},{6,2},{7,3},{8,12},{9,13},{10,... | collective-permute-start | bytes 835592 | tf_op jit(solution)/shard_map/ppermute | solution.py:283
  49.7 6.3 %run_experts.5 = (bf16[64,2048]{1,0:T(8,128)(2,1)S(1)}, bf16[64,2048]{1,0:T(8,128)(2,1)S(1)}, bf16[64,2048]{1,0:T(8,128)(2,1)S(1)}, bf16[64,2048]{1,0:T(8,128)(2,1)S(1)}) custom-call(s32[2]{0:T(128)S(1)} %pad_add_fusion.me_ref, bf16[64,2176]{1,0:T(8,128)(2,1)S(1)} %collective-permute-done.10.refs_0_, bf16[64,2176]{1,0:T(8,128)(2,1)S(1)} %collective-permute-done.4.refs_1_, ...), custom_call_target="tpu_custom_call" | custom-call | flops 3221225472 | bytes 14680064 | tf_op jit(solution)/shard_map/run_experts/pallas_call | solution.py:260
  56.1 0.0 collective-permute-done.13.refs_1_
  56.1 0.8 collective-permute-start.18
  56.9 1.4 %collective-permute-start.17 = (bf16[64,2048]{1,0:T(8,128)(2,1)S(1)}, bf16[64,2048]{1,0:T(8,128)(2,1)S(1)}, u32[]{:S(2)}, u32[]{:S(2)}) collective-permute-start(bf16[64,2048]{1,0:T(8,128)(2,1)S(1)} %get-tuple-element.65), channel_id=1, source_target_pairs={{0,16},{1,17},{2,18},{3,19},{4,20},{5,21},{6,22},{7,23},{8,24},{9,... | collective-permute-start | bytes 786440 | tf_op jit(solution)/shard_map/ppermute | solution.py:283
  58.3 0.6 collective-permute-start.16
  58.9 1.7 %collective-permute-done.14.refs_2_ = bf16[64,2176]{1,0:T(8,128)(2,1)S(1)} collective-permute-done((bf16[64,2176]{1,0:T(8,128)(2,1)S(1)}, bf16[64,2176]{1,0:T(8,128)(2,1)S(1)}, u32[]{:S(2)}, u32[]{:S(2)}) %collective-permute-start.14) | collective-permute-done | bytes 278560 | tf_op jit(solution)/shard_map/ppermute | solution.py:283
  60.5 6.3 %run_experts.6 = (bf16[64,2048]{1,0:T(8,128)(2,1)S(1)}, bf16[64,2048]{1,0:T(8,128)(2,1)S(1)}, bf16[64,2048]{1,0:T(8,128)(2,1)S(1)}, bf16[64,2048]{1,0:T(8,128)(2,1)S(1)}) custom-call(s32[2]{0:T(128)S(1)} %pad_add_fusion.me_ref, bf16[64,2176]{1,0:T(8,128)(2,1)S(1)} %collective-permute-done.9.refs_0_, bf16[64,2176]{1,0:T(8,128)(2,1)S(1)} %collective-permute-done.13.refs_1_, ...), custom_call_target="tpu_custom_call" | custom-call | flops 3221225472 | bytes 14680064 | tf_op jit(solution)/shard_map/run_experts/pallas_call | solution.py:260
  66.9 1.0 collective-permute-start.20
  67.9 0.6 collective-permute-start.21
  68.5 0.1 add_convert_fusion.7
  68.6 1.5 %collective-permute-start.19 = (bf16[64,2048]{1,0:T(8,128)(2,1)S(1)}, bf16[64,2048]{1,0:T(8,128)(2,1)S(1)}, u32[]{:S(2)}, u32[]{:S(2)}) collective-permute-start(bf16[64,2048]{1,0:T(8,128)(2,1)S(1)} %add_convert_fusion.7), channel_id=1, source_target_pairs={{0,16},{1,17},{2,18},{3,19},{4,20},{5,21},{6,22},{7,23},{8,24},{9,... | collective-permute-start | bytes 786440 | tf_op jit(solution)/shard_map/ppermute | solution.py:283
  70.1 0.1 add_convert_fusion.3
  70.2 2.3 %collective-permute-start.27 = (bf16[64,2048]{1,0:T(8,128)(2,1)S(1)}, bf16[64,2048]{1,0:T(8,128)(2,1)S(1)}, u32[]{:S(2)}, u32[]{:S(2)}) collective-permute-start(bf16[64,2048]{1,0:T(8,128)(2,1)S(1)} %add_convert_fusion.3), channel_id=1, source_target_pairs={{0,8},{1,9},{2,10},{3,11},{4,12},{5,13},{6,14},{7,15},{8,0},{9,1},... | collective-permute-start | bytes 786440 | tf_op jit(solution)/shard_map/ppermute | solution.py:283
  72.5 1.0 collective-permute-start.28
  73.6 0.1 add_convert_fusion.6
  73.6 2.0 %collective-permute-done.21 = bf16[64,2048]{1,0:T(8,128)(2,1)S(1)} collective-permute-done((bf16[64,2048]{1,0:T(8,128)(2,1)S(1)}, bf16[64,2048]{1,0:T(8,128)(2,1)S(1)}, u32[]{:S(2)}, u32[]{:S(2)}) %collective-permute-start.21) | collective-permute-done | bytes 262176 | tf_op jit(solution)/shard_map/ppermute | solution.py:283
  75.6 1.0 collective-permute-start.22
  76.6 0.5 collective-permute-done.19
  77.1 2.1 %collective-permute-start.25 = (bf16[64,2048]{1,0:T(8,128)(2,1)S(1)}, bf16[64,2048]{1,0:T(8,128)(2,1)S(1)}, u32[]{:S(2)}, u32[]{:S(2)}) collective-permute-start(bf16[64,2048]{1,0:T(8,128)(2,1)S(1)} %get-tuple-element.81), channel_id=1, source_target_pairs={{0,16},{1,17},{2,18},{3,19},{4,20},{5,21},{6,22},{7,23},{8,24},{9,... | collective-permute-start | bytes 786440 | tf_op jit(solution)/shard_map/ppermute | solution.py:283
  79.2 5.2 %run_experts.7 = (bf16[64,2048]{1,0:T(8,128)(2,1)S(1)}, bf16[64,2048]{1,0:T(8,128)(2,1)S(1)}, bf16[64,2048]{1,0:T(8,128)(2,1)S(1)}, bf16[64,2048]{1,0:T(8,128)(2,1)S(1)}) custom-call(s32[2]{0:T(128)S(1)} %pad_add_fusion.me_ref, bf16[64,2176]{1,0:T(8,128)(2,1)S(1)} %copy-done, bf16[64,2176]{1,0:T(8,128)(2,1)S(1)} %collective-permute-done.2.refs_1_, ...), custom_call_target="tpu_custom_call" | custom-call | flops 3221225472 | bytes 14680064 | tf_op jit(solution)/shard_map/run_experts/pallas_call | solution.py:260
  84.4 1.6 %collective-permute-start.24 = (bf16[64,2048]{1,0:T(8,128)(2,1)S(1)}, bf16[64,2048]{1,0:T(8,128)(2,1)S(1)}, u32[]{:S(2)}, u32[]{:S(2)}) collective-permute-start(bf16[64,2048]{1,0:T(8,128)(2,1)S(1)} %get-tuple-element.78), channel_id=1, source_target_pairs={{0,2},{1,3},{2,0},{3,1},{4,6},{5,7},{6,4},{7,5},{8,10},{9,11},{10,... | collective-permute-start | bytes 786440 | tf_op jit(solution)/shard_map/ppermute | solution.py:283
  86.0 0.1 add_convert_fusion.2
  86.1 0.6 collective-permute-start.29
  86.7 0.1 add_convert_fusion.5
  86.7 1.4 %collective-permute-start.23 = (bf16[64,2048]{1,0:T(8,128)(2,1)S(1)}, bf16[64,2048]{1,0:T(8,128)(2,1)S(1)}, u32[]{:S(2)}, u32[]{:S(2)}) collective-permute-start(bf16[64,2048]{1,0:T(8,128)(2,1)S(1)} %add_convert_fusion.5), channel_id=1, source_target_pairs={{0,16},{1,17},{2,18},{3,19},{4,20},{5,21},{6,22},{7,23},{8,24},{9,... | collective-permute-start | bytes 786440 | tf_op jit(solution)/shard_map/ppermute | solution.py:283
  88.1 0.1 add_convert_fusion.4
  88.2 0.6 collective-permute-start.26
  88.9 4.8 %collective-permute-done.29 = bf16[64,2048]{1,0:T(8,128)(2,1)S(1)} collective-permute-done((bf16[64,2048]{1,0:T(8,128)(2,1)S(1)}, bf16[64,2048]{1,0:T(8,128)(2,1)S(1)}, u32[]{:S(2)}, u32[]{:S(2)}) %collective-permute-start.29) | collective-permute-done | bytes 262176 | tf_op jit(solution)/shard_map/ppermute | solution.py:283
  93.7 0.1 add_convert_fusion.1
  93.8 1.4 %collective-permute-start.30 = (bf16[64,2048]{1,0:T(8,128)(2,1)S(1)}, bf16[64,2048]{1,0:T(8,128)(2,1)S(1)}, u32[]{:S(2)}, u32[]{:S(2)}) collective-permute-start(bf16[64,2048]{1,0:T(8,128)(2,1)S(1)} %add_convert_fusion.1), channel_id=1, source_target_pairs={{0,12},{1,13},{2,14},{3,15},{4,8},{5,9},{6,10},{7,11},{8,4},{9,5},... | collective-permute-start | bytes 786440 | tf_op jit(solution)/shard_map/ppermute | solution.py:283
  95.2 1.9 %collective-permute-done.26 = bf16[64,2048]{1,0:T(8,128)(2,1)S(1)} collective-permute-done((bf16[64,2048]{1,0:T(8,128)(2,1)S(1)}, bf16[64,2048]{1,0:T(8,128)(2,1)S(1)}, u32[]{:S(2)}, u32[]{:S(2)}) %collective-permute-start.26) | collective-permute-done | bytes 262176 | tf_op jit(solution)/shard_map/ppermute | solution.py:283
  97.1 5.0 %collective-permute-done.30 = bf16[64,2048]{1,0:T(8,128)(2,1)S(1)} collective-permute-done((bf16[64,2048]{1,0:T(8,128)(2,1)S(1)}, bf16[64,2048]{1,0:T(8,128)(2,1)S(1)}, u32[]{:S(2)}, u32[]{:S(2)}) %collective-permute-start.30) | collective-permute-done | bytes 262176 | tf_op jit(solution)/shard_map/ppermute | solution.py:283
  102.1 0.9 add_convert_fusion
  (16 shorter events, 0.0 us)
Async XLA Ops:
  1.8 17.0 %collective-permute-start = (bf16[64,2176]{1,0:T(8,128)(2,1)}, bf16[64,2176]{1,0:T(8,128)(2,1)S(1)}, u32[]{:S(2)}, u32[]{:S(2)}) collective-permute-start(bf16[64,2176]{1,0:T(8,128)(2,1)} %pack.1.refs_0_), channel_id=1, source_target_pairs={{0,8},{1,9},{2,10},{3,11},{4,12},{5,13},{6,14},{7,15},{8,0},{9,1},... | collective-permute-start | bytes 835592 | tf_op jit(solution)/shard_map/ppermute | solution.py:283
  5.9 12.9 %collective-permute-start.2 = (bf16[64,2176]{1,0:T(8,128)(2,1)}, bf16[64,2176]{1,0:T(8,128)(2,1)S(1)}, u32[]{:S(2)}, u32[]{:S(2)}) collective-permute-start(bf16[64,2176]{1,0:T(8,128)(2,1)} %pack.1.refs_0_), channel_id=1, source_target_pairs={{0,16},{1,17},{2,18},{3,19},{4,20},{5,21},{6,22},{7,23},{8,24},{9,... | collective-permute-start | bytes 835592 | tf_op jit(solution)/shard_map/ppermute | solution.py:283
  7.4 12.8 %collective-permute-start.7 = (bf16[64,2176]{1,0:T(8,128)(2,1)}, bf16[64,2176]{1,0:T(8,128)(2,1)S(1)}, u32[]{:S(2)}, u32[]{:S(2)}) collective-permute-start(bf16[64,2176]{1,0:T(8,128)(2,1)} %pack.1.refs_0_), channel_id=1, source_target_pairs={{0,4},{1,5},{2,6},{3,7},{4,0},{5,1},{6,2},{7,3},{8,12},{9,13},{10,... | collective-permute-start | bytes 835592 | tf_op jit(solution)/shard_map/ppermute | solution.py:283
  8.9 11.3 %collective-permute-start.5 = (bf16[64,2176]{1,0:T(8,128)(2,1)}, bf16[64,2176]{1,0:T(8,128)(2,1)S(1)}, u32[]{:S(2)}, u32[]{:S(2)}) collective-permute-start(bf16[64,2176]{1,0:T(8,128)(2,1)} %pack.1.refs_0_), channel_id=1, source_target_pairs={{0,2},{1,3},{2,0},{3,1},{4,6},{5,7},{6,4},{7,5},{8,10},{9,11},{10,... | collective-permute-start | bytes 835592 | tf_op jit(solution)/shard_map/ppermute | solution.py:283
  10.5 13.1 %copy-start = (bf16[64,2176]{1,0:T(8,128)(2,1)S(1)}, bf16[64,2176]{1,0:T(8,128)(2,1)}, u32[]{:S(2)}) copy-start(bf16[64,2176]{1,0:T(8,128)(2,1)} %pack.1.refs_0_) | copy-start | bytes 835588
  20.2 14.4 %collective-permute-start.8 = (bf16[2048,1536]{1,0:T(8,128)(2,1)}, bf16[2048,1536]{1,0:T(8,128)(2,1)}, u32[]{:S(2)}, u32[]{:S(2)}) collective-permute-start(bf16[2048,1536]{1,0:T(8,128)(2,1)} %scale_weights.1.refs_4_), channel_id=1, source_target_pairs={{0,1},{1,0},{2,3},{3,2},{4,5},{5,4},{6,7},{7,6},{8,9},{9,8},{10,11... | collective-permute-start | bytes 18874376 | tf_op jit(solution)/shard_map/ppermute | solution.py:283
  20.2 9.1 %collective-permute-start.6 = (bf16[64,2176]{1,0:T(8,128)(2,1)S(1)}, bf16[64,2176]{1,0:T(8,128)(2,1)S(1)}, u32[]{:S(2)}, u32[]{:S(2)}) collective-permute-start(bf16[64,2176]{1,0:T(8,128)(2,1)S(1)} %collective-permute-done.refs_0_), channel_id=1, source_target_pairs={{0,2},{1,3},{2,0},{3,1},{4,6},{5,7},{6,4},{7,5},{8,10},{9,11},{10,... | collective-permute-start | bytes 835592 | tf_op jit(solution)/shard_map/ppermute | solution.py:283
  21.8 8.8 %collective-permute-start.1 = (bf16[64,2176]{1,0:T(8,128)(2,1)S(1)}, bf16[64,2176]{1,0:T(8,128)(2,1)S(1)}, u32[]{:S(2)}, u32[]{:S(2)}) collective-permute-start(bf16[64,2176]{1,0:T(8,128)(2,1)S(1)} %collective-permute-done.refs_0_), channel_id=1, source_target_pairs={{0,4},{1,5},{2,6},{3,7},{4,0},{5,1},{6,2},{7,3},{8,12},{9,13},{10,... | collective-permute-start | bytes 835592 | tf_op jit(solution)/shard_map/ppermute | solution.py:283
  22.0 9.0 %collective-permute-start.3 = (bf16[64,2176]{1,0:T(8,128)(2,1)S(1)}, bf16[64,2176]{1,0:T(8,128)(2,1)S(1)}, u32[]{:S(2)}, u32[]{:S(2)}) collective-permute-start(bf16[64,2176]{1,0:T(8,128)(2,1)S(1)} %collective-permute-done.refs_0_), channel_id=1, source_target_pairs={{0,16},{1,17},{2,18},{3,19},{4,20},{5,21},{6,22},{7,23},{8,24},{9,... | collective-permute-start | bytes 835592 | tf_op jit(solution)/shard_map/ppermute | solution.py:283
  30.6 12.2 %collective-permute-start.12 = (bf16[64,2176]{1,0:T(8,128)(2,1)S(1)}, bf16[64,2176]{1,0:T(8,128)(2,1)S(1)}, u32[]{:S(2)}, u32[]{:S(2)}) collective-permute-start(bf16[64,2176]{1,0:T(8,128)(2,1)S(1)} %collective-permute-done.2.refs_1_), channel_id=1, source_target_pairs={{0,2},{1,3},{2,0},{3,1},{4,6},{5,7},{6,4},{7,5},{8,10},{9,11},{10,... | collective-permute-start | bytes 835592 | tf_op jit(solution)/shard_map/ppermute | solution.py:283
  31.0 11.8 %collective-permute-start.4 = (bf16[64,2176]{1,0:T(8,128)(2,1)S(1)}, bf16[64,2176]{1,0:T(8,128)(2,1)S(1)}, u32[]{:S(2)}, u32[]{:S(2)}) collective-permute-start(bf16[64,2176]{1,0:T(8,128)(2,1)S(1)} %collective-permute-done.1.refs_1_), channel_id=1, source_target_pairs={{0,16},{1,17},{2,18},{3,19},{4,20},{5,21},{6,22},{7,23},{8,24},{9,... | collective-permute-start | bytes 835592 | tf_op jit(solution)/shard_map/ppermute | solution.py:283
  32.0 13.8 %collective-permute-start.10 = (bf16[64,2176]{1,0:T(8,128)(2,1)S(1)}, bf16[64,2176]{1,0:T(8,128)(2,1)S(1)}, u32[]{:S(2)}, u32[]{:S(2)}) collective-permute-start(bf16[64,2176]{1,0:T(8,128)(2,1)S(1)} %collective-permute-done.6.refs_3_), channel_id=1, source_target_pairs={{0,16},{1,17},{2,18},{3,19},{4,20},{5,21},{6,22},{7,23},{8,24},{9,... | collective-permute-start | bytes 835592 | tf_op jit(solution)/shard_map/ppermute | solution.py:283
  33.1 16.7 %collective-permute-start.11 = (bf16[64,2176]{1,0:T(8,128)(2,1)S(1)}, bf16[64,2176]{1,0:T(8,128)(2,1)S(1)}, u32[]{:S(2)}, u32[]{:S(2)}) collective-permute-start(bf16[64,2176]{1,0:T(8,128)(2,1)S(1)} %collective-permute-done.1.refs_1_), channel_id=1, source_target_pairs={{0,2},{1,3},{2,0},{3,1},{4,6},{5,7},{6,4},{7,5},{8,10},{9,11},{10,... | collective-permute-start | bytes 835592 | tf_op jit(solution)/shard_map/ppermute | solution.py:283
  42.8 13.3 %collective-permute-start.13 = (bf16[64,2176]{1,0:T(8,128)(2,1)S(1)}, bf16[64,2176]{1,0:T(8,128)(2,1)S(1)}, u32[]{:S(2)}, u32[]{:S(2)}) collective-permute-start(bf16[64,2176]{1,0:T(8,128)(2,1)S(1)} %collective-permute-done.7.refs_3_), channel_id=1, source_target_pairs={{0,16},{1,17},{2,18},{3,19},{4,20},{5,21},{6,22},{7,23},{8,24},{9,... | collective-permute-start | bytes 835592 | tf_op jit(solution)/shard_map/ppermute | solution.py:283
  45.9 10.2 %collective-permute-start.9 = (bf16[64,2176]{1,0:T(8,128)(2,1)S(1)}, bf16[64,2176]{1,0:T(8,128)(2,1)S(1)}, u32[]{:S(2)}, u32[]{:S(2)}) collective-permute-start(bf16[64,2176]{1,0:T(8,128)(2,1)S(1)} %collective-permute-done.4.refs_1_), channel_id=1, source_target_pairs={{0,2},{1,3},{2,0},{3,1},{4,6},{5,7},{6,4},{7,5},{8,10},{9,11},{10,... | collective-permute-start | bytes 835592 | tf_op jit(solution)/shard_map/ppermute | solution.py:283
  48.2 12.4 %collective-permute-start.14 = (bf16[64,2176]{1,0:T(8,128)(2,1)S(1)}, bf16[64,2176]{1,0:T(8,128)(2,1)S(1)}, u32[]{:S(2)}, u32[]{:S(2)}) collective-permute-start(bf16[64,2176]{1,0:T(8,128)(2,1)S(1)} %collective-permute-done.7.refs_3_), channel_id=1, source_target_pairs={{0,2},{1,3},{2,0},{3,1},{4,6},{5,7},{6,4},{7,5},{8,10},{9,11},{10,... | collective-permute-start | bytes 835592 | tf_op jit(solution)/shard_map/ppermute | solution.py:283
  48.2 10.1 %collective-permute-start.15 = (bf16[64,2176]{1,0:T(8,128)(2,1)S(1)}, bf16[64,2176]{1,0:T(8,128)(2,1)S(1)}, u32[]{:S(2)}, u32[]{:S(2)}) collective-permute-start(bf16[64,2176]{1,0:T(8,128)(2,1)S(1)} %collective-permute-done.12.refs_3_), channel_id=1, source_target_pairs={{0,4},{1,5},{2,6},{3,7},{4,0},{5,1},{6,2},{7,3},{8,12},{9,13},{10,... | collective-permute-start | bytes 835592 | tf_op jit(solution)/shard_map/ppermute | solution.py:283
  56.1 10.8 %collective-permute-start.18 = (bf16[64,2048]{1,0:T(8,128)(2,1)S(1)}, bf16[64,2048]{1,0:T(8,128)(2,1)S(1)}, u32[]{:S(2)}, u32[]{:S(2)}) collective-permute-start(bf16[64,2048]{1,0:T(8,128)(2,1)S(1)} %get-tuple-element.67), channel_id=1, source_target_pairs={{0,2},{1,3},{2,0},{3,1},{4,6},{5,7},{6,4},{7,5},{8,10},{9,11},{10,... | collective-permute-start | bytes 786440 | tf_op jit(solution)/shard_map/ppermute | solution.py:283
  56.9 10.0 %collective-permute-start.17 = (bf16[64,2048]{1,0:T(8,128)(2,1)S(1)}, bf16[64,2048]{1,0:T(8,128)(2,1)S(1)}, u32[]{:S(2)}, u32[]{:S(2)}) collective-permute-start(bf16[64,2048]{1,0:T(8,128)(2,1)S(1)} %get-tuple-element.65), channel_id=1, source_target_pairs={{0,16},{1,17},{2,18},{3,19},{4,20},{5,21},{6,22},{7,23},{8,24},{9,... | collective-permute-start | bytes 786440 | tf_op jit(solution)/shard_map/ppermute | solution.py:283
  58.3 8.6 %collective-permute-start.16 = (bf16[64,2048]{1,0:T(8,128)(2,1)S(1)}, bf16[64,2048]{1,0:T(8,128)(2,1)S(1)}, u32[]{:S(2)}, u32[]{:S(2)}) collective-permute-start(bf16[64,2048]{1,0:T(8,128)(2,1)S(1)} %get-tuple-element.63), channel_id=1, source_target_pairs={{0,4},{1,5},{2,6},{3,7},{4,0},{5,1},{6,2},{7,3},{8,12},{9,13},{10,... | collective-permute-start | bytes 786440 | tf_op jit(solution)/shard_map/ppermute | solution.py:283
  66.9 6.7 %collective-permute-start.20 = (bf16[64,2048]{1,0:T(8,128)(2,1)S(1)}, bf16[64,2048]{1,0:T(8,128)(2,1)S(1)}, u32[]{:S(2)}, u32[]{:S(2)}) collective-permute-start(bf16[64,2048]{1,0:T(8,128)(2,1)S(1)} %get-tuple-element.70), channel_id=1, source_target_pairs={{0,4},{1,5},{2,6},{3,7},{4,0},{5,1},{6,2},{7,3},{8,12},{9,13},{10,... | collective-permute-start | bytes 786440 | tf_op jit(solution)/shard_map/ppermute | solution.py:283
  67.9 7.8 %collective-permute-start.21 = (bf16[64,2048]{1,0:T(8,128)(2,1)S(1)}, bf16[64,2048]{1,0:T(8,128)(2,1)S(1)}, u32[]{:S(2)}, u32[]{:S(2)}) collective-permute-start(bf16[64,2048]{1,0:T(8,128)(2,1)S(1)} %get-tuple-element.76), channel_id=1, source_target_pairs={{0,2},{1,3},{2,0},{3,1},{4,6},{5,7},{6,4},{7,5},{8,10},{9,11},{10,... | collective-permute-start | bytes 786440 | tf_op jit(solution)/shard_map/ppermute | solution.py:283
  68.6 8.6 %collective-permute-start.19 = (bf16[64,2048]{1,0:T(8,128)(2,1)S(1)}, bf16[64,2048]{1,0:T(8,128)(2,1)S(1)}, u32[]{:S(2)}, u32[]{:S(2)}) collective-permute-start(bf16[64,2048]{1,0:T(8,128)(2,1)S(1)} %add_convert_fusion.7), channel_id=1, source_target_pairs={{0,16},{1,17},{2,18},{3,19},{4,20},{5,21},{6,22},{7,23},{8,24},{9,... | collective-permute-start | bytes 786440 | tf_op jit(solution)/shard_map/ppermute | solution.py:283
  70.2 25.0 %collective-permute-start.27 = (bf16[64,2048]{1,0:T(8,128)(2,1)S(1)}, bf16[64,2048]{1,0:T(8,128)(2,1)S(1)}, u32[]{:S(2)}, u32[]{:S(2)}) collective-permute-start(bf16[64,2048]{1,0:T(8,128)(2,1)S(1)} %add_convert_fusion.3), channel_id=1, source_target_pairs={{0,8},{1,9},{2,10},{3,11},{4,12},{5,13},{6,14},{7,15},{8,0},{9,1},... | collective-permute-start | bytes 786440 | tf_op jit(solution)/shard_map/ppermute | solution.py:283
  72.5 15.7 %collective-permute-start.28 = (bf16[64,2048]{1,0:T(8,128)(2,1)S(1)}, bf16[64,2048]{1,0:T(8,128)(2,1)S(1)}, u32[]{:S(2)}, u32[]{:S(2)}) collective-permute-start(bf16[64,2048]{1,0:T(8,128)(2,1)S(1)} %get-tuple-element.85), channel_id=1, source_target_pairs={{0,16},{1,17},{2,18},{3,19},{4,20},{5,21},{6,22},{7,23},{8,24},{9,... | collective-permute-start | bytes 786440 | tf_op jit(solution)/shard_map/ppermute | solution.py:283
  75.6 10.4 %collective-permute-start.22 = (bf16[64,2048]{1,0:T(8,128)(2,1)S(1)}, bf16[64,2048]{1,0:T(8,128)(2,1)S(1)}, u32[]{:S(2)}, u32[]{:S(2)}) collective-permute-start(bf16[64,2048]{1,0:T(8,128)(2,1)S(1)} %add_convert_fusion.6), channel_id=1, source_target_pairs={{0,2},{1,3},{2,0},{3,1},{4,6},{5,7},{6,4},{7,5},{8,10},{9,11},{10,... | collective-permute-start | bytes 786440 | tf_op jit(solution)/shard_map/ppermute | solution.py:283
  77.1 9.6 %collective-permute-start.25 = (bf16[64,2048]{1,0:T(8,128)(2,1)S(1)}, bf16[64,2048]{1,0:T(8,128)(2,1)S(1)}, u32[]{:S(2)}, u32[]{:S(2)}) collective-permute-start(bf16[64,2048]{1,0:T(8,128)(2,1)S(1)} %get-tuple-element.81), channel_id=1, source_target_pairs={{0,16},{1,17},{2,18},{3,19},{4,20},{5,21},{6,22},{7,23},{8,24},{9,... | collective-permute-start | bytes 786440 | tf_op jit(solution)/shard_map/ppermute | solution.py:283
  84.4 10.8 %collective-permute-start.24 = (bf16[64,2048]{1,0:T(8,128)(2,1)S(1)}, bf16[64,2048]{1,0:T(8,128)(2,1)S(1)}, u32[]{:S(2)}, u32[]{:S(2)}) collective-permute-start(bf16[64,2048]{1,0:T(8,128)(2,1)S(1)} %get-tuple-element.78), channel_id=1, source_target_pairs={{0,2},{1,3},{2,0},{3,1},{4,6},{5,7},{6,4},{7,5},{8,10},{9,11},{10,... | collective-permute-start | bytes 786440 | tf_op jit(solution)/shard_map/ppermute | solution.py:283
  86.1 7.6 %collective-permute-start.29 = (bf16[64,2048]{1,0:T(8,128)(2,1)S(1)}, bf16[64,2048]{1,0:T(8,128)(2,1)S(1)}, u32[]{:S(2)}, u32[]{:S(2)}) collective-permute-start(bf16[64,2048]{1,0:T(8,128)(2,1)S(1)} %add_convert_fusion.2), channel_id=1, source_target_pairs={{0,2},{1,3},{2,0},{3,1},{4,6},{5,7},{6,4},{7,5},{8,10},{9,11},{10,... | collective-permute-start | bytes 786440 | tf_op jit(solution)/shard_map/ppermute | solution.py:283
  86.7 8.5 %collective-permute-start.23 = (bf16[64,2048]{1,0:T(8,128)(2,1)S(1)}, bf16[64,2048]{1,0:T(8,128)(2,1)S(1)}, u32[]{:S(2)}, u32[]{:S(2)}) collective-permute-start(bf16[64,2048]{1,0:T(8,128)(2,1)S(1)} %add_convert_fusion.5), channel_id=1, source_target_pairs={{0,16},{1,17},{2,18},{3,19},{4,20},{5,21},{6,22},{7,23},{8,24},{9,... | collective-permute-start | bytes 786440 | tf_op jit(solution)/shard_map/ppermute | solution.py:283
  88.2 8.9 %collective-permute-start.26 = (bf16[64,2048]{1,0:T(8,128)(2,1)S(1)}, bf16[64,2048]{1,0:T(8,128)(2,1)S(1)}, u32[]{:S(2)}, u32[]{:S(2)}) collective-permute-start(bf16[64,2048]{1,0:T(8,128)(2,1)S(1)} %add_convert_fusion.4), channel_id=1, source_target_pairs={{0,4},{1,5},{2,6},{3,7},{4,0},{5,1},{6,2},{7,3},{8,12},{9,13},{10,... | collective-permute-start | bytes 786440 | tf_op jit(solution)/shard_map/ppermute | solution.py:283
  93.8 8.3 %collective-permute-start.30 = (bf16[64,2048]{1,0:T(8,128)(2,1)S(1)}, bf16[64,2048]{1,0:T(8,128)(2,1)S(1)}, u32[]{:S(2)}, u32[]{:S(2)}) collective-permute-start(bf16[64,2048]{1,0:T(8,128)(2,1)S(1)} %add_convert_fusion.1), channel_id=1, source_target_pairs={{0,12},{1,13},{2,14},{3,15},{4,8},{5,9},{6,10},{7,11},{8,4},{9,5},... | collective-permute-start | bytes 786440 | tf_op jit(solution)/shard_map/ppermute | solution.py:283

commit v2 on v1

--- a/solution.py
+++ b/solution.py
@@ -172,37 +172,7 @@
     return (gate_act / (1.0 + jnp.exp(-gate_act)) * up_act * gates).astype(jnp.bfloat16)
 
 
-def hidden_kernel(me_ref, *refs):
-    *messages, weight, out_ref, rows_ref = refs
-    rows = messages[0].shape[0]
-    for i, message in enumerate(messages):
-        rows_ref[pl.ds(i * rows, rows), :] = message[...]
-    width, half = rows_ref.shape[1] - LANES, out_ref.shape[1]
-    out_ref[...] = hidden_units(me_ref, 0, rows_ref, weight, width, half)
-
-
-def own_hidden(me, messages, weight):
-    rows, columns = messages[0].shape
-    total = len(messages) * rows
-    width, half = columns - LANES, weight.shape[1] // 3
-    vmem = pl.BlockSpec(memory_space=pltpu.VMEM)
-    return pl.pallas_call(
-        hidden_kernel,
-        in_specs=[pl.BlockSpec(memory_space=pltpu.SMEM)] + [vmem] * (len(messages) + 1),
-        out_specs=vmem,
-        out_shape=pltpu.VMEM((total, half), jnp.bfloat16),
-        scratch_shapes=[pltpu.VMEM((total, columns), jnp.bfloat16)],
-        cost_estimate=pl.CostEstimate(
-            flops=4 * total * width * half,
-            bytes_accessed=4 * width * half + 2 * total * width,
-            transcendentals=total * half,
-        ),
-        compiler_params=pltpu.CompilerParams(vmem_limit_bytes=20 * 2**20),
-        name="own_hidden",
-    )(me, *messages, weight)
-
-
-def expert_kernel(me_ref, *refs, blocks, fetch, begun):
+def expert_kernel(me_ref, *refs, blocks, fetch):
     refs = list(refs)
 
     def take(count):
@@ -212,59 +182,50 @@
 
     messages = take(blocks)
     mine, other = take(2)
-    before = take(1) if begun else []
-    outs = take(blocks)
-    kept = take(1) if fetch else []
-    rows_ref, *sems = refs
-    rows, width = outs[0].shape
+    kept = None
+    if fetch:
+        *outs, kept, rows_ref, sem = refs
+        copy = pltpu.make_async_copy(other, kept, sem)
+        copy.start()
+        other = kept
+    else:
+        *outs, rows_ref = refs
+    width = outs[0].shape[1]
     half = mine.shape[1] // 3
-    copies = []
+    row = 0
+    for message in messages:
+        rows_ref[pl.ds(row, message.shape[0]), :] = message[...]
+        row += message.shape[0]
+    first = hidden_units(me_ref, 0, rows_ref, mine, width, half)
     if fetch:
-        for part in range(3):
-            at = pl.ds(part * half, half)
-            source, target = other.at[:, at], kept[0].at[:, at]
-            copies.append(pltpu.make_async_copy(source, target, sems[0].at[part]))
-        other = kept[0]
-    for copy in copies:
-        copy.start()
-    for i, message in enumerate(messages):
-        rows_ref[pl.ds(i * rows, rows), :] = message[...]
-    if begun:
-        first = before[0][...]
-    else:
-        first = hidden_units(me_ref, 0, rows_ref, mine, width, half)
-    for copy in copies:
         copy.wait()
     second = hidden_units(me_ref, 1, rows_ref, other, width, half)
     for j in range(width // half):
         at = pl.ds(j * half, half)
         answer = contract_last(first, mine[at, 2 * half :])
         answer += contract_last(second, other[at, 2 * half :])
-        for i in range(blocks):
-            outs[i][:, at] = answer[i * rows : (i + 1) * rows].astype(outs[i].dtype)
-
-
-def run_experts(me, messages, mine, other, before=None, fetch=False):
-    rows, columns = messages[0].shape
+        row = 0
+        for out in outs:
+            out[:, at] = answer[row : row + out.shape[0]].astype(out.dtype)
+            row += out.shape[0]
+
+
+def run_experts(me, messages, mine, other, rows_out, fetch=False):
+    columns = messages[0].shape[1]
     width, half = columns - LANES, mine.shape[1] // 3
-    blocks = len(messages)
-    total = blocks * rows
+    total = sum(message.shape[0] for message in messages)
     vmem = pl.BlockSpec(memory_space=pltpu.VMEM)
-    out_shape = [jax.ShapeDtypeStruct((rows, width), jnp.bfloat16)] * blocks
+    out_shape = [jax.ShapeDtypeStruct((n, width), jnp.bfloat16) for n in rows_out]
     scratch_shapes = [pltpu.VMEM((total, columns), jnp.bfloat16)]
     if fetch:
         out_shape.append(pltpu.VMEM(other.shape, jnp.bfloat16))
-        scratch_shapes.append(pltpu.SemaphoreType.DMA((3,)))
-    others = [] if before is None else [before]
+        scratch_shapes.append(pltpu.SemaphoreType.DMA)
     return list(
         pl.pallas_call(
-            functools.partial(
-                expert_kernel, blocks=blocks, fetch=fetch, begun=before is not None
-            ),
+            functools.partial(expert_kernel, blocks=len(messages), fetch=fetch),
             in_specs=[pl.BlockSpec(memory_space=pltpu.SMEM)]
-            + [vmem] * (blocks + 1)
-            + [pl.BlockSpec(memory_space=pl.ANY) if fetch else vmem]
-            + [vmem] * len(others),
+            + [vmem] * (len(messages) + 1)
+            + [pl.BlockSpec(memory_space=pl.ANY) if fetch else vmem],
             out_specs=[vmem] * len(out_shape),
             out_shape=out_shape,
             scratch_shapes=scratch_shapes,
@@ -273,9 +234,9 @@
                 bytes_accessed=12 * width * half + 4 * total * width,
                 transcendentals=2 * total * half,
             ),
-            compiler_params=pltpu.CompilerParams(vmem_limit_bytes=20 * 2**20),
+            compiler_params=pltpu.CompilerParams(vmem_limit_bytes=24 * 2**20),
             name="run_experts",
-        )(me, *messages, mine, other, *others)
+        )(me, *messages, mine, other)
     )
 
 
@@ -317,52 +278,45 @@
     pair = jnp.stack([me, me ^ 1]).astype(jnp.int32)
     s0 = pack(tokens, route_gates, expert_ids, slot_index)
     s2 = send(s0, z2)
-    s1 = send(s0, z1)
     x0 = send(s0, x)
     y0 = send(s0, y)
     mine = scale_weights(
         (gate_quant, up_quant, down_quant), (gate_scale, up_scale, down_scale)
     )
-    swapped = send(after(mine, s2, s1, x0, y0), core)
-    s3 = send(s2, z1)
+    swapped = send(after(mine, s2, x0, y0), core)
+    s13 = send(jnp.concatenate([s0, s2]), z1)
     y2 = send(after(s2, y0), y)
     x2 = send(after(s2, x0), x)
-    begun = own_hidden(pair, (s0, x0, y0, s1), mine)
-    d0 = send(after(x0, y2, s3, begun), y)
-    d2 = send(after(y2, x2, s3, begun), x)
-    x3 = send(after(s3, x2), x)
-    y3 = send(after(s3, y2), y)
-    last = (s0, x0, y0, s1)
-    s2, s3, x2, y2, swapped = run_experts(pair, (s2, s3, x2, y2), mine, swapped, fetch=True)
-
-    def work(*messages):
-        return run_experts(pair, messages, mine, swapped)
-
-    d3 = send(after(x3, s2), y)
-    x1 = send(after(s1, x3, d0, s2), x)
-    d1 = send(after(d0, s2), z1)
-    y1 = send(after(s1, d0, s2), y)
-    d2, x3, y3, d0 = work(after(d2, s2), x3, y3, d0)
-    bx2 = send(after(x2, d3, x1, d2), x)
-    by2 = send(after(y2, d3, x1, d2), y)
-    bd2 = send(after(d2, d3, x1, d1), z1)
-    d3, x1, y1, d1 = work(after(d3, d2), x1, y1, d1)
-    bd3 = send(after(add(d3, bd2), bx2, by2), x)
-    bd1 = send(after(d1, bd2, bx2, by2), z1)
-    by1 = send(after(y1, bd2, bx2, by2), y)
-    bx3 = send(after(x3, bd2, bx2, by2, d3), x)
-    bs2 = send(after(add(s2, bx2, by2), bd2, d3), z2)
+    d0 = send(after(x0, s2), y)
+    d2 = send(after(y2, x2), x)
+    x13 = send(after(s13, x2), x)
+    y13 = send(after(s13, y2), y)
+    d13 = send(jnp.concatenate([d0, d2]), z1)
+    rows = s0.shape[0]
+    x02, y02, d02, s0, s2, swapped = run_experts(
+        pair,
+        (x0, x2, y0, y2, d0, d2, s0, s2),
+        mine,
+        swapped,
+        (2 * rows, 2 * rows, 2 * rows, rows, rows),
+        fetch=True,
+    )
+    bx02 = send(after(x02, x13, y13), x)
+    by02 = send(after(y02, x13, y13), y)
+    bd02 = send(after(d02, d13), z1)
+    d1, d3, x1, x3, y1, y3, s1, s3 = run_experts(
+        pair, (after(d13, d02), x13, y13, s13), mine, swapped, (rows,) * 8
+    )
+    bd3 = send(after(add(d3, bd02[rows:]), bx02, by02), x)
+    bd1 = send(after(add(d1, bd02[:rows]), bx02, by02), y)
+    bs2 = send(after(add(s2, bx02[rows:], by02[rows:]), bd02, s3), z2)
+    by1 = send(after(y1, bx02, by02, bd02), y)
+    bx3 = send(after(x3, bd3), x)
     by3 = send(add(y3, bd3), y)
-    bd0 = send(after(add(d0, bd1), by1), y)
-    bx1 = send(after(x1, bd3, by1), x)
-    s0, x0, y0, s1 = run_experts(
-        pair, (after(last[0], d3, bd3, bd1), *last[1:]), mine, swapped, before=begun
-    )
-    by0 = send(y0, y)
+    bx1 = send(after(add(x1, bd1), bd3, bx3), x)
     bs3 = send(add(s3, bx3, by3), z3)
     bs1 = send(add(s1, bx1, by1), z1)
-    bx0 = send(add(x0, bd0), x)
-    return add(s0, bx0, by0, bs1, bs2, bs3)
+    return add(s0, bx02[:rows], by02[:rows], bs1, bs2, bs3)
 
 
 def solution(mesh):

time: 103 us -> 96.4 us (0.936)
  Pallas kernels: 37.6 us -> 27.5 us
  waiting for transfers between devices: 25.4 us -> 30.9 us
  starting transfers between devices: 38.3 us -> 36 us
    pallas_call x5 -> x2, Pallas kernels: 30.1 us -> 19.9 us  [run_experts(): pl.pallas_call(functools.partial(expert_kernel, blocks=len(messages), fet...]
    ppermute x31 -> x24, waiting for transfers between devices: 25.4 us -> 30.9 us  [hop(): return lax.ppermute(value, AXES, [(i, i ^ bit) for i in range(devices)])]
    ppermute x31 -> x24, starting transfers between devices: 38.3 us -> 36 us  [hop(): return lax.ppermute(value, AXES, [(i, i ^ bit) for i in range(devices)])]
  transfers between devices with their start and end apart: 31 -> 24, of which waited for: 11 -> 11; matrix products, arithmetic and copies ran while one was open for 1% -> 1% of each run, Pallas kernels for 35% -> 27%
where the time goes in v2:
time: 96.4 us; the launch traced here: 96.2 us
  starting transfers between devices  36 us (37%)
  waiting for transfers between devices  30.9 us (32%)
  Pallas kernels  27.5 us (29%)
  other arithmetic  1.63 us (2%)
    ppermute x24, starting transfers between devices, hop(): return lax.ppermute(value, AXES, [(i, i ^ bit) for i in range(devices)])  36 us
    ppermute x24, waiting for transfers between devices, hop(): return lax.ppermute(value, AXES, [(i, i ^ bit) for i in range(devices)])  30.9 us
    pallas_call x2, Pallas kernels, run_experts(): pl.pallas_call(functools.partial(expert_kernel, blocks=len(messages), fet...  19.9 us
    pallas_call x1, Pallas kernels, scale_weights(): pl.pallas_call(functools.partial(scale_kernel, pieces=pieces), in_specs=[...  5.73 us
  transfers between devices with their start and end apart: 24, of which 11 were waited for; matrix products, arithmetic and copies ran while one was open for 1% of the time, Pallas kernels for 27%

profile of v2, /device:TPU:0, one launch (start us, length us, event | category | flops | bytes accessed | tf_op | source)
XLA Modules:
  0.0 96.2 jit_solution(18130088027529301960)
XLA Ops:
  0.0 1.8 %pack.1.refs_6_ = bf16[64,2176]{1,0:T(8,128)(2,1)} custom-call(f32[8,64]{1,0:T(8,128)} %bitcast.14, s32[8,64]{1,0:T(8,128)} %bitcast.15, s32[8,64]{1,0:T(8,128)} %bitcast.16, bf16[64,2048]{1,0:T(8,128)(2,1)} %tokens_ref.1), custom_call_target="tpu_custom_call" | custom-call | flops 131072 | bytes 524288 | tf_op jit(solution)/shard_map/pack/pallas_call | solution.py:89
  1.8 4.0 %collective-permute-start.1 = (bf16[64,2176]{1,0:T(8,128)(2,1)}, bf16[64,2176]{1,0:T(8,128)(2,1)S(1)}, u32[]{:S(2)}, u32[]{:S(2)}) collective-permute-start(bf16[64,2176]{1,0:T(8,128)(2,1)} %pack.1.refs_6_), channel_id=1, source_target_pairs={{0,8},{1,9},{2,10},{3,11},{4,12},{5,13},{6,14},{7,15},{8,0},{9,1},... | collective-permute-start | bytes 835592 | tf_op jit(solution)/shard_map/ppermute | solution.py:244
  5.9 1.5 %collective-permute-start = (bf16[64,2176]{1,0:T(8,128)(2,1)}, bf16[64,2176]{1,0:T(8,128)(2,1)S(1)}, u32[]{:S(2)}, u32[]{:S(2)}) collective-permute-start(bf16[64,2176]{1,0:T(8,128)(2,1)} %pack.1.refs_6_), channel_id=1, source_target_pairs={{0,16},{1,17},{2,18},{3,19},{4,20},{5,21},{6,22},{7,23},{8,24},{9,... | collective-permute-start | bytes 835592 | tf_op jit(solution)/shard_map/ppermute | solution.py:244
  7.4 1.5 %collective-permute-start.3 = (bf16[64,2176]{1,0:T(8,128)(2,1)}, bf16[64,2176]{1,0:T(8,128)(2,1)S(1)}, u32[]{:S(2)}, u32[]{:S(2)}) collective-permute-start(bf16[64,2176]{1,0:T(8,128)(2,1)} %pack.1.refs_6_), channel_id=1, source_target_pairs={{0,2},{1,3},{2,0},{3,1},{4,6},{5,7},{6,4},{7,5},{8,10},{9,11},{10,... | collective-permute-start | bytes 835592 | tf_op jit(solution)/shard_map/ppermute | solution.py:244
  8.9 0.0 copy-start
  8.9 5.7 %scale_weights.1.refs_8_.refs_4_ = bf16[2048,1536]{1,0:T(8,128)(2,1)} custom-call(f32[4,16]{1,0:T(4,128)} %bitcast.17, f32[4,16]{1,0:T(4,128)} %bitcast.18, f32[4,16]{1,0:T(4,128)} %bitcast.19, bf16[1,2048,512]{2,1,0:T(8,128)(2,1)} %refs_3_.1, bf16[1,2048,512]{2,1,0:T(8,128)(2,1)} %refs_4_.1, bf16[1,2048,512]{2,1,0:T(8,128)(2,1)} %refs_5_.1), custom_call_target="tpu_custom_call" | custom-call | flops 3145728 | bytes 12582912 | tf_op jit(solution)/shard_map/scale_weights/pallas_call | solution.py:142
  14.6 4.1 %collective-permute-done.1.refs_7_ = bf16[64,2176]{1,0:T(8,128)(2,1)S(1)} collective-permute-done((bf16[64,2176]{1,0:T(8,128)(2,1)}, bf16[64,2176]{1,0:T(8,128)(2,1)S(1)}, u32[]{:S(2)}, u32[]{:S(2)}) %collective-permute-start.1) | collective-permute-done | bytes 278560 | tf_op jit(solution)/shard_map/ppermute | solution.py:244
  18.7 0.0 collective-permute-done.refs_0_
  18.7 0.0 collective-permute-done.3.refs_2_
  18.7 0.0 collective-permute-start.7
  18.7 0.0 copy-done
  18.8 0.9 collective-permute-start.8
  19.7 1.5 %collective-permute-start.2 = (bf16[64,2176]{1,0:T(8,128)(2,1)S(1)}, bf16[64,2176]{1,0:T(8,128)(2,1)S(1)}, u32[]{:S(2)}, u32[]{:S(2)}) collective-permute-start(bf16[64,2176]{1,0:T(8,128)(2,1)S(1)} %collective-permute-done.1.refs_7_), channel_id=1, source_target_pairs={{0,16},{1,17},{2,18},{3,19},{4,20},{5,21},{6,22},{7,23},{8,24},{9,... | collective-permute-start | bytes 835592 | tf_op jit(solution)/shard_map/ppermute | solution.py:244
  21.2 1.5 %collective-permute-start.4 = (bf16[64,2176]{1,0:T(8,128)(2,1)S(1)}, bf16[64,2176]{1,0:T(8,128)(2,1)S(1)}, u32[]{:S(2)}, u32[]{:S(2)}) collective-permute-start(bf16[64,2176]{1,0:T(8,128)(2,1)S(1)} %collective-permute-done.1.refs_7_), channel_id=1, source_target_pairs={{0,2},{1,3},{2,0},{3,1},{4,6},{5,7},{6,4},{7,5},{8,10},{9,11},{10,... | collective-permute-start | bytes 835592 | tf_op jit(solution)/shard_map/ppermute | solution.py:244
  22.7 0.5 collective-permute-start.5
  23.2 5.3 %collective-permute-done.2.refs_1_ = bf16[64,2176]{1,0:T(8,128)(2,1)S(1)} collective-permute-done((bf16[64,2176]{1,0:T(8,128)(2,1)S(1)}, bf16[64,2176]{1,0:T(8,128)(2,1)S(1)}, u32[]{:S(2)}, u32[]{:S(2)}) %collective-permute-start.2) | collective-permute-done | bytes 278560 | tf_op jit(solution)/shard_map/ppermute | solution.py:244
  28.4 2.3 %collective-permute-done.4.refs_3_ = bf16[64,2176]{1,0:T(8,128)(2,1)S(1)} collective-permute-done((bf16[64,2176]{1,0:T(8,128)(2,1)S(1)}, bf16[64,2176]{1,0:T(8,128)(2,1)S(1)}, u32[]{:S(2)}, u32[]{:S(2)}) %collective-permute-start.4) | collective-permute-done | bytes 278560 | tf_op jit(solution)/shard_map/ppermute | solution.py:244
  30.7 0.5 collective-permute-start.6
  31.2 0.1 pad_add_fusion.me_ref
  31.3 2.6 %collective-permute-done.8.refs_3_ = bf16[128,2176]{1,0:T(8,128)(2,1)S(1)} collective-permute-done((bf16[128,2176]{1,0:T(8,128)(2,1)S(1)}, bf16[128,2176]{1,0:T(8,128)(2,1)S(1)}, u32[]{:S(2)}, u32[]{:S(2)}) %collective-permute-start.8) | collective-permute-done | bytes 557088 | tf_op jit(solution)/shard_map/ppermute | solution.py:244
  33.9 1.5 %collective-permute-start.9 = (bf16[128,2176]{1,0:T(8,128)(2,1)S(1)}, bf16[128,2176]{1,0:T(8,128)(2,1)S(1)}, u32[]{:S(2)}, u32[]{:S(2)}) collective-permute-start(bf16[128,2176]{1,0:T(8,128)(2,1)S(1)} %collective-permute-done.8.refs_3_), channel_id=1, source_target_pairs={{0,16},{1,17},{2,18},{3,19},{4,20},{5,21},{6,22},{7,23},{8,24},{9,... | collective-permute-start | bytes 1671176 | tf_op jit(solution)/shard_map/ppermute | solution.py:244
  35.4 1.5 %collective-permute-start.10 = (bf16[128,2176]{1,0:T(8,128)(2,1)S(1)}, bf16[128,2176]{1,0:T(8,128)(2,1)S(1)}, u32[]{:S(2)}, u32[]{:S(2)}) collective-permute-start(bf16[128,2176]{1,0:T(8,128)(2,1)S(1)} %collective-permute-done.8.refs_3_), channel_id=1, source_target_pairs={{0,2},{1,3},{2,0},{3,1},{4,6},{5,7},{6,4},{7,5},{8,10},{9,11},{10,... | collective-permute-start | bytes 1671176 | tf_op jit(solution)/shard_map/ppermute | solution.py:244
  36.9 0.0 collective-permute-done.5.refs_4_
  36.9 1.4 %collective-permute-done.6.refs_5_ = bf16[64,2176]{1,0:T(8,128)(2,1)S(1)} collective-permute-done((bf16[64,2176]{1,0:T(8,128)(2,1)S(1)}, bf16[64,2176]{1,0:T(8,128)(2,1)S(1)}, u32[]{:S(2)}, u32[]{:S(2)}) %collective-permute-start.6) | collective-permute-done | bytes 278560 | tf_op jit(solution)/shard_map/ppermute | solution.py:244
  38.4 1.7 %collective-permute-start.13 = (bf16[128,2176]{1,0:T(8,128)(2,1)S(1)}, bf16[128,2176]{1,0:T(8,128)(2,1)S(1)}, u32[]{:S(2)}, u32[]{:S(2)}) collective-permute-start(bf16[128,2176]{1,0:T(8,128)(2,1)S(1)} %pad_maximum_fusion.1), channel_id=1, source_target_pairs={{0,4},{1,5},{2,6},{3,7},{4,0},{5,1},{6,2},{7,3},{8,12},{9,13},{10,... | collective-permute-start | bytes 1671176 | tf_op jit(solution)/shard_map/ppermute | solution.py:244
  40.1 0.0 collective-permute-done.7.refs_9_
  40.1 10.2 %run_experts.2 = (bf16[128,2048]{1,0:T(8,128)(2,1)S(1)}, bf16[128,2048]{1,0:T(8,128)(2,1)S(1)}, bf16[128,2048]{1,0:T(8,128)(2,1)S(1)}, bf16[64,2048]{1,0:T(8,128...) custom-call(s32[2]{0:T(128)S(1)} %pad_add_fusion.me_ref, ...), custom_call_target="tpu_custom_call" | custom-call | flops 6442450944 | bytes 16777216 | tf_op jit(solution)/shard_map/run_experts/pallas_call | solution.py:224
  50.3 0.0 collective-permute-done.9.refs_1_
  50.3 0.0 collective-permute-done.10.refs_2_
  50.4 1.6 %collective-permute-start.12 = (bf16[128,2048]{1,0:T(8,128)(2,1)S(1)}, bf16[128,2048]{1,0:T(8,128)(2,1)S(1)}, u32[]{:S(2)}, u32[]{:S(2)}) collective-permute-start(bf16[128,2048]{1,0:T(8,128)(2,1)S(1)} %get-tuple-element.47), channel_id=1, source_target_pairs={{0,2},{1,3},{2,0},{3,1},{4,6},{5,7},{6,4},{7,5},{8,10},{9,11},{10,... | collective-permute-start | bytes 1572872 | tf_op jit(solution)/shard_map/ppermute | solution.py:244
  51.9 0.0 collective-permute-start.11
  51.9 0.0 collective-permute-done.13.refs_0_
  51.9 0.7 collective-permute-start.14
  52.6 9.7 %run_experts.3 = (bf16[64,2048]{1,0:T(8,128)(2,1)S(1)}, bf16[64,2048]{1,0:T(8,128)(2,1)S(1)}, bf16[64,2048]{1,0:T(8,128)(2,1)S(1)}, bf16[64,2048]{1,0:T(8,128)(2...) custom-call(s32[2]{0:T(128)S(1)} %pad_add_fusion.me_ref, ...), custom_call_target="tpu_custom_call" | custom-call | flops 6442450944 | bytes 16777216 | tf_op jit(solution)/shard_map/run_experts/pallas_call | solution.py:224
  62.3 1.3 %collective-permute-done.14 = bf16[128,2048]{1,0:T(8,128)(2,1)S(1)} collective-permute-done((bf16[128,2048]{1,0:T(8,128)(2,1)S(1)}, bf16[128,2048]{1,0:T(8,128)(2,1)S(1)}, u32[]{:S(2)}, u32[]{:S(2)}) %collective-permute-start.14) | collective-permute-done | bytes 524320 | tf_op jit(solution)/shard_map/ppermute | solution.py:244
  63.6 0.1 add_convert_fusion.7
  63.8 0.0 collective-permute-done.12
  63.8 0.0 collective-permute-done.11
  63.8 0.6 collective-permute-start.15
  64.3 1.5 %collective-permute-start.16 = (bf16[64,2048]{1,0:T(8,128)(2,1)S(1)}, bf16[64,2048]{1,0:T(8,128)(2,1)S(1)}, u32[]{:S(2)}, u32[]{:S(2)}) collective-permute-start(bf16[64,2048]{1,0:T(8,128)(2,1)S(1)} %get-tuple-element.57), channel_id=1, source_target_pairs={{0,16},{1,17},{2,18},{3,19},{4,20},{5,21},{6,22},{7,23},{8,24},{9,... | collective-permute-start | bytes 786440 | tf_op jit(solution)/shard_map/ppermute | solution.py:244
  65.8 1.6 %collective-permute-start.19 = (bf16[64,2048]{1,0:T(8,128)(2,1)S(1)}, bf16[64,2048]{1,0:T(8,128)(2,1)S(1)}, u32[]{:S(2)}, u32[]{:S(2)}) collective-permute-start(bf16[64,2048]{1,0:T(8,128)(2,1)S(1)} %get-tuple-element.62), channel_id=1, source_target_pairs={{0,2},{1,3},{2,0},{3,1},{4,6},{5,7},{6,4},{7,5},{8,10},{9,11},{10,... | collective-permute-start | bytes 786440 | tf_op jit(solution)/shard_map/ppermute | solution.py:244
  67.4 0.1 add_convert_fusion.3
  67.5 3.0 %collective-permute-start.21 = (bf16[64,2048]{1,0:T(8,128)(2,1)S(1)}, bf16[64,2048]{1,0:T(8,128)(2,1)S(1)}, u32[]{:S(2)}, u32[]{:S(2)}) collective-permute-start(bf16[64,2048]{1,0:T(8,128)(2,1)S(1)} %add_convert_fusion.3), channel_id=1, source_target_pairs={{0,8},{1,9},{2,10},{3,11},{4,12},{5,13},{6,14},{7,15},{8,0},{9,1},... | collective-permute-start | bytes 786440 | tf_op jit(solution)/shard_map/ppermute | solution.py:244
  70.5 1.7 %collective-permute-done.16 = bf16[64,2048]{1,0:T(8,128)(2,1)S(1)} collective-permute-done((bf16[64,2048]{1,0:T(8,128)(2,1)S(1)}, bf16[64,2048]{1,0:T(8,128)(2,1)S(1)}, u32[]{:S(2)}, u32[]{:S(2)}) %collective-permute-start.16) | collective-permute-done | bytes 262176 | tf_op jit(solution)/shard_map/ppermute | solution.py:244
  72.2 1.3 %collective-permute-start.17 = (bf16[64,2048]{1,0:T(8,128)(2,1)S(1)}, bf16[64,2048]{1,0:T(8,128)(2,1)S(1)}, u32[]{:S(2)}, u32[]{:S(2)}) collective-permute-start(bf16[64,2048]{1,0:T(8,128)(2,1)S(1)} %get-tuple-element.59), channel_id=1, source_target_pairs={{0,16},{1,17},{2,18},{3,19},{4,20},{5,21},{6,22},{7,23},{8,24},{9,... | collective-permute-start | bytes 786440 | tf_op jit(solution)/shard_map/ppermute | solution.py:244
  73.5 0.1 add_convert_fusion.2
  73.6 2.8 %collective-permute-start.22 = (bf16[64,2048]{1,0:T(8,128)(2,1)S(1)}, bf16[64,2048]{1,0:T(8,128)(2,1)S(1)}, u32[]{:S(2)}, u32[]{:S(2)}) collective-permute-start(bf16[64,2048]{1,0:T(8,128)(2,1)S(1)} %add_convert_fusion.2), channel_id=1, source_target_pairs={{0,2},{1,3},{2,0},{3,1},{4,6},{5,7},{6,4},{7,5},{8,10},{9,11},{10,... | collective-permute-start | bytes 786440 | tf_op jit(solution)/shard_map/ppermute | solution.py:244
  76.4 0.0 collective-permute-done.15
  76.4 0.1 add_convert_fusion.6
  76.5 4.5 %collective-permute-done.17 = bf16[64,2048]{1,0:T(8,128)(2,1)S(1)} collective-permute-done((bf16[64,2048]{1,0:T(8,128)(2,1)S(1)}, bf16[64,2048]{1,0:T(8,128)(2,1)S(1)}, u32[]{:S(2)}, u32[]{:S(2)}) %collective-permute-start.17) | collective-permute-done | bytes 262176 | tf_op jit(solution)/shard_map/ppermute | solution.py:244
  81.0 1.2 %collective-permute-start.18 = (bf16[64,2048]{1,0:T(8,128)(2,1)S(1)}, bf16[64,2048]{1,0:T(8,128)(2,1)S(1)}, u32[]{:S(2)}, u32[]{:S(2)}) collective-permute-start(bf16[64,2048]{1,0:T(8,128)(2,1)S(1)} %add_convert_fusion.6), channel_id=1, source_target_pairs={{0,16},{1,17},{2,18},{3,19},{4,20},{5,21},{6,22},{7,23},{8,24},{9,... | collective-permute-start | bytes 786440 | tf_op jit(solution)/shard_map/ppermute | solution.py:244
  82.1 0.0 collective-permute-done.22
  82.1 0.1 add_convert_fusion.1
  82.2 4.8 %collective-permute-start.23 = (bf16[64,2048]{1,0:T(8,128)(2,1)S(1)}, bf16[64,2048]{1,0:T(8,128)(2,1)S(1)}, u32[]{:S(2)}, u32[]{:S(2)}) collective-permute-start(bf16[64,2048]{1,0:T(8,128)(2,1)S(1)} %add_convert_fusion.1), channel_id=1, source_target_pairs={{0,12},{1,13},{2,14},{3,15},{4,8},{5,9},{6,10},{7,11},{8,4},{9,5},... | collective-permute-start | bytes 786440 | tf_op jit(solution)/shard_map/ppermute | solution.py:244
  87.0 0.0 collective-permute-done.19
  87.0 0.3 collective-permute-done.18
  87.3 0.1 add_convert_fusion.4
  87.4 0.3 collective-permute-start.20
  87.7 0.0 collective-permute-done.21
  87.7 4.8 %collective-permute-done.23 = bf16[64,2048]{1,0:T(8,128)(2,1)S(1)} collective-permute-done((bf16[64,2048]{1,0:T(8,128)(2,1)S(1)}, bf16[64,2048]{1,0:T(8,128)(2,1)S(1)}, u32[]{:S(2)}, u32[]{:S(2)}) %collective-permute-start.23) | collective-permute-done | bytes 262176 | tf_op jit(solution)/shard_map/ppermute | solution.py:244
  92.6 2.7 %collective-permute-done.20 = bf16[64,2048]{1,0:T(8,128)(2,1)S(1)} collective-permute-done((bf16[64,2048]{1,0:T(8,128)(2,1)S(1)}, bf16[64,2048]{1,0:T(8,128)(2,1)S(1)}, u32[]{:S(2)}, u32[]{:S(2)}) %collective-permute-start.20) | collective-permute-done | bytes 262176 | tf_op jit(solution)/shard_map/ppermute | solution.py:244
  95.3 0.9 add_convert_fusion
  (2 shorter events, 0.1 us)
Async XLA Ops:
  1.8 16.9 %collective-permute-start.1 = (bf16[64,2176]{1,0:T(8,128)(2,1)}, bf16[64,2176]{1,0:T(8,128)(2,1)S(1)}, u32[]{:S(2)}, u32[]{:S(2)}) collective-permute-start(bf16[64,2176]{1,0:T(8,128)(2,1)} %pack.1.refs_6_), channel_id=1, source_target_pairs={{0,8},{1,9},{2,10},{3,11},{4,12},{5,13},{6,14},{7,15},{8,0},{9,1},... | collective-permute-start | bytes 835592 | tf_op jit(solution)/shard_map/ppermute | solution.py:244
  5.9 12.8 %collective-permute-start = (bf16[64,2176]{1,0:T(8,128)(2,1)}, bf16[64,2176]{1,0:T(8,128)(2,1)S(1)}, u32[]{:S(2)}, u32[]{:S(2)}) collective-permute-start(bf16[64,2176]{1,0:T(8,128)(2,1)} %pack.1.refs_6_), channel_id=1, source_target_pairs={{0,16},{1,17},{2,18},{3,19},{4,20},{5,21},{6,22},{7,23},{8,24},{9,... | collective-permute-start | bytes 835592 | tf_op jit(solution)/shard_map/ppermute | solution.py:244
  7.4 11.3 %collective-permute-start.3 = (bf16[64,2176]{1,0:T(8,128)(2,1)}, bf16[64,2176]{1,0:T(8,128)(2,1)S(1)}, u32[]{:S(2)}, u32[]{:S(2)}) collective-permute-start(bf16[64,2176]{1,0:T(8,128)(2,1)} %pack.1.refs_6_), channel_id=1, source_target_pairs={{0,2},{1,3},{2,0},{3,1},{4,6},{5,7},{6,4},{7,5},{8,10},{9,11},{10,... | collective-permute-start | bytes 835592 | tf_op jit(solution)/shard_map/ppermute | solution.py:244
  8.9 9.8 %copy-start = (bf16[64,2176]{1,0:T(8,128)(2,1)S(1)}, bf16[64,2176]{1,0:T(8,128)(2,1)}, u32[]{:S(2)}) copy-start(bf16[64,2176]{1,0:T(8,128)(2,1)} %pack.1.refs_6_) | copy-start | bytes 835588
  18.7 21.4 %collective-permute-start.7 = (bf16[2048,1536]{1,0:T(8,128)(2,1)}, bf16[2048,1536]{1,0:T(8,128)(2,1)}, u32[]{:S(2)}, u32[]{:S(2)}) collective-permute-start(bf16[2048,1536]{1,0:T(8,128)(2,1)} %scale_weights.1.refs_8_.refs_4_), channel_id=1, source_target_pairs={{0,1},{1,0},{2,3},{3,2},{4,5},{5,4},{6,7},{7,6},{8,9},{9,8},{10,11... | collective-permute-start | bytes 18874376 | tf_op jit(solution)/shard_map/ppermute | solution.py:244
  18.8 15.1 %collective-permute-start.8 = (bf16[128,2176]{1,0:T(8,128)(2,1)S(1)}, bf16[128,2176]{1,0:T(8,128)(2,1)S(1)}, u32[]{:S(2)}, u32[]{:S(2)}) collective-permute-start(bf16[128,2176]{1,0:T(8,128)(2,1)S(1)} %pad_maximum_fusion), channel_id=1, source_target_pairs={{0,4},{1,5},{2,6},{3,7},{4,0},{5,1},{6,2},{7,3},{8,12},{9,13},{10,... | collective-permute-start | bytes 1671176 | tf_op jit(solution)/shard_map/ppermute | solution.py:244
  19.7 8.8 %collective-permute-start.2 = (bf16[64,2176]{1,0:T(8,128)(2,1)S(1)}, bf16[64,2176]{1,0:T(8,128)(2,1)S(1)}, u32[]{:S(2)}, u32[]{:S(2)}) collective-permute-start(bf16[64,2176]{1,0:T(8,128)(2,1)S(1)} %collective-permute-done.1.refs_7_), channel_id=1, source_target_pairs={{0,16},{1,17},{2,18},{3,19},{4,20},{5,21},{6,22},{7,23},{8,24},{9,... | collective-permute-start | bytes 835592 | tf_op jit(solution)/shard_map/ppermute | solution.py:244
  21.2 9.5 %collective-permute-start.4 = (bf16[64,2176]{1,0:T(8,128)(2,1)S(1)}, bf16[64,2176]{1,0:T(8,128)(2,1)S(1)}, u32[]{:S(2)}, u32[]{:S(2)}) collective-permute-start(bf16[64,2176]{1,0:T(8,128)(2,1)S(1)} %collective-permute-done.1.refs_7_), channel_id=1, source_target_pairs={{0,2},{1,3},{2,0},{3,1},{4,6},{5,7},{6,4},{7,5},{8,10},{9,11},{10,... | collective-permute-start | bytes 835592 | tf_op jit(solution)/shard_map/ppermute | solution.py:244
  22.7 14.2 %collective-permute-start.5 = (bf16[64,2176]{1,0:T(8,128)(2,1)S(1)}, bf16[64,2176]{1,0:T(8,128)(2,1)S(1)}, u32[]{:S(2)}, u32[]{:S(2)}) collective-permute-start(bf16[64,2176]{1,0:T(8,128)(2,1)S(1)} %collective-permute-done.refs_0_), channel_id=1, source_target_pairs={{0,2},{1,3},{2,0},{3,1},{4,6},{5,7},{6,4},{7,5},{8,10},{9,11},{10,... | collective-permute-start | bytes 835592 | tf_op jit(solution)/shard_map/ppermute | solution.py:244
  30.7 7.6 %collective-permute-start.6 = (bf16[64,2176]{1,0:T(8,128)(2,1)S(1)}, bf16[64,2176]{1,0:T(8,128)(2,1)S(1)}, u32[]{:S(2)}, u32[]{:S(2)}) collective-permute-start(bf16[64,2176]{1,0:T(8,128)(2,1)S(1)} %collective-permute-done.4.refs_3_), channel_id=1, source_target_pairs={{0,16},{1,17},{2,18},{3,19},{4,20},{5,21},{6,22},{7,23},{8,24},{9,... | collective-permute-start | bytes 835592 | tf_op jit(solution)/shard_map/ppermute | solution.py:244
  33.9 16.5 %collective-permute-start.9 = (bf16[128,2176]{1,0:T(8,128)(2,1)S(1)}, bf16[128,2176]{1,0:T(8,128)(2,1)S(1)}, u32[]{:S(2)}, u32[]{:S(2)}) collective-permute-start(bf16[128,2176]{1,0:T(8,128)(2,1)S(1)} %collective-permute-done.8.refs_3_), channel_id=1, source_target_pairs={{0,16},{1,17},{2,18},{3,19},{4,20},{5,21},{6,22},{7,23},{8,24},{9,... | collective-permute-start | bytes 1671176 | tf_op jit(solution)/shard_map/ppermute | solution.py:244
  35.4 14.9 %collective-permute-start.10 = (bf16[128,2176]{1,0:T(8,128)(2,1)S(1)}, bf16[128,2176]{1,0:T(8,128)(2,1)S(1)}, u32[]{:S(2)}, u32[]{:S(2)}) collective-permute-start(bf16[128,2176]{1,0:T(8,128)(2,1)S(1)} %collective-permute-done.8.refs_3_), channel_id=1, source_target_pairs={{0,2},{1,3},{2,0},{3,1},{4,6},{5,7},{6,4},{7,5},{8,10},{9,11},{10,... | collective-permute-start | bytes 1671176 | tf_op jit(solution)/shard_map/ppermute | solution.py:244
  38.4 13.6 %collective-permute-start.13 = (bf16[128,2176]{1,0:T(8,128)(2,1)S(1)}, bf16[128,2176]{1,0:T(8,128)(2,1)S(1)}, u32[]{:S(2)}, u32[]{:S(2)}) collective-permute-start(bf16[128,2176]{1,0:T(8,128)(2,1)S(1)} %pad_maximum_fusion.1), channel_id=1, source_target_pairs={{0,4},{1,5},{2,6},{3,7},{4,0},{5,1},{6,2},{7,3},{8,12},{9,13},{10,... | collective-permute-start | bytes 1671176 | tf_op jit(solution)/shard_map/ppermute | solution.py:244
  50.4 13.4 %collective-permute-start.12 = (bf16[128,2048]{1,0:T(8,128)(2,1)S(1)}, bf16[128,2048]{1,0:T(8,128)(2,1)S(1)}, u32[]{:S(2)}, u32[]{:S(2)}) collective-permute-start(bf16[128,2048]{1,0:T(8,128)(2,1)S(1)} %get-tuple-element.47), channel_id=1, source_target_pairs={{0,2},{1,3},{2,0},{3,1},{4,6},{5,7},{6,4},{7,5},{8,10},{9,11},{10,... | collective-permute-start | bytes 1572872 | tf_op jit(solution)/shard_map/ppermute | solution.py:244
  51.9 11.8 %collective-permute-start.11 = (bf16[128,2048]{1,0:T(8,128)(2,1)S(1)}, bf16[128,2048]{1,0:T(8,128)(2,1)S(1)}, u32[]{:S(2)}, u32[]{:S(2)}) collective-permute-start(bf16[128,2048]{1,0:T(8,128)(2,1)S(1)} %get-tuple-element.45), channel_id=1, source_target_pairs={{0,16},{1,17},{2,18},{3,19},{4,20},{5,21},{6,22},{7,23},{8,24},{9,... | collective-permute-start | bytes 1572872 | tf_op jit(solution)/shard_map/ppermute | solution.py:244
  51.9 11.7 %collective-permute-start.14 = (bf16[128,2048]{1,0:T(8,128)(2,1)S(1)}, bf16[128,2048]{1,0:T(8,128)(2,1)S(1)}, u32[]{:S(2)}, u32[]{:S(2)}) collective-permute-start(bf16[128,2048]{1,0:T(8,128)(2,1)S(1)} %get-tuple-element.54), channel_id=1, source_target_pairs={{0,4},{1,5},{2,6},{3,7},{4,0},{5,1},{6,2},{7,3},{8,12},{9,13},{10,... | collective-permute-start | bytes 1572872 | tf_op jit(solution)/shard_map/ppermute | solution.py:244
  63.8 12.6 %collective-permute-start.15 = (bf16[64,2048]{1,0:T(8,128)(2,1)S(1)}, bf16[64,2048]{1,0:T(8,128)(2,1)S(1)}, u32[]{:S(2)}, u32[]{:S(2)}) collective-permute-start(bf16[64,2048]{1,0:T(8,128)(2,1)S(1)} %get-tuple-element.55), channel_id=1, source_target_pairs={{0,2},{1,3},{2,0},{3,1},{4,6},{5,7},{6,4},{7,5},{8,10},{9,11},{10,... | collective-permute-start | bytes 786440 | tf_op jit(solution)/shard_map/ppermute | solution.py:244
  64.3 7.8 %collective-permute-start.16 = (bf16[64,2048]{1,0:T(8,128)(2,1)S(1)}, bf16[64,2048]{1,0:T(8,128)(2,1)S(1)}, u32[]{:S(2)}, u32[]{:S(2)}) collective-permute-start(bf16[64,2048]{1,0:T(8,128)(2,1)S(1)} %get-tuple-element.57), channel_id=1, source_target_pairs={{0,16},{1,17},{2,18},{3,19},{4,20},{5,21},{6,22},{7,23},{8,24},{9,... | collective-permute-start | bytes 786440 | tf_op jit(solution)/shard_map/ppermute | solution.py:244
  65.8 21.2 %collective-permute-start.19 = (bf16[64,2048]{1,0:T(8,128)(2,1)S(1)}, bf16[64,2048]{1,0:T(8,128)(2,1)S(1)}, u32[]{:S(2)}, u32[]{:S(2)}) collective-permute-start(bf16[64,2048]{1,0:T(8,128)(2,1)S(1)} %get-tuple-element.62), channel_id=1, source_target_pairs={{0,2},{1,3},{2,0},{3,1},{4,6},{5,7},{6,4},{7,5},{8,10},{9,11},{10,... | collective-permute-start | bytes 786440 | tf_op jit(solution)/shard_map/ppermute | solution.py:244
  67.5 20.2 %collective-permute-start.21 = (bf16[64,2048]{1,0:T(8,128)(2,1)S(1)}, bf16[64,2048]{1,0:T(8,128)(2,1)S(1)}, u32[]{:S(2)}, u32[]{:S(2)}) collective-permute-start(bf16[64,2048]{1,0:T(8,128)(2,1)S(1)} %add_convert_fusion.3), channel_id=1, source_target_pairs={{0,8},{1,9},{2,10},{3,11},{4,12},{5,13},{6,14},{7,15},{8,0},{9,1},... | collective-permute-start | bytes 786440 | tf_op jit(solution)/shard_map/ppermute | solution.py:244
  72.2 8.8 %collective-permute-start.17 = (bf16[64,2048]{1,0:T(8,128)(2,1)S(1)}, bf16[64,2048]{1,0:T(8,128)(2,1)S(1)}, u32[]{:S(2)}, u32[]{:S(2)}) collective-permute-start(bf16[64,2048]{1,0:T(8,128)(2,1)S(1)} %get-tuple-element.59), channel_id=1, source_target_pairs={{0,16},{1,17},{2,18},{3,19},{4,20},{5,21},{6,22},{7,23},{8,24},{9,... | collective-permute-start | bytes 786440 | tf_op jit(solution)/shard_map/ppermute | solution.py:244
  73.6 8.5 %collective-permute-start.22 = (bf16[64,2048]{1,0:T(8,128)(2,1)S(1)}, bf16[64,2048]{1,0:T(8,128)(2,1)S(1)}, u32[]{:S(2)}, u32[]{:S(2)}) collective-permute-start(bf16[64,2048]{1,0:T(8,128)(2,1)S(1)} %add_convert_fusion.2), channel_id=1, source_target_pairs={{0,2},{1,3},{2,0},{3,1},{4,6},{5,7},{6,4},{7,5},{8,10},{9,11},{10,... | collective-permute-start | bytes 786440 | tf_op jit(solution)/shard_map/ppermute | solution.py:244
  81.0 6.4 %collective-permute-start.18 = (bf16[64,2048]{1,0:T(8,128)(2,1)S(1)}, bf16[64,2048]{1,0:T(8,128)(2,1)S(1)}, u32[]{:S(2)}, u32[]{:S(2)}) collective-permute-start(bf16[64,2048]{1,0:T(8,128)(2,1)S(1)} %add_convert_fusion.6), channel_id=1, source_target_pairs={{0,16},{1,17},{2,18},{3,19},{4,20},{5,21},{6,22},{7,23},{8,24},{9,... | collective-permute-start | bytes 786440 | tf_op jit(solution)/shard_map/ppermute | solution.py:244
  82.2 10.3 %collective-permute-start.23 = (bf16[64,2048]{1,0:T(8,128)(2,1)S(1)}, bf16[64,2048]{1,0:T(8,128)(2,1)S(1)}, u32[]{:S(2)}, u32[]{:S(2)}) collective-permute-start(bf16[64,2048]{1,0:T(8,128)(2,1)S(1)} %add_convert_fusion.1), channel_id=1, source_target_pairs={{0,12},{1,13},{2,14},{3,15},{4,8},{5,9},{6,10},{7,11},{8,4},{9,5},... | collective-permute-start | bytes 786440 | tf_op jit(solution)/shard_map/ppermute | solution.py:244
  87.4 7.8 %collective-permute-start.20 = (bf16[64,2048]{1,0:T(8,128)(2,1)S(1)}, bf16[64,2048]{1,0:T(8,128)(2,1)S(1)}, u32[]{:S(2)}, u32[]{:S(2)}) collective-permute-start(bf16[64,2048]{1,0:T(8,128)(2,1)S(1)} %add_convert_fusion.4), channel_id=1, source_target_pairs={{0,4},{1,5},{2,6},{3,7},{4,0},{5,1},{6,2},{7,3},{8,12},{9,13},{10,... | collective-permute-start | bytes 786440 | tf_op jit(solution)/shard_map/ppermute | solution.py:244

commit v3 on v2

--- a/solution.py
+++ b/solution.py
@@ -159,20 +159,49 @@
     return lax.dot_general(a, b, (((1,), (1,)), ((), ())), preferred_element_type=jnp.float32)
 
 
-def hidden_units(me, which, rows_ref, weight, width, half):
-    columns = rows_ref[:, width:].astype(jnp.float32)
+def hidden_units(me, which, rows_ref, weight, half, start=0):
+    width = rows_ref.shape[1] - LANES
+    columns = rows_ref[start:, width:].astype(jnp.float32)
     rank = lax.rem(lax.broadcasted_iota(jnp.int32, columns.shape, 1), LANES // 2)
     gates = jnp.sum(
         jnp.where(rank == me[which], columns, jnp.float32(0.0)), axis=1, keepdims=True
     )
-    gate_act = jnp.dot(rows_ref[:, :width], weight[:, :half], preferred_element_type=jnp.float32)
-    up_act = jnp.dot(
-        rows_ref[:, :width], weight[:, half : 2 * half], preferred_element_type=jnp.float32
-    )
+    tokens = rows_ref[start:, :width]
+    gate_act = jnp.dot(tokens, weight[:, :half], preferred_element_type=jnp.float32)
+    up_act = jnp.dot(tokens, weight[:, half : 2 * half], preferred_element_type=jnp.float32)
     return (gate_act / (1.0 + jnp.exp(-gate_act)) * up_act * gates).astype(jnp.bfloat16)
 
 
-def expert_kernel(me_ref, *refs, blocks, fetch):
+def hidden_kernel(me_ref, *refs):
+    *messages, weight, out_ref, rows_ref = refs
+    rows = messages[0].shape[0]
+    for i, message in enumerate(messages):
+        rows_ref[pl.ds(i * rows, rows), :] = message[...]
+    out_ref[...] = hidden_units(me_ref, 0, rows_ref, weight, out_ref.shape[1])
+
+
+def own_hidden(me, messages, weight):
+    rows, columns = messages[0].shape
+    total = len(messages) * rows
+    width, half = columns - LANES, weight.shape[1] // 3
+    vmem = pl.BlockSpec(memory_space=pltpu.VMEM)
+    return pl.pallas_call(
+        hidden_kernel,
+        in_specs=[pl.BlockSpec(memory_space=pltpu.SMEM)] + [vmem] * (len(messages) + 1),
+        out_specs=vmem,
+        out_shape=pltpu.VMEM((total, half), jnp.bfloat16),
+        scratch_shapes=[pltpu.VMEM((total, columns), jnp.bfloat16)],
+        cost_estimate=pl.CostEstimate(
+            flops=4 * total * width * half,
+            bytes_accessed=4 * width * half + 2 * total * width,
+            transcendentals=total * half,
+        ),
+        compiler_params=pltpu.CompilerParams(vmem_limit_bytes=20 * 2**20),
+        name="own_hidden",
+    )(me, *messages, weight)
+
+
+def expert_kernel(me_ref, *refs, blocks, places, begun):
     refs = list(refs)
 
     def take(count):
@@ -182,9 +211,8 @@
 
     messages = take(blocks)
     mine, other = take(2)
-    kept = None
-    if fetch:
-        *outs, kept, rows_ref, sem = refs
+    if begun:
+        before, *outs, kept, rows_ref, total_ref, sem = refs
         copy = pltpu.make_async_copy(other, kept, sem)
         copy.start()
         other = kept
@@ -196,36 +224,55 @@
     for message in messages:
         rows_ref[pl.ds(row, message.shape[0]), :] = message[...]
         row += message.shape[0]
-    first = hidden_units(me_ref, 0, rows_ref, mine, width, half)
-    if fetch:
+    if begun:
+        first = hidden_units(me_ref, 0, rows_ref, mine, half, before.shape[0])
+        first = jnp.concatenate([before[...], first], axis=0)
+        for j in range(width // half):
+            at = pl.ds(j * half, half)
+            total_ref[:, at] = contract_last(first, mine[at, 2 * half :])
         copy.wait()
-    second = hidden_units(me_ref, 1, rows_ref, other, width, half)
+    else:
+        first = hidden_units(me_ref, 0, rows_ref, mine, half)
+    second = hidden_units(me_ref, 1, rows_ref, other, half)
     for j in range(width // half):
         at = pl.ds(j * half, half)
-        answer = contract_last(first, mine[at, 2 * half :])
-        answer += contract_last(second, other[at, 2 * half :])
+        answer = contract_last(second, other[at, 2 * half :])
+        if begun:
+            answer += total_ref[:, at]
+        else:
+            answer += contract_last(first, mine[at, 2 * half :])
         row = 0
-        for out in outs:
-            out[:, at] = answer[row : row + out.shape[0]].astype(out.dtype)
-            row += out.shape[0]
-
-
-def run_experts(me, messages, mine, other, rows_out, fetch=False):
+        for out, place, count in places:
+            part = answer[row : row + count].astype(outs[out].dtype)
+            outs[out][pl.ds(place, count), at] = part
+            row += count
+
+
+def run_experts(me, messages, mine, other, places, before=None):
     columns = messages[0].shape[1]
     width, half = columns - LANES, mine.shape[1] // 3
     total = sum(message.shape[0] for message in messages)
+    begun = before is not None
     vmem = pl.BlockSpec(memory_space=pltpu.VMEM)
+    rows_out = [0] * (1 + max(out for out, _, _ in places))
+    for out, _, count in places:
+        rows_out[out] += count
     out_shape = [jax.ShapeDtypeStruct((n, width), jnp.bfloat16) for n in rows_out]
     scratch_shapes = [pltpu.VMEM((total, columns), jnp.bfloat16)]
-    if fetch:
+    if begun:
         out_shape.append(pltpu.VMEM(other.shape, jnp.bfloat16))
+        scratch_shapes.append(pltpu.VMEM((total, width), jnp.float32))
         scratch_shapes.append(pltpu.SemaphoreType.DMA)
+    others = [before] if begun else []
     return list(
         pl.pallas_call(
-            functools.partial(expert_kernel, blocks=len(messages), fetch=fetch),
+            functools.partial(
+                expert_kernel, blocks=len(messages), places=tuple(places), begun=begun
+            ),
             in_specs=[pl.BlockSpec(memory_space=pltpu.SMEM)]
             + [vmem] * (len(messages) + 1)
-            + [pl.BlockSpec(memory_space=pl.ANY) if fetch else vmem],
+            + [pl.BlockSpec(memory_space=pl.ANY) if begun else vmem]
+            + [vmem] * len(others),
             out_specs=[vmem] * len(out_shape),
             out_shape=out_shape,
             scratch_shapes=scratch_shapes,
@@ -234,9 +281,9 @@
                 bytes_accessed=12 * width * half + 4 * total * width,
                 transcendentals=2 * total * half,
             ),
-            compiler_params=pltpu.CompilerParams(vmem_limit_bytes=24 * 2**20),
+            compiler_params=pltpu.CompilerParams(vmem_limit_bytes=20 * 2**20),
             name="run_experts",
-        )(me, *messages, mine, other)
+        )(me, *messages, mine, other, *others)
     )
 
 
@@ -287,25 +334,29 @@
     s13 = send(jnp.concatenate([s0, s2]), z1)
     y2 = send(after(s2, y0), y)
     x2 = send(after(s2, x0), x)
+    begun = own_hidden(pair, (x0, y0, s0, s2), mine)
     d0 = send(after(x0, s2), y)
-    d2 = send(after(y2, x2), x)
+    d2 = send(after(y2, x2, begun), x)
     x13 = send(after(s13, x2), x)
     y13 = send(after(s13, y2), y)
     d13 = send(jnp.concatenate([d0, d2]), z1)
     rows = s0.shape[0]
     x02, y02, d02, s0, s2, swapped = run_experts(
         pair,
-        (x0, x2, y0, y2, d0, d2, s0, s2),
+        (x0, y0, s0, s2, x2, y2, d0, d2),
         mine,
         swapped,
-        (2 * rows, 2 * rows, 2 * rows, rows, rows),
-        fetch=True,
+        [
+            (out, place * rows, rows)
+            for out, place in ((0, 0), (1, 0), (3, 0), (4, 0), (0, 1), (1, 1), (2, 0), (2, 1))
+        ],
+        before=begun,
     )
     bx02 = send(after(x02, x13, y13), x)
-    by02 = send(after(y02, x13, y13), y)
-    bd02 = send(after(d02, d13), z1)
+    by02 = send(after(y02, y13), y)
+    bd02 = send(d02, z1)
     d1, d3, x1, x3, y1, y3, s1, s3 = run_experts(
-        pair, (after(d13, d02), x13, y13, s13), mine, swapped, (rows,) * 8
+        pair, (after(d13, d02), x13, y13, s13), mine, swapped, [(i, 0, rows) for i in range(8)]
     )
     bd3 = send(after(add(d3, bd02[rows:]), bx02, by02), x)
     bd1 = send(after(add(d1, bd02[:rows]), bx02, by02), y)

time: 96.4 us -> 95.4 us (0.990)
  Pallas kernels: 27.5 us -> 30.2 us
  starting transfers between devices: 36 us -> 33.4 us
  waiting for transfers between devices: 30.9 us -> 29.8 us
    pallas_call x2 -> x3, Pallas kernels: 19.9 us -> 22.7 us  [the longest x2 18.6 us: run_experts(): pl.pallas_call(functools.partial(expert_kernel, blocks=len(messages), pla...]
    ppermute x24, starting transfers between devices: 36 us -> 33.4 us  [hop(): return lax.ppermute(value, AXES, [(i, i ^ bit) for i in range(devices)])]
    ppermute x24, waiting for transfers between devices: 30.9 us -> 29.8 us  [hop(): return lax.ppermute(value, AXES, [(i, i ^ bit) for i in range(devices)])]
  transfers between devices with their start and end apart: 24 -> 24, of which waited for: 11 -> 15; matrix products, arithmetic and copies ran while one was open for 1% -> 1% of each run, Pallas kernels for 27% -> 30%
where the time goes in v3:
time: 95.4 us; the launch traced here: 95.2 us
  starting transfers between devices  33.4 us (35%)
  Pallas kernels  30.2 us (32%)
  waiting for transfers between devices  29.8 us (31%)
  other arithmetic  1.64 us (2%)
    ppermute x24, starting transfers between devices, hop(): return lax.ppermute(value, AXES, [(i, i ^ bit) for i in range(devices)])  33.4 us
    ppermute x24, waiting for transfers between devices, hop(): return lax.ppermute(value, AXES, [(i, i ^ bit) for i in range(devices)])  29.8 us
    pallas_call x2, Pallas kernels, run_experts(): pl.pallas_call(functools.partial(expert_kernel, blocks=len(messages), pla...  18.6 us
    pallas_call x1, Pallas kernels, scale_weights(): pl.pallas_call(functools.partial(scale_kernel, pieces=pieces), in_specs=[...  5.73 us
    pallas_call x1, Pallas kernels, own_hidden(): pl.pallas_call(hidden_kernel, in_specs=[pl.BlockSpec(memory_space=pltpu.S...  4.05 us
  transfers between devices with their start and end apart: 24, of which 15 were waited for; matrix products, arithmetic and copies ran while one was open for 1% of the time, Pallas kernels for 30%

profile of v3, /device:TPU:0, one launch (start us, length us, event | category | flops | bytes accessed | tf_op | source)
XLA Modules:
  0.0 95.2 jit_solution(12944809354300958093)
XLA Ops:
  0.0 1.8 %pack.1.refs_2_ = bf16[64,2176]{1,0:T(8,128)(2,1)} custom-call(f32[8,64]{1,0:T(8,128)} %bitcast.14, s32[8,64]{1,0:T(8,128)} %bitcast.15, s32[8,64]{1,0:T(8,128)} %bitcast.16, bf16[64,2048]{1,0:T(8,128)(2,1)} %tokens_ref.1), custom_call_target="tpu_custom_call" | custom-call | flops 131072 | bytes 524288 | tf_op jit(solution)/shard_map/pack/pallas_call | solution.py:89
  1.8 4.0 %collective-permute-start.2 = (bf16[64,2176]{1,0:T(8,128)(2,1)}, bf16[64,2176]{1,0:T(8,128)(2,1)S(1)}, u32[]{:S(2)}, u32[]{:S(2)}) collective-permute-start(bf16[64,2176]{1,0:T(8,128)(2,1)} %pack.1.refs_2_), channel_id=1, source_target_pairs={{0,8},{1,9},{2,10},{3,11},{4,12},{5,13},{6,14},{7,15},{8,0},{9,1},... | collective-permute-start | bytes 835592 | tf_op jit(solution)/shard_map/ppermute | solution.py:291
  5.9 1.5 %collective-permute-start = (bf16[64,2176]{1,0:T(8,128)(2,1)}, bf16[64,2176]{1,0:T(8,128)(2,1)S(1)}, u32[]{:S(2)}, u32[]{:S(2)}) collective-permute-start(bf16[64,2176]{1,0:T(8,128)(2,1)} %pack.1.refs_2_), channel_id=1, source_target_pairs={{0,16},{1,17},{2,18},{3,19},{4,20},{5,21},{6,22},{7,23},{8,24},{9,... | collective-permute-start | bytes 835592 | tf_op jit(solution)/shard_map/ppermute | solution.py:291
  7.4 1.5 %collective-permute-start.1 = (bf16[64,2176]{1,0:T(8,128)(2,1)}, bf16[64,2176]{1,0:T(8,128)(2,1)S(1)}, u32[]{:S(2)}, u32[]{:S(2)}) collective-permute-start(bf16[64,2176]{1,0:T(8,128)(2,1)} %pack.1.refs_2_), channel_id=1, source_target_pairs={{0,2},{1,3},{2,0},{3,1},{4,6},{5,7},{6,4},{7,5},{8,10},{9,11},{10,... | collective-permute-start | bytes 835592 | tf_op jit(solution)/shard_map/ppermute | solution.py:291
  8.9 0.0 copy-start
  8.9 5.7 %scale_weights.1.refs_4_.refs_8_ = bf16[2048,1536]{1,0:T(8,128)(2,1)} custom-call(f32[4,16]{1,0:T(4,128)} %bitcast.17, f32[4,16]{1,0:T(4,128)} %bitcast.18, f32[4,16]{1,0:T(4,128)} %bitcast.19, bf16[1,2048,512]{2,1,0:T(8,128)(2,1)} %refs_3_.1, bf16[1,2048,512]{2,1,0:T(8,128)(2,1)} %refs_4_.1, bf16[1,2048,512]{2,1,0:T(8,128)(2,1)} %refs_5_.1), custom_call_target="tpu_custom_call" | custom-call | flops 3145728 | bytes 12582912 | tf_op jit(solution)/shard_map/scale_weights/pallas_call | solution.py:142
  14.6 4.1 %collective-permute-done.2.refs_3_ = bf16[64,2176]{1,0:T(8,128)(2,1)S(1)} collective-permute-done((bf16[64,2176]{1,0:T(8,128)(2,1)}, bf16[64,2176]{1,0:T(8,128)(2,1)S(1)}, u32[]{:S(2)}, u32[]{:S(2)}) %collective-permute-start.2) | collective-permute-done | bytes 278560 | tf_op jit(solution)/shard_map/ppermute | solution.py:291
  18.7 0.0 collective-permute-done.refs_0_
  18.7 0.0 collective-permute-done.1.refs_1_
  18.7 0.0 collective-permute-start.7
  18.7 0.0 copy-done
  18.8 0.9 collective-permute-start.8
  19.7 1.5 %collective-permute-start.3 = (bf16[64,2176]{1,0:T(8,128)(2,1)S(1)}, bf16[64,2176]{1,0:T(8,128)(2,1)S(1)}, u32[]{:S(2)}, u32[]{:S(2)}) collective-permute-start(bf16[64,2176]{1,0:T(8,128)(2,1)S(1)} %collective-permute-done.2.refs_3_), channel_id=1, source_target_pairs={{0,16},{1,17},{2,18},{3,19},{4,20},{5,21},{6,22},{7,23},{8,24},{9,... | collective-permute-start | bytes 835592 | tf_op jit(solution)/shard_map/ppermute | solution.py:291
  21.2 1.5 %collective-permute-start.4 = (bf16[64,2176]{1,0:T(8,128)(2,1)S(1)}, bf16[64,2176]{1,0:T(8,128)(2,1)S(1)}, u32[]{:S(2)}, u32[]{:S(2)}) collective-permute-start(bf16[64,2176]{1,0:T(8,128)(2,1)S(1)} %collective-permute-done.2.refs_3_), channel_id=1, source_target_pairs={{0,2},{1,3},{2,0},{3,1},{4,6},{5,7},{6,4},{7,5},{8,10},{9,11},{10,... | collective-permute-start | bytes 835592 | tf_op jit(solution)/shard_map/ppermute | solution.py:291
  22.7 0.1 pad_add_fusion.me_ref
  22.7 0.5 collective-permute-start.5
  23.3 4.1 %own_hidden.1.refs_10_ = bf16[256,512]{1,0:T(8,128)(2,1)S(1)} custom-call(s32[2]{0:T(128)S(1)} %pad_add_fusion.me_ref, bf16[64,2176]{1,0:T(8,128)(2,1)S(1)} %collective-permute-done.refs_0_, bf16[64,2176]{1,0:T(8,128)(2,1)S(1)} %collective-permute-done.1.refs_1_, bf16[64,2176]{1,0:T(8,128)(2,1)S(1)} %copy-done, ...), custom_call_target="tpu_custom_call" | custom-call | flops 1073741824 | bytes 5242880 | tf_op jit(solution)/shard_map/own_hidden/pallas_call | solution.py:188
  27.3 1.1 %collective-permute-done.3.refs_4_ = bf16[64,2176]{1,0:T(8,128)(2,1)S(1)} collective-permute-done((bf16[64,2176]{1,0:T(8,128)(2,1)S(1)}, bf16[64,2176]{1,0:T(8,128)(2,1)S(1)}, u32[]{:S(2)}, u32[]{:S(2)}) %collective-permute-start.3) | collective-permute-done | bytes 278560 | tf_op jit(solution)/shard_map/ppermute | solution.py:291
  28.4 2.3 %collective-permute-done.4.refs_5_ = bf16[64,2176]{1,0:T(8,128)(2,1)S(1)} collective-permute-done((bf16[64,2176]{1,0:T(8,128)(2,1)S(1)}, bf16[64,2176]{1,0:T(8,128)(2,1)S(1)}, u32[]{:S(2)}, u32[]{:S(2)}) %collective-permute-start.4) | collective-permute-done | bytes 278560 | tf_op jit(solution)/shard_map/ppermute | solution.py:291
  30.7 0.5 collective-permute-start.6
  31.2 2.6 %collective-permute-done.8.refs_3_ = bf16[128,2176]{1,0:T(8,128)(2,1)S(1)} collective-permute-done((bf16[128,2176]{1,0:T(8,128)(2,1)S(1)}, bf16[128,2176]{1,0:T(8,128)(2,1)S(1)}, u32[]{:S(2)}, u32[]{:S(2)}) %collective-permute-start.8) | collective-permute-done | bytes 557088 | tf_op jit(solution)/shard_map/ppermute | solution.py:291
  33.9 1.5 %collective-permute-start.9 = (bf16[128,2176]{1,0:T(8,128)(2,1)S(1)}, bf16[128,2176]{1,0:T(8,128)(2,1)S(1)}, u32[]{:S(2)}, u32[]{:S(2)}) collective-permute-start(bf16[128,2176]{1,0:T(8,128)(2,1)S(1)} %collective-permute-done.8.refs_3_), channel_id=1, source_target_pairs={{0,16},{1,17},{2,18},{3,19},{4,20},{5,21},{6,22},{7,23},{8,24},{9,... | collective-permute-start | bytes 1671176 | tf_op jit(solution)/shard_map/ppermute | solution.py:291
  35.4 1.5 %collective-permute-start.10 = (bf16[128,2176]{1,0:T(8,128)(2,1)S(1)}, bf16[128,2176]{1,0:T(8,128)(2,1)S(1)}, u32[]{:S(2)}, u32[]{:S(2)}) collective-permute-start(bf16[128,2176]{1,0:T(8,128)(2,1)S(1)} %collective-permute-done.8.refs_3_), channel_id=1, source_target_pairs={{0,2},{1,3},{2,0},{3,1},{4,6},{5,7},{6,4},{7,5},{8,10},{9,11},{10,... | collective-permute-start | bytes 1671176 | tf_op jit(solution)/shard_map/ppermute | solution.py:291
  36.9 0.0 collective-permute-done.5.refs_6_
  36.9 1.4 %collective-permute-done.6.refs_7_ = bf16[64,2176]{1,0:T(8,128)(2,1)S(1)} collective-permute-done((bf16[64,2176]{1,0:T(8,128)(2,1)S(1)}, bf16[64,2176]{1,0:T(8,128)(2,1)S(1)}, u32[]{:S(2)}, u32[]{:S(2)}) %collective-permute-start.6) | collective-permute-done | bytes 278560 | tf_op jit(solution)/shard_map/ppermute | solution.py:291
  38.4 1.7 %collective-permute-start.13 = (bf16[128,2176]{1,0:T(8,128)(2,1)S(1)}, bf16[128,2176]{1,0:T(8,128)(2,1)S(1)}, u32[]{:S(2)}, u32[]{:S(2)}) collective-permute-start(bf16[128,2176]{1,0:T(8,128)(2,1)S(1)} %pad_maximum_fusion.1), channel_id=1, source_target_pairs={{0,4},{1,5},{2,6},{3,7},{4,0},{5,1},{6,2},{7,3},{8,12},{9,13},{10,... | collective-permute-start | bytes 1671176 | tf_op jit(solution)/shard_map/ppermute | solution.py:291
  40.1 0.0 collective-permute-done.7.refs_9_
  40.1 9.0 %run_experts.2 = (bf16[128,2048]{1,0:T(8,128)(2,1)S(1)}, bf16[128,2048]{1,0:T(8,128)(2,1)S(1)}, bf16[128,2048]{1,0:T(8,128)(2,1)S(1)}, bf16[64,2048]{1,0:T(8,128...) custom-call(s32[2]{0:T(128)S(1)} %pad_add_fusion.me_ref, ...), custom_call_target="tpu_custom_call" | custom-call | flops 6442450944 | bytes 16777216 | tf_op jit(solution)/shard_map/run_experts/pallas_call | solution.py:268
  49.1 0.1 collective-permute-done.9.refs_1_
  49.2 0.1 collective-permute-done.10.refs_2_
  49.4 0.5 collective-permute-start.11
  49.8 1.2 %collective-permute-start.14 = (bf16[128,2048]{1,0:T(8,128)(2,1)S(1)}, bf16[128,2048]{1,0:T(8,128)(2,1)S(1)}, u32[]{:S(2)}, u32[]{:S(2)}) collective-permute-start(bf16[128,2048]{1,0:T(8,128)(2,1)S(1)} %get-tuple-element.47), channel_id=1, source_target_pairs={{0,4},{1,5},{2,6},{3,7},{4,0},{5,1},{6,2},{7,3},{8,12},{9,13},{10,... | collective-permute-start | bytes 1572872 | tf_op jit(solution)/shard_map/ppermute | solution.py:291
  51.1 0.0 collective-permute-done.13.refs_0_
  51.1 1.5 %collective-permute-start.12 = (bf16[128,2048]{1,0:T(8,128)(2,1)S(1)}, bf16[128,2048]{1,0:T(8,128)(2,1)S(1)}, u32[]{:S(2)}, u32[]{:S(2)}) collective-permute-start(bf16[128,2048]{1,0:T(8,128)(2,1)S(1)} %get-tuple-element.46), channel_id=1, source_target_pairs={{0,2},{1,3},{2,0},{3,1},{4,6},{5,7},{6,4},{7,5},{8,10},{9,11},{10,... | collective-permute-start | bytes 1572872 | tf_op jit(solution)/shard_map/ppermute | solution.py:291
  52.6 9.6 %run_experts.3 = (bf16[64,2048]{1,0:T(8,128)(2,1)S(1)}, bf16[64,2048]{1,0:T(8,128)(2,1)S(1)}, bf16[64,2048]{1,0:T(8,128)(2,1)S(1)}, bf16[64,2048]{1,0:T(8,128)(2...) custom-call(s32[2]{0:T(128)S(1)} %pad_add_fusion.me_ref, ...), custom_call_target="tpu_custom_call" | custom-call | flops 6442450944 | bytes 16777216 | tf_op jit(solution)/shard_map/run_experts/pallas_call | solution.py:268
  62.2 0.2 collective-permute-done.14
  62.4 0.1 add_convert_fusion.7
  62.5 0.0 collective-permute-done.11
  62.5 1.3 %collective-permute-done.12 = bf16[128,2048]{1,0:T(8,128)(2,1)S(1)} collective-permute-done((bf16[128,2048]{1,0:T(8,128)(2,1)S(1)}, bf16[128,2048]{1,0:T(8,128)(2,1)S(1)}, u32[]{:S(2)}, u32[]{:S(2)}) %collective-permute-start.12) | collective-permute-done | bytes 524320 | tf_op jit(solution)/shard_map/ppermute | solution.py:291
  63.8 1.5 %collective-permute-start.15 = (bf16[64,2048]{1,0:T(8,128)(2,1)S(1)}, bf16[64,2048]{1,0:T(8,128)(2,1)S(1)}, u32[]{:S(2)}, u32[]{:S(2)}) collective-permute-start(bf16[64,2048]{1,0:T(8,128)(2,1)S(1)} %get-tuple-element.53), channel_id=1, source_target_pairs={{0,2},{1,3},{2,0},{3,1},{4,6},{5,7},{6,4},{7,5},{8,10},{9,11},{10,... | collective-permute-start | bytes 786440 | tf_op jit(solution)/shard_map/ppermute | solution.py:291
  65.3 0.6 collective-permute-start.16
  65.9 0.5 collective-permute-start.19
  66.5 0.1 add_convert_fusion.3
  66.6 3.4 %collective-permute-start.21 = (bf16[64,2048]{1,0:T(8,128)(2,1)S(1)}, bf16[64,2048]{1,0:T(8,128)(2,1)S(1)}, u32[]{:S(2)}, u32[]{:S(2)}) collective-permute-start(bf16[64,2048]{1,0:T(8,128)(2,1)S(1)} %add_convert_fusion.3), channel_id=1, source_target_pairs={{0,8},{1,9},{2,10},{3,11},{4,12},{5,13},{6,14},{7,15},{8,0},{9,1},... | collective-permute-start | bytes 786440 | tf_op jit(solution)/shard_map/ppermute | solution.py:291
  69.9 2.3 %collective-permute-done.16 = bf16[64,2048]{1,0:T(8,128)(2,1)S(1)} collective-permute-done((bf16[64,2048]{1,0:T(8,128)(2,1)S(1)}, bf16[64,2048]{1,0:T(8,128)(2,1)S(1)}, u32[]{:S(2)}, u32[]{:S(2)}) %collective-permute-start.16) | collective-permute-done | bytes 262176 | tf_op jit(solution)/shard_map/ppermute | solution.py:291
  72.2 0.9 collective-permute-start.17
  73.1 0.1 add_convert_fusion.2
  73.2 0.9 collective-permute-start.22
  74.1 0.0 collective-permute-done.15
  74.1 0.1 add_convert_fusion.6
  74.2 5.7 %collective-permute-done.17 = bf16[64,2048]{1,0:T(8,128)(2,1)S(1)} collective-permute-done((bf16[64,2048]{1,0:T(8,128)(2,1)S(1)}, bf16[64,2048]{1,0:T(8,128)(2,1)S(1)}, u32[]{:S(2)}, u32[]{:S(2)}) %collective-permute-start.17) | collective-permute-done | bytes 262176 | tf_op jit(solution)/shard_map/ppermute | solution.py:291
  79.8 1.2 %collective-permute-start.18 = (bf16[64,2048]{1,0:T(8,128)(2,1)S(1)}, bf16[64,2048]{1,0:T(8,128)(2,1)S(1)}, u32[]{:S(2)}, u32[]{:S(2)}) collective-permute-start(bf16[64,2048]{1,0:T(8,128)(2,1)S(1)} %add_convert_fusion.6), channel_id=1, source_target_pairs={{0,16},{1,17},{2,18},{3,19},{4,20},{5,21},{6,22},{7,23},{8,24},{9,... | collective-permute-start | bytes 786440 | tf_op jit(solution)/shard_map/ppermute | solution.py:291
  81.1 0.2 collective-permute-done.22
  81.3 0.1 add_convert_fusion.1
  81.4 3.3 %collective-permute-start.23 = (bf16[64,2048]{1,0:T(8,128)(2,1)S(1)}, bf16[64,2048]{1,0:T(8,128)(2,1)S(1)}, u32[]{:S(2)}, u32[]{:S(2)}) collective-permute-start(bf16[64,2048]{1,0:T(8,128)(2,1)S(1)} %add_convert_fusion.1), channel_id=1, source_target_pairs={{0,12},{1,13},{2,14},{3,15},{4,8},{5,9},{6,10},{7,11},{8,4},{9,5},... | collective-permute-start | bytes 786440 | tf_op jit(solution)/shard_map/ppermute | solution.py:291
  84.7 0.0 collective-permute-done.19
  84.7 1.5 %collective-permute-done.18 = bf16[64,2048]{1,0:T(8,128)(2,1)S(1)} collective-permute-done((bf16[64,2048]{1,0:T(8,128)(2,1)S(1)}, bf16[64,2048]{1,0:T(8,128)(2,1)S(1)}, u32[]{:S(2)}, u32[]{:S(2)}) %collective-permute-start.18) | collective-permute-done | bytes 262176 | tf_op jit(solution)/shard_map/ppermute | solution.py:291
  86.2 0.1 add_convert_fusion.4
  86.3 1.0 %collective-permute-start.20 = (bf16[64,2048]{1,0:T(8,128)(2,1)S(1)}, bf16[64,2048]{1,0:T(8,128)(2,1)S(1)}, u32[]{:S(2)}, u32[]{:S(2)}) collective-permute-start(bf16[64,2048]{1,0:T(8,128)(2,1)S(1)} %add_convert_fusion.4), channel_id=1, source_target_pairs={{0,4},{1,5},{2,6},{3,7},{4,0},{5,1},{6,2},{7,3},{8,12},{9,13},{10,... | collective-permute-start | bytes 786440 | tf_op jit(solution)/shard_map/ppermute | solution.py:291
  87.3 0.0 collective-permute-done.21
  87.3 4.5 %collective-permute-done.23 = bf16[64,2048]{1,0:T(8,128)(2,1)S(1)} collective-permute-done((bf16[64,2048]{1,0:T(8,128)(2,1)S(1)}, bf16[64,2048]{1,0:T(8,128)(2,1)S(1)}, u32[]{:S(2)}, u32[]{:S(2)}) %collective-permute-start.23) | collective-permute-done | bytes 262176 | tf_op jit(solution)/shard_map/ppermute | solution.py:291
  91.7 2.5 %collective-permute-done.20 = bf16[64,2048]{1,0:T(8,128)(2,1)S(1)} collective-permute-done((bf16[64,2048]{1,0:T(8,128)(2,1)S(1)}, bf16[64,2048]{1,0:T(8,128)(2,1)S(1)}, u32[]{:S(2)}, u32[]{:S(2)}) %collective-permute-start.20) | collective-permute-done | bytes 262176 | tf_op jit(solution)/shard_map/ppermute | solution.py:291
  94.2 0.9 add_convert_fusion
  (2 shorter events, 0.1 us)
Async XLA Ops:
  1.8 16.9 %collective-permute-start.2 = (bf16[64,2176]{1,0:T(8,128)(2,1)}, bf16[64,2176]{1,0:T(8,128)(2,1)S(1)}, u32[]{:S(2)}, u32[]{:S(2)}) collective-permute-start(bf16[64,2176]{1,0:T(8,128)(2,1)} %pack.1.refs_2_), channel_id=1, source_target_pairs={{0,8},{1,9},{2,10},{3,11},{4,12},{5,13},{6,14},{7,15},{8,0},{9,1},... | collective-permute-start | bytes 835592 | tf_op jit(solution)/shard_map/ppermute | solution.py:291
  5.9 12.8 %collective-permute-start = (bf16[64,2176]{1,0:T(8,128)(2,1)}, bf16[64,2176]{1,0:T(8,128)(2,1)S(1)}, u32[]{:S(2)}, u32[]{:S(2)}) collective-permute-start(bf16[64,2176]{1,0:T(8,128)(2,1)} %pack.1.refs_2_), channel_id=1, source_target_pairs={{0,16},{1,17},{2,18},{3,19},{4,20},{5,21},{6,22},{7,23},{8,24},{9,... | collective-permute-start | bytes 835592 | tf_op jit(solution)/shard_map/ppermute | solution.py:291
  7.4 11.3 %collective-permute-start.1 = (bf16[64,2176]{1,0:T(8,128)(2,1)}, bf16[64,2176]{1,0:T(8,128)(2,1)S(1)}, u32[]{:S(2)}, u32[]{:S(2)}) collective-permute-start(bf16[64,2176]{1,0:T(8,128)(2,1)} %pack.1.refs_2_), channel_id=1, source_target_pairs={{0,2},{1,3},{2,0},{3,1},{4,6},{5,7},{6,4},{7,5},{8,10},{9,11},{10,... | collective-permute-start | bytes 835592 | tf_op jit(solution)/shard_map/ppermute | solution.py:291
  8.9 9.8 %copy-start = (bf16[64,2176]{1,0:T(8,128)(2,1)S(1)}, bf16[64,2176]{1,0:T(8,128)(2,1)}, u32[]{:S(2)}) copy-start(bf16[64,2176]{1,0:T(8,128)(2,1)} %pack.1.refs_2_) | copy-start | bytes 835588
  18.7 21.4 %collective-permute-start.7 = (bf16[2048,1536]{1,0:T(8,128)(2,1)}, bf16[2048,1536]{1,0:T(8,128)(2,1)}, u32[]{:S(2)}, u32[]{:S(2)}) collective-permute-start(bf16[2048,1536]{1,0:T(8,128)(2,1)} %scale_weights.1.refs_4_.refs_8_), channel_id=1, source_target_pairs={{0,1},{1,0},{2,3},{3,2},{4,5},{5,4},{6,7},{7,6},{8,9},{9,8},{10,11... | collective-permute-start | bytes 18874376 | tf_op jit(solution)/shard_map/ppermute | solution.py:291
  18.8 15.1 %collective-permute-start.8 = (bf16[128,2176]{1,0:T(8,128)(2,1)S(1)}, bf16[128,2176]{1,0:T(8,128)(2,1)S(1)}, u32[]{:S(2)}, u32[]{:S(2)}) collective-permute-start(bf16[128,2176]{1,0:T(8,128)(2,1)S(1)} %pad_maximum_fusion), channel_id=1, source_target_pairs={{0,4},{1,5},{2,6},{3,7},{4,0},{5,1},{6,2},{7,3},{8,12},{9,13},{10,... | collective-permute-start | bytes 1671176 | tf_op jit(solution)/shard_map/ppermute | solution.py:291
  19.7 8.8 %collective-permute-start.3 = (bf16[64,2176]{1,0:T(8,128)(2,1)S(1)}, bf16[64,2176]{1,0:T(8,128)(2,1)S(1)}, u32[]{:S(2)}, u32[]{:S(2)}) collective-permute-start(bf16[64,2176]{1,0:T(8,128)(2,1)S(1)} %collective-permute-done.2.refs_3_), channel_id=1, source_target_pairs={{0,16},{1,17},{2,18},{3,19},{4,20},{5,21},{6,22},{7,23},{8,24},{9,... | collective-permute-start | bytes 835592 | tf_op jit(solution)/shard_map/ppermute | solution.py:291
  21.2 9.5 %collective-permute-start.4 = (bf16[64,2176]{1,0:T(8,128)(2,1)S(1)}, bf16[64,2176]{1,0:T(8,128)(2,1)S(1)}, u32[]{:S(2)}, u32[]{:S(2)}) collective-permute-start(bf16[64,2176]{1,0:T(8,128)(2,1)S(1)} %collective-permute-done.2.refs_3_), channel_id=1, source_target_pairs={{0,2},{1,3},{2,0},{3,1},{4,6},{5,7},{6,4},{7,5},{8,10},{9,11},{10,... | collective-permute-start | bytes 835592 | tf_op jit(solution)/shard_map/ppermute | solution.py:291
  22.7 14.2 %collective-permute-start.5 = (bf16[64,2176]{1,0:T(8,128)(2,1)S(1)}, bf16[64,2176]{1,0:T(8,128)(2,1)S(1)}, u32[]{:S(2)}, u32[]{:S(2)}) collective-permute-start(bf16[64,2176]{1,0:T(8,128)(2,1)S(1)} %collective-permute-done.refs_0_), channel_id=1, source_target_pairs={{0,2},{1,3},{2,0},{3,1},{4,6},{5,7},{6,4},{7,5},{8,10},{9,11},{10,... | collective-permute-start | bytes 835592 | tf_op jit(solution)/shard_map/ppermute | solution.py:291
  30.7 7.6 %collective-permute-start.6 = (bf16[64,2176]{1,0:T(8,128)(2,1)S(1)}, bf16[64,2176]{1,0:T(8,128)(2,1)S(1)}, u32[]{:S(2)}, u32[]{:S(2)}) collective-permute-start(bf16[64,2176]{1,0:T(8,128)(2,1)S(1)} %collective-permute-done.4.refs_5_), channel_id=1, source_target_pairs={{0,16},{1,17},{2,18},{3,19},{4,20},{5,21},{6,22},{7,23},{8,24},{9,... | collective-permute-start | bytes 835592 | tf_op jit(solution)/shard_map/ppermute | solution.py:291
  33.9 15.4 %collective-permute-start.9 = (bf16[128,2176]{1,0:T(8,128)(2,1)S(1)}, bf16[128,2176]{1,0:T(8,128)(2,1)S(1)}, u32[]{:S(2)}, u32[]{:S(2)}) collective-permute-start(bf16[128,2176]{1,0:T(8,128)(2,1)S(1)} %collective-permute-done.8.refs_3_), channel_id=1, source_target_pairs={{0,16},{1,17},{2,18},{3,19},{4,20},{5,21},{6,22},{7,23},{8,24},{9,... | collective-permute-start | bytes 1671176 | tf_op jit(solution)/shard_map/ppermute | solution.py:291
  35.4 14.0 %collective-permute-start.10 = (bf16[128,2176]{1,0:T(8,128)(2,1)S(1)}, bf16[128,2176]{1,0:T(8,128)(2,1)S(1)}, u32[]{:S(2)}, u32[]{:S(2)}) collective-permute-start(bf16[128,2176]{1,0:T(8,128)(2,1)S(1)} %collective-permute-done.8.refs_3_), channel_id=1, source_target_pairs={{0,2},{1,3},{2,0},{3,1},{4,6},{5,7},{6,4},{7,5},{8,10},{9,11},{10,... | collective-permute-start | bytes 1671176 | tf_op jit(solution)/shard_map/ppermute | solution.py:291
  38.4 12.7 %collective-permute-start.13 = (bf16[128,2176]{1,0:T(8,128)(2,1)S(1)}, bf16[128,2176]{1,0:T(8,128)(2,1)S(1)}, u32[]{:S(2)}, u32[]{:S(2)}) collective-permute-start(bf16[128,2176]{1,0:T(8,128)(2,1)S(1)} %pad_maximum_fusion.1), channel_id=1, source_target_pairs={{0,4},{1,5},{2,6},{3,7},{4,0},{5,1},{6,2},{7,3},{8,12},{9,13},{10,... | collective-permute-start | bytes 1671176 | tf_op jit(solution)/shard_map/ppermute | solution.py:291
  49.4 13.2 %collective-permute-start.11 = (bf16[128,2048]{1,0:T(8,128)(2,1)S(1)}, bf16[128,2048]{1,0:T(8,128)(2,1)S(1)}, u32[]{:S(2)}, u32[]{:S(2)}) collective-permute-start(bf16[128,2048]{1,0:T(8,128)(2,1)S(1)} %get-tuple-element.44), channel_id=1, source_target_pairs={{0,16},{1,17},{2,18},{3,19},{4,20},{5,21},{6,22},{7,23},{8,24},{9,... | collective-permute-start | bytes 1572872 | tf_op jit(solution)/shard_map/ppermute | solution.py:291
  49.8 12.5 %collective-permute-start.14 = (bf16[128,2048]{1,0:T(8,128)(2,1)S(1)}, bf16[128,2048]{1,0:T(8,128)(2,1)S(1)}, u32[]{:S(2)}, u32[]{:S(2)}) collective-permute-start(bf16[128,2048]{1,0:T(8,128)(2,1)S(1)} %get-tuple-element.47), channel_id=1, source_target_pairs={{0,4},{1,5},{2,6},{3,7},{4,0},{5,1},{6,2},{7,3},{8,12},{9,13},{10,... | collective-permute-start | bytes 1572872 | tf_op jit(solution)/shard_map/ppermute | solution.py:291
  51.1 12.7 %collective-permute-start.12 = (bf16[128,2048]{1,0:T(8,128)(2,1)S(1)}, bf16[128,2048]{1,0:T(8,128)(2,1)S(1)}, u32[]{:S(2)}, u32[]{:S(2)}) collective-permute-start(bf16[128,2048]{1,0:T(8,128)(2,1)S(1)} %get-tuple-element.46), channel_id=1, source_target_pairs={{0,2},{1,3},{2,0},{3,1},{4,6},{5,7},{6,4},{7,5},{8,10},{9,11},{10,... | collective-permute-start | bytes 1572872 | tf_op jit(solution)/shard_map/ppermute | solution.py:291
  63.8 10.3 %collective-permute-start.15 = (bf16[64,2048]{1,0:T(8,128)(2,1)S(1)}, bf16[64,2048]{1,0:T(8,128)(2,1)S(1)}, u32[]{:S(2)}, u32[]{:S(2)}) collective-permute-start(bf16[64,2048]{1,0:T(8,128)(2,1)S(1)} %get-tuple-element.53), channel_id=1, source_target_pairs={{0,2},{1,3},{2,0},{3,1},{4,6},{5,7},{6,4},{7,5},{8,10},{9,11},{10,... | collective-permute-start | bytes 786440 | tf_op jit(solution)/shard_map/ppermute | solution.py:291
  65.3 6.9 %collective-permute-start.16 = (bf16[64,2048]{1,0:T(8,128)(2,1)S(1)}, bf16[64,2048]{1,0:T(8,128)(2,1)S(1)}, u32[]{:S(2)}, u32[]{:S(2)}) collective-permute-start(bf16[64,2048]{1,0:T(8,128)(2,1)S(1)} %get-tuple-element.55), channel_id=1, source_target_pairs={{0,16},{1,17},{2,18},{3,19},{4,20},{5,21},{6,22},{7,23},{8,24},{9,... | collective-permute-start | bytes 786440 | tf_op jit(solution)/shard_map/ppermute | solution.py:291
  65.9 18.8 %collective-permute-start.19 = (bf16[64,2048]{1,0:T(8,128)(2,1)S(1)}, bf16[64,2048]{1,0:T(8,128)(2,1)S(1)}, u32[]{:S(2)}, u32[]{:S(2)}) collective-permute-start(bf16[64,2048]{1,0:T(8,128)(2,1)S(1)} %get-tuple-element.60), channel_id=1, source_target_pairs={{0,2},{1,3},{2,0},{3,1},{4,6},{5,7},{6,4},{7,5},{8,10},{9,11},{10,... | collective-permute-start | bytes 786440 | tf_op jit(solution)/shard_map/ppermute | solution.py:291
  66.6 20.7 %collective-permute-start.21 = (bf16[64,2048]{1,0:T(8,128)(2,1)S(1)}, bf16[64,2048]{1,0:T(8,128)(2,1)S(1)}, u32[]{:S(2)}, u32[]{:S(2)}) collective-permute-start(bf16[64,2048]{1,0:T(8,128)(2,1)S(1)} %add_convert_fusion.3), channel_id=1, source_target_pairs={{0,8},{1,9},{2,10},{3,11},{4,12},{5,13},{6,14},{7,15},{8,0},{9,1},... | collective-permute-start | bytes 786440 | tf_op jit(solution)/shard_map/ppermute | solution.py:291
  72.2 7.6 %collective-permute-start.17 = (bf16[64,2048]{1,0:T(8,128)(2,1)S(1)}, bf16[64,2048]{1,0:T(8,128)(2,1)S(1)}, u32[]{:S(2)}, u32[]{:S(2)}) collective-permute-start(bf16[64,2048]{1,0:T(8,128)(2,1)S(1)} %get-tuple-element.57), channel_id=1, source_target_pairs={{0,16},{1,17},{2,18},{3,19},{4,20},{5,21},{6,22},{7,23},{8,24},{9,... | collective-permute-start | bytes 786440 | tf_op jit(solution)/shard_map/ppermute | solution.py:291
  73.2 8.1 %collective-permute-start.22 = (bf16[64,2048]{1,0:T(8,128)(2,1)S(1)}, bf16[64,2048]{1,0:T(8,128)(2,1)S(1)}, u32[]{:S(2)}, u32[]{:S(2)}) collective-permute-start(bf16[64,2048]{1,0:T(8,128)(2,1)S(1)} %add_convert_fusion.2), channel_id=1, source_target_pairs={{0,2},{1,3},{2,0},{3,1},{4,6},{5,7},{6,4},{7,5},{8,10},{9,11},{10,... | collective-permute-start | bytes 786440 | tf_op jit(solution)/shard_map/ppermute | solution.py:291
  79.8 6.4 %collective-permute-start.18 = (bf16[64,2048]{1,0:T(8,128)(2,1)S(1)}, bf16[64,2048]{1,0:T(8,128)(2,1)S(1)}, u32[]{:S(2)}, u32[]{:S(2)}) collective-permute-start(bf16[64,2048]{1,0:T(8,128)(2,1)S(1)} %add_convert_fusion.6), channel_id=1, source_target_pairs={{0,16},{1,17},{2,18},{3,19},{4,20},{5,21},{6,22},{7,23},{8,24},{9,... | collective-permute-start | bytes 786440 | tf_op jit(solution)/shard_map/ppermute | solution.py:291
  81.4 10.4 %collective-permute-start.23 = (bf16[64,2048]{1,0:T(8,128)(2,1)S(1)}, bf16[64,2048]{1,0:T(8,128)(2,1)S(1)}, u32[]{:S(2)}, u32[]{:S(2)}) collective-permute-start(bf16[64,2048]{1,0:T(8,128)(2,1)S(1)} %add_convert_fusion.1), channel_id=1, source_target_pairs={{0,12},{1,13},{2,14},{3,15},{4,8},{5,9},{6,10},{7,11},{8,4},{9,5},... | collective-permute-start | bytes 786440 | tf_op jit(solution)/shard_map/ppermute | solution.py:291
  86.3 7.9 %collective-permute-start.20 = (bf16[64,2048]{1,0:T(8,128)(2,1)S(1)}, bf16[64,2048]{1,0:T(8,128)(2,1)S(1)}, u32[]{:S(2)}, u32[]{:S(2)}) collective-permute-start(bf16[64,2048]{1,0:T(8,128)(2,1)S(1)} %add_convert_fusion.4), channel_id=1, source_target_pairs={{0,4},{1,5},{2,6},{3,7},{4,0},{5,1},{6,2},{7,3},{8,12},{9,13},{10,... | collective-permute-start | bytes 786440 | tf_op jit(solution)/shard_map/ppermute | solution.py:291

commit v4 on v3

--- a/solution.py
+++ b/solution.py
@@ -358,8 +358,8 @@
     d1, d3, x1, x3, y1, y3, s1, s3 = run_experts(
         pair, (after(d13, d02), x13, y13, s13), mine, swapped, [(i, 0, rows) for i in range(8)]
     )
-    bd3 = send(after(add(d3, bd02[rows:]), bx02, by02), x)
-    bd1 = send(after(add(d1, bd02[:rows]), bx02, by02), y)
+    bd3 = send(after(add(d3, bd02[rows:]), bx02), x)
+    bd1 = send(after(add(d1, bd02[:rows]), bx02), y)
     bs2 = send(after(add(s2, bx02[rows:], by02[rows:]), bd02, s3), z2)
     by1 = send(after(y1, bx02, by02, bd02), y)
     bx3 = send(after(x3, bd3), x)

time: 95.4 us -> 95.5 us (level)
  starting transfers between devices: 33.4 us -> 34.9 us
  waiting for transfers between devices: 29.8 us -> 28.3 us
    ppermute x24, starting transfers between devices: 33.4 us -> 34.9 us  [hop(): return lax.ppermute(value, AXES, [(i, i ^ bit) for i in range(devices)])]
    ppermute x24, waiting for transfers between devices: 29.8 us -> 28.3 us  [hop(): return lax.ppermute(value, AXES, [(i, i ^ bit) for i in range(devices)])]
  transfers between devices with their start and end apart: 24 -> 24, of which waited for: 15 -> 14; matrix products, arithmetic and copies ran while one was open for 1% -> 1% of each run, Pallas kernels for 30% -> 30%
where the time goes in v4:
time: 95.5 us; the launch traced here: 95.2 us
  starting transfers between devices  34.9 us (37%)
  Pallas kernels  30.2 us (32%)
  waiting for transfers between devices  28.3 us (30%)
  other arithmetic  1.64 us (2%)
    ppermute x24, starting transfers between devices, hop(): return lax.ppermute(value, AXES, [(i, i ^ bit) for i in range(devices)])  34.9 us
    ppermute x24, waiting for transfers between devices, hop(): return lax.ppermute(value, AXES, [(i, i ^ bit) for i in range(devices)])  28.3 us
    pallas_call x2, Pallas kernels, run_experts(): pl.pallas_call(functools.partial(expert_kernel, blocks=len(messages), pla...  18.6 us
    pallas_call x1, Pallas kernels, scale_weights(): pl.pallas_call(functools.partial(scale_kernel, pieces=pieces), in_specs=[...  5.73 us
    pallas_call x1, Pallas kernels, own_hidden(): pl.pallas_call(hidden_kernel, in_specs=[pl.BlockSpec(memory_space=pltpu.S...  4.05 us
  transfers between devices with their start and end apart: 24, of which 14 were waited for; matrix products, arithmetic and copies ran while one was open for 1% of the time, Pallas kernels for 30%

profile of v4, /device:TPU:0, one launch (start us, length us, event | category | flops | bytes accessed | tf_op | source)
XLA Modules:
  0.0 95.2 jit_solution(9703543933458006328)
XLA Ops:
  0.0 1.8 %pack.1.refs_2_ = bf16[64,2176]{1,0:T(8,128)(2,1)} custom-call(f32[8,64]{1,0:T(8,128)} %bitcast.14, s32[8,64]{1,0:T(8,128)} %bitcast.15, s32[8,64]{1,0:T(8,128)} %bitcast.16, bf16[64,2048]{1,0:T(8,128)(2,1)} %tokens_ref.1), custom_call_target="tpu_custom_call" | custom-call | flops 131072 | bytes 524288 | tf_op jit(solution)/shard_map/pack/pallas_call | solution.py:89
  1.8 4.0 %collective-permute-start.2 = (bf16[64,2176]{1,0:T(8,128)(2,1)}, bf16[64,2176]{1,0:T(8,128)(2,1)S(1)}, u32[]{:S(2)}, u32[]{:S(2)}) collective-permute-start(bf16[64,2176]{1,0:T(8,128)(2,1)} %pack.1.refs_2_), channel_id=1, source_target_pairs={{0,8},{1,9},{2,10},{3,11},{4,12},{5,13},{6,14},{7,15},{8,0},{9,1},... | collective-permute-start | bytes 835592 | tf_op jit(solution)/shard_map/ppermute | solution.py:291
  5.9 1.5 %collective-permute-start = (bf16[64,2176]{1,0:T(8,128)(2,1)}, bf16[64,2176]{1,0:T(8,128)(2,1)S(1)}, u32[]{:S(2)}, u32[]{:S(2)}) collective-permute-start(bf16[64,2176]{1,0:T(8,128)(2,1)} %pack.1.refs_2_), channel_id=1, source_target_pairs={{0,16},{1,17},{2,18},{3,19},{4,20},{5,21},{6,22},{7,23},{8,24},{9,... | collective-permute-start | bytes 835592 | tf_op jit(solution)/shard_map/ppermute | solution.py:291
  7.4 1.5 %collective-permute-start.1 = (bf16[64,2176]{1,0:T(8,128)(2,1)}, bf16[64,2176]{1,0:T(8,128)(2,1)S(1)}, u32[]{:S(2)}, u32[]{:S(2)}) collective-permute-start(bf16[64,2176]{1,0:T(8,128)(2,1)} %pack.1.refs_2_), channel_id=1, source_target_pairs={{0,2},{1,3},{2,0},{3,1},{4,6},{5,7},{6,4},{7,5},{8,10},{9,11},{10,... | collective-permute-start | bytes 835592 | tf_op jit(solution)/shard_map/ppermute | solution.py:291
  8.9 0.0 copy-start
  8.9 5.7 %scale_weights.1.refs_4_.refs_8_ = bf16[2048,1536]{1,0:T(8,128)(2,1)} custom-call(f32[4,16]{1,0:T(4,128)} %bitcast.17, f32[4,16]{1,0:T(4,128)} %bitcast.18, f32[4,16]{1,0:T(4,128)} %bitcast.19, bf16[1,2048,512]{2,1,0:T(8,128)(2,1)} %refs_3_.1, bf16[1,2048,512]{2,1,0:T(8,128)(2,1)} %refs_4_.1, bf16[1,2048,512]{2,1,0:T(8,128)(2,1)} %refs_5_.1), custom_call_target="tpu_custom_call" | custom-call | flops 3145728 | bytes 12582912 | tf_op jit(solution)/shard_map/scale_weights/pallas_call | solution.py:142
  14.6 4.1 %collective-permute-done.2.refs_3_ = bf16[64,2176]{1,0:T(8,128)(2,1)S(1)} collective-permute-done((bf16[64,2176]{1,0:T(8,128)(2,1)}, bf16[64,2176]{1,0:T(8,128)(2,1)S(1)}, u32[]{:S(2)}, u32[]{:S(2)}) %collective-permute-start.2) | collective-permute-done | bytes 278560 | tf_op jit(solution)/shard_map/ppermute | solution.py:291
  18.7 0.0 collective-permute-done.refs_0_
  18.7 0.0 collective-permute-done.1.refs_1_
  18.7 0.0 collective-permute-start.7
  18.7 0.0 copy-done
  18.8 0.9 collective-permute-start.8
  19.7 1.5 %collective-permute-start.3 = (bf16[64,2176]{1,0:T(8,128)(2,1)S(1)}, bf16[64,2176]{1,0:T(8,128)(2,1)S(1)}, u32[]{:S(2)}, u32[]{:S(2)}) collective-permute-start(bf16[64,2176]{1,0:T(8,128)(2,1)S(1)} %collective-permute-done.2.refs_3_), channel_id=1, source_target_pairs={{0,16},{1,17},{2,18},{3,19},{4,20},{5,21},{6,22},{7,23},{8,24},{9,... | collective-permute-start | bytes 835592 | tf_op jit(solution)/shard_map/ppermute | solution.py:291
  21.2 1.5 %collective-permute-start.4 = (bf16[64,2176]{1,0:T(8,128)(2,1)S(1)}, bf16[64,2176]{1,0:T(8,128)(2,1)S(1)}, u32[]{:S(2)}, u32[]{:S(2)}) collective-permute-start(bf16[64,2176]{1,0:T(8,128)(2,1)S(1)} %collective-permute-done.2.refs_3_), channel_id=1, source_target_pairs={{0,2},{1,3},{2,0},{3,1},{4,6},{5,7},{6,4},{7,5},{8,10},{9,11},{10,... | collective-permute-start | bytes 835592 | tf_op jit(solution)/shard_map/ppermute | solution.py:291
  22.7 0.1 pad_add_fusion.me_ref
  22.7 0.5 collective-permute-start.5
  23.3 4.1 %own_hidden.1.refs_10_ = bf16[256,512]{1,0:T(8,128)(2,1)S(1)} custom-call(s32[2]{0:T(128)S(1)} %pad_add_fusion.me_ref, bf16[64,2176]{1,0:T(8,128)(2,1)S(1)} %collective-permute-done.refs_0_, bf16[64,2176]{1,0:T(8,128)(2,1)S(1)} %collective-permute-done.1.refs_1_, bf16[64,2176]{1,0:T(8,128)(2,1)S(1)} %copy-done, ...), custom_call_target="tpu_custom_call" | custom-call | flops 1073741824 | bytes 5242880 | tf_op jit(solution)/shard_map/own_hidden/pallas_call | solution.py:188
  27.3 1.1 %collective-permute-done.3.refs_4_ = bf16[64,2176]{1,0:T(8,128)(2,1)S(1)} collective-permute-done((bf16[64,2176]{1,0:T(8,128)(2,1)S(1)}, bf16[64,2176]{1,0:T(8,128)(2,1)S(1)}, u32[]{:S(2)}, u32[]{:S(2)}) %collective-permute-start.3) | collective-permute-done | bytes 278560 | tf_op jit(solution)/shard_map/ppermute | solution.py:291
  28.4 2.3 %collective-permute-done.4.refs_5_ = bf16[64,2176]{1,0:T(8,128)(2,1)S(1)} collective-permute-done((bf16[64,2176]{1,0:T(8,128)(2,1)S(1)}, bf16[64,2176]{1,0:T(8,128)(2,1)S(1)}, u32[]{:S(2)}, u32[]{:S(2)}) %collective-permute-start.4) | collective-permute-done | bytes 278560 | tf_op jit(solution)/shard_map/ppermute | solution.py:291
  30.7 0.5 collective-permute-start.6
  31.2 2.6 %collective-permute-done.8.refs_3_ = bf16[128,2176]{1,0:T(8,128)(2,1)S(1)} collective-permute-done((bf16[128,2176]{1,0:T(8,128)(2,1)S(1)}, bf16[128,2176]{1,0:T(8,128)(2,1)S(1)}, u32[]{:S(2)}, u32[]{:S(2)}) %collective-permute-start.8) | collective-permute-done | bytes 557088 | tf_op jit(solution)/shard_map/ppermute | solution.py:291
  33.9 1.5 %collective-permute-start.9 = (bf16[128,2176]{1,0:T(8,128)(2,1)S(1)}, bf16[128,2176]{1,0:T(8,128)(2,1)S(1)}, u32[]{:S(2)}, u32[]{:S(2)}) collective-permute-start(bf16[128,2176]{1,0:T(8,128)(2,1)S(1)} %collective-permute-done.8.refs_3_), channel_id=1, source_target_pairs={{0,16},{1,17},{2,18},{3,19},{4,20},{5,21},{6,22},{7,23},{8,24},{9,... | collective-permute-start | bytes 1671176 | tf_op jit(solution)/shard_map/ppermute | solution.py:291
  35.4 1.5 %collective-permute-start.10 = (bf16[128,2176]{1,0:T(8,128)(2,1)S(1)}, bf16[128,2176]{1,0:T(8,128)(2,1)S(1)}, u32[]{:S(2)}, u32[]{:S(2)}) collective-permute-start(bf16[128,2176]{1,0:T(8,128)(2,1)S(1)} %collective-permute-done.8.refs_3_), channel_id=1, source_target_pairs={{0,2},{1,3},{2,0},{3,1},{4,6},{5,7},{6,4},{7,5},{8,10},{9,11},{10,... | collective-permute-start | bytes 1671176 | tf_op jit(solution)/shard_map/ppermute | solution.py:291
  36.9 0.0 collective-permute-done.5.refs_6_
  36.9 1.4 %collective-permute-done.6.refs_7_ = bf16[64,2176]{1,0:T(8,128)(2,1)S(1)} collective-permute-done((bf16[64,2176]{1,0:T(8,128)(2,1)S(1)}, bf16[64,2176]{1,0:T(8,128)(2,1)S(1)}, u32[]{:S(2)}, u32[]{:S(2)}) %collective-permute-start.6) | collective-permute-done | bytes 278560 | tf_op jit(solution)/shard_map/ppermute | solution.py:291
  38.4 1.7 %collective-permute-start.13 = (bf16[128,2176]{1,0:T(8,128)(2,1)S(1)}, bf16[128,2176]{1,0:T(8,128)(2,1)S(1)}, u32[]{:S(2)}, u32[]{:S(2)}) collective-permute-start(bf16[128,2176]{1,0:T(8,128)(2,1)S(1)} %pad_maximum_fusion.1), channel_id=1, source_target_pairs={{0,4},{1,5},{2,6},{3,7},{4,0},{5,1},{6,2},{7,3},{8,12},{9,13},{10,... | collective-permute-start | bytes 1671176 | tf_op jit(solution)/shard_map/ppermute | solution.py:291
  40.1 0.0 collective-permute-done.7.refs_9_
  40.1 9.0 %run_experts.2 = (bf16[128,2048]{1,0:T(8,128)(2,1)S(1)}, bf16[128,2048]{1,0:T(8,128)(2,1)S(1)}, bf16[128,2048]{1,0:T(8,128)(2,1)S(1)}, bf16[64,2048]{1,0:T(8,128...) custom-call(s32[2]{0:T(128)S(1)} %pad_add_fusion.me_ref, ...), custom_call_target="tpu_custom_call" | custom-call | flops 6442450944 | bytes 16777216 | tf_op jit(solution)/shard_map/run_experts/pallas_call | solution.py:268
  49.1 0.1 collective-permute-done.9.refs_1_
  49.2 0.1 collective-permute-done.10.refs_2_
  49.4 0.5 collective-permute-start.11
  49.8 1.2 %collective-permute-start.14 = (bf16[128,2048]{1,0:T(8,128)(2,1)S(1)}, bf16[128,2048]{1,0:T(8,128)(2,1)S(1)}, u32[]{:S(2)}, u32[]{:S(2)}) collective-permute-start(bf16[128,2048]{1,0:T(8,128)(2,1)S(1)} %get-tuple-element.47), channel_id=1, source_target_pairs={{0,4},{1,5},{2,6},{3,7},{4,0},{5,1},{6,2},{7,3},{8,12},{9,13},{10,... | collective-permute-start | bytes 1572872 | tf_op jit(solution)/shard_map/ppermute | solution.py:291
  51.1 0.0 collective-permute-done.13.refs_0_
  51.1 1.5 %collective-permute-start.12 = (bf16[128,2048]{1,0:T(8,128)(2,1)S(1)}, bf16[128,2048]{1,0:T(8,128)(2,1)S(1)}, u32[]{:S(2)}, u32[]{:S(2)}) collective-permute-start(bf16[128,2048]{1,0:T(8,128)(2,1)S(1)} %get-tuple-element.46), channel_id=1, source_target_pairs={{0,2},{1,3},{2,0},{3,1},{4,6},{5,7},{6,4},{7,5},{8,10},{9,11},{10,... | collective-permute-start | bytes 1572872 | tf_op jit(solution)/shard_map/ppermute | solution.py:291
  52.6 9.6 %run_experts.3 = (bf16[64,2048]{1,0:T(8,128)(2,1)S(1)}, bf16[64,2048]{1,0:T(8,128)(2,1)S(1)}, bf16[64,2048]{1,0:T(8,128)(2,1)S(1)}, bf16[64,2048]{1,0:T(8,128)(2...) custom-call(s32[2]{0:T(128)S(1)} %pad_add_fusion.me_ref, ...), custom_call_target="tpu_custom_call" | custom-call | flops 6442450944 | bytes 16777216 | tf_op jit(solution)/shard_map/run_experts/pallas_call | solution.py:268
  62.2 0.2 collective-permute-done.14
  62.4 0.1 add_convert_fusion.7
  62.5 0.0 collective-permute-done.11
  62.5 1.6 %collective-permute-start.15 = (bf16[64,2048]{1,0:T(8,128)(2,1)S(1)}, bf16[64,2048]{1,0:T(8,128)(2,1)S(1)}, u32[]{:S(2)}, u32[]{:S(2)}) collective-permute-start(bf16[64,2048]{1,0:T(8,128)(2,1)S(1)} %get-tuple-element.53), channel_id=1, source_target_pairs={{0,2},{1,3},{2,0},{3,1},{4,6},{5,7},{6,4},{7,5},{8,10},{9,11},{10,... | collective-permute-start | bytes 786440 | tf_op jit(solution)/shard_map/ppermute | solution.py:291
  64.1 1.5 %collective-permute-start.16 = (bf16[64,2048]{1,0:T(8,128)(2,1)S(1)}, bf16[64,2048]{1,0:T(8,128)(2,1)S(1)}, u32[]{:S(2)}, u32[]{:S(2)}) collective-permute-start(bf16[64,2048]{1,0:T(8,128)(2,1)S(1)} %get-tuple-element.55), channel_id=1, source_target_pairs={{0,16},{1,17},{2,18},{3,19},{4,20},{5,21},{6,22},{7,23},{8,24},{9,... | collective-permute-start | bytes 786440 | tf_op jit(solution)/shard_map/ppermute | solution.py:291
  65.6 0.0 collective-permute-done.12
  65.6 0.6 collective-permute-start.19
  66.2 0.1 add_convert_fusion.3
  66.3 2.9 %collective-permute-start.21 = (bf16[64,2048]{1,0:T(8,128)(2,1)S(1)}, bf16[64,2048]{1,0:T(8,128)(2,1)S(1)}, u32[]{:S(2)}, u32[]{:S(2)}) collective-permute-start(bf16[64,2048]{1,0:T(8,128)(2,1)S(1)} %add_convert_fusion.3), channel_id=1, source_target_pairs={{0,8},{1,9},{2,10},{3,11},{4,12},{5,13},{6,14},{7,15},{8,0},{9,1},... | collective-permute-start | bytes 786440 | tf_op jit(solution)/shard_map/ppermute | solution.py:291
  69.2 2.0 %collective-permute-done.16 = bf16[64,2048]{1,0:T(8,128)(2,1)S(1)} collective-permute-done((bf16[64,2048]{1,0:T(8,128)(2,1)S(1)}, bf16[64,2048]{1,0:T(8,128)(2,1)S(1)}, u32[]{:S(2)}, u32[]{:S(2)}) %collective-permute-start.16) | collective-permute-done | bytes 262176 | tf_op jit(solution)/shard_map/ppermute | solution.py:291
  71.2 1.5 %collective-permute-start.17 = (bf16[64,2048]{1,0:T(8,128)(2,1)S(1)}, bf16[64,2048]{1,0:T(8,128)(2,1)S(1)}, u32[]{:S(2)}, u32[]{:S(2)}) collective-permute-start(bf16[64,2048]{1,0:T(8,128)(2,1)S(1)} %get-tuple-element.57), channel_id=1, source_target_pairs={{0,16},{1,17},{2,18},{3,19},{4,20},{5,21},{6,22},{7,23},{8,24},{9,... | collective-permute-start | bytes 786440 | tf_op jit(solution)/shard_map/ppermute | solution.py:291
  72.7 0.1 add_convert_fusion.2
  72.8 0.8 collective-permute-start.22
  73.6 0.0 collective-permute-done.15
  73.6 0.1 add_convert_fusion.6
  73.7 5.5 %collective-permute-done.17 = bf16[64,2048]{1,0:T(8,128)(2,1)S(1)} collective-permute-done((bf16[64,2048]{1,0:T(8,128)(2,1)S(1)}, bf16[64,2048]{1,0:T(8,128)(2,1)S(1)}, u32[]{:S(2)}, u32[]{:S(2)}) %collective-permute-start.17) | collective-permute-done | bytes 262176 | tf_op jit(solution)/shard_map/ppermute | solution.py:291
  79.2 1.4 %collective-permute-start.18 = (bf16[64,2048]{1,0:T(8,128)(2,1)S(1)}, bf16[64,2048]{1,0:T(8,128)(2,1)S(1)}, u32[]{:S(2)}, u32[]{:S(2)}) collective-permute-start(bf16[64,2048]{1,0:T(8,128)(2,1)S(1)} %add_convert_fusion.6), channel_id=1, source_target_pairs={{0,16},{1,17},{2,18},{3,19},{4,20},{5,21},{6,22},{7,23},{8,24},{9,... | collective-permute-start | bytes 786440 | tf_op jit(solution)/shard_map/ppermute | solution.py:291
  80.6 0.1 collective-permute-done.22
  80.7 0.1 add_convert_fusion.1
  80.8 3.9 %collective-permute-start.23 = (bf16[64,2048]{1,0:T(8,128)(2,1)S(1)}, bf16[64,2048]{1,0:T(8,128)(2,1)S(1)}, u32[]{:S(2)}, u32[]{:S(2)}) collective-permute-start(bf16[64,2048]{1,0:T(8,128)(2,1)S(1)} %add_convert_fusion.1), channel_id=1, source_target_pairs={{0,12},{1,13},{2,14},{3,15},{4,8},{5,9},{6,10},{7,11},{8,4},{9,5},... | collective-permute-start | bytes 786440 | tf_op jit(solution)/shard_map/ppermute | solution.py:291
  84.7 0.0 collective-permute-done.19
  84.7 0.8 collective-permute-done.18
  85.5 0.1 add_convert_fusion.4
  85.6 0.7 collective-permute-start.20
  86.3 0.0 collective-permute-done.21
  86.3 5.2 %collective-permute-done.23 = bf16[64,2048]{1,0:T(8,128)(2,1)S(1)} collective-permute-done((bf16[64,2048]{1,0:T(8,128)(2,1)S(1)}, bf16[64,2048]{1,0:T(8,128)(2,1)S(1)}, u32[]{:S(2)}, u32[]{:S(2)}) %collective-permute-start.23) | collective-permute-done | bytes 262176 | tf_op jit(solution)/shard_map/ppermute | solution.py:291
  91.5 2.7 %collective-permute-done.20 = bf16[64,2048]{1,0:T(8,128)(2,1)S(1)} collective-permute-done((bf16[64,2048]{1,0:T(8,128)(2,1)S(1)}, bf16[64,2048]{1,0:T(8,128)(2,1)S(1)}, u32[]{:S(2)}, u32[]{:S(2)}) %collective-permute-start.20) | collective-permute-done | bytes 262176 | tf_op jit(solution)/shard_map/ppermute | solution.py:291
  94.3 0.9 add_convert_fusion
  (2 shorter events, 0.1 us)
Async XLA Ops:
  1.8 16.9 %collective-permute-start.2 = (bf16[64,2176]{1,0:T(8,128)(2,1)}, bf16[64,2176]{1,0:T(8,128)(2,1)S(1)}, u32[]{:S(2)}, u32[]{:S(2)}) collective-permute-start(bf16[64,2176]{1,0:T(8,128)(2,1)} %pack.1.refs_2_), channel_id=1, source_target_pairs={{0,8},{1,9},{2,10},{3,11},{4,12},{5,13},{6,14},{7,15},{8,0},{9,1},... | collective-permute-start | bytes 835592 | tf_op jit(solution)/shard_map/ppermute | solution.py:291
  5.9 12.8 %collective-permute-start = (bf16[64,2176]{1,0:T(8,128)(2,1)}, bf16[64,2176]{1,0:T(8,128)(2,1)S(1)}, u32[]{:S(2)}, u32[]{:S(2)}) collective-permute-start(bf16[64,2176]{1,0:T(8,128)(2,1)} %pack.1.refs_2_), channel_id=1, source_target_pairs={{0,16},{1,17},{2,18},{3,19},{4,20},{5,21},{6,22},{7,23},{8,24},{9,... | collective-permute-start | bytes 835592 | tf_op jit(solution)/shard_map/ppermute | solution.py:291
  7.4 11.3 %collective-permute-start.1 = (bf16[64,2176]{1,0:T(8,128)(2,1)}, bf16[64,2176]{1,0:T(8,128)(2,1)S(1)}, u32[]{:S(2)}, u32[]{:S(2)}) collective-permute-start(bf16[64,2176]{1,0:T(8,128)(2,1)} %pack.1.refs_2_), channel_id=1, source_target_pairs={{0,2},{1,3},{2,0},{3,1},{4,6},{5,7},{6,4},{7,5},{8,10},{9,11},{10,... | collective-permute-start | bytes 835592 | tf_op jit(solution)/shard_map/ppermute | solution.py:291
  8.9 9.8 %copy-start = (bf16[64,2176]{1,0:T(8,128)(2,1)S(1)}, bf16[64,2176]{1,0:T(8,128)(2,1)}, u32[]{:S(2)}) copy-start(bf16[64,2176]{1,0:T(8,128)(2,1)} %pack.1.refs_2_) | copy-start | bytes 835588
  18.7 21.4 %collective-permute-start.7 = (bf16[2048,1536]{1,0:T(8,128)(2,1)}, bf16[2048,1536]{1,0:T(8,128)(2,1)}, u32[]{:S(2)}, u32[]{:S(2)}) collective-permute-start(bf16[2048,1536]{1,0:T(8,128)(2,1)} %scale_weights.1.refs_4_.refs_8_), channel_id=1, source_target_pairs={{0,1},{1,0},{2,3},{3,2},{4,5},{5,4},{6,7},{7,6},{8,9},{9,8},{10,11... | collective-permute-start | bytes 18874376 | tf_op jit(solution)/shard_map/ppermute | solution.py:291
  18.8 15.1 %collective-permute-start.8 = (bf16[128,2176]{1,0:T(8,128)(2,1)S(1)}, bf16[128,2176]{1,0:T(8,128)(2,1)S(1)}, u32[]{:S(2)}, u32[]{:S(2)}) collective-permute-start(bf16[128,2176]{1,0:T(8,128)(2,1)S(1)} %pad_maximum_fusion), channel_id=1, source_target_pairs={{0,4},{1,5},{2,6},{3,7},{4,0},{5,1},{6,2},{7,3},{8,12},{9,13},{10,... | collective-permute-start | bytes 1671176 | tf_op jit(solution)/shard_map/ppermute | solution.py:291
  19.7 8.8 %collective-permute-start.3 = (bf16[64,2176]{1,0:T(8,128)(2,1)S(1)}, bf16[64,2176]{1,0:T(8,128)(2,1)S(1)}, u32[]{:S(2)}, u32[]{:S(2)}) collective-permute-start(bf16[64,2176]{1,0:T(8,128)(2,1)S(1)} %collective-permute-done.2.refs_3_), channel_id=1, source_target_pairs={{0,16},{1,17},{2,18},{3,19},{4,20},{5,21},{6,22},{7,23},{8,24},{9,... | collective-permute-start | bytes 835592 | tf_op jit(solution)/shard_map/ppermute | solution.py:291
  21.2 9.5 %collective-permute-start.4 = (bf16[64,2176]{1,0:T(8,128)(2,1)S(1)}, bf16[64,2176]{1,0:T(8,128)(2,1)S(1)}, u32[]{:S(2)}, u32[]{:S(2)}) collective-permute-start(bf16[64,2176]{1,0:T(8,128)(2,1)S(1)} %collective-permute-done.2.refs_3_), channel_id=1, source_target_pairs={{0,2},{1,3},{2,0},{3,1},{4,6},{5,7},{6,4},{7,5},{8,10},{9,11},{10,... | collective-permute-start | bytes 835592 | tf_op jit(solution)/shard_map/ppermute | solution.py:291
  22.7 14.2 %collective-permute-start.5 = (bf16[64,2176]{1,0:T(8,128)(2,1)S(1)}, bf16[64,2176]{1,0:T(8,128)(2,1)S(1)}, u32[]{:S(2)}, u32[]{:S(2)}) collective-permute-start(bf16[64,2176]{1,0:T(8,128)(2,1)S(1)} %collective-permute-done.refs_0_), channel_id=1, source_target_pairs={{0,2},{1,3},{2,0},{3,1},{4,6},{5,7},{6,4},{7,5},{8,10},{9,11},{10,... | collective-permute-start | bytes 835592 | tf_op jit(solution)/shard_map/ppermute | solution.py:291
  30.7 7.6 %collective-permute-start.6 = (bf16[64,2176]{1,0:T(8,128)(2,1)S(1)}, bf16[64,2176]{1,0:T(8,128)(2,1)S(1)}, u32[]{:S(2)}, u32[]{:S(2)}) collective-permute-start(bf16[64,2176]{1,0:T(8,128)(2,1)S(1)} %collective-permute-done.4.refs_5_), channel_id=1, source_target_pairs={{0,16},{1,17},{2,18},{3,19},{4,20},{5,21},{6,22},{7,23},{8,24},{9,... | collective-permute-start | bytes 835592 | tf_op jit(solution)/shard_map/ppermute | solution.py:291
  33.9 15.4 %collective-permute-start.9 = (bf16[128,2176]{1,0:T(8,128)(2,1)S(1)}, bf16[128,2176]{1,0:T(8,128)(2,1)S(1)}, u32[]{:S(2)}, u32[]{:S(2)}) collective-permute-start(bf16[128,2176]{1,0:T(8,128)(2,1)S(1)} %collective-permute-done.8.refs_3_), channel_id=1, source_target_pairs={{0,16},{1,17},{2,18},{3,19},{4,20},{5,21},{6,22},{7,23},{8,24},{9,... | collective-permute-start | bytes 1671176 | tf_op jit(solution)/shard_map/ppermute | solution.py:291
  35.4 14.0 %collective-permute-start.10 = (bf16[128,2176]{1,0:T(8,128)(2,1)S(1)}, bf16[128,2176]{1,0:T(8,128)(2,1)S(1)}, u32[]{:S(2)}, u32[]{:S(2)}) collective-permute-start(bf16[128,2176]{1,0:T(8,128)(2,1)S(1)} %collective-permute-done.8.refs_3_), channel_id=1, source_target_pairs={{0,2},{1,3},{2,0},{3,1},{4,6},{5,7},{6,4},{7,5},{8,10},{9,11},{10,... | collective-permute-start | bytes 1671176 | tf_op jit(solution)/shard_map/ppermute | solution.py:291
  38.4 12.7 %collective-permute-start.13 = (bf16[128,2176]{1,0:T(8,128)(2,1)S(1)}, bf16[128,2176]{1,0:T(8,128)(2,1)S(1)}, u32[]{:S(2)}, u32[]{:S(2)}) collective-permute-start(bf16[128,2176]{1,0:T(8,128)(2,1)S(1)} %pad_maximum_fusion.1), channel_id=1, source_target_pairs={{0,4},{1,5},{2,6},{3,7},{4,0},{5,1},{6,2},{7,3},{8,12},{9,13},{10,... | collective-permute-start | bytes 1671176 | tf_op jit(solution)/shard_map/ppermute | solution.py:291
  49.4 13.2 %collective-permute-start.11 = (bf16[128,2048]{1,0:T(8,128)(2,1)S(1)}, bf16[128,2048]{1,0:T(8,128)(2,1)S(1)}, u32[]{:S(2)}, u32[]{:S(2)}) collective-permute-start(bf16[128,2048]{1,0:T(8,128)(2,1)S(1)} %get-tuple-element.44), channel_id=1, source_target_pairs={{0,16},{1,17},{2,18},{3,19},{4,20},{5,21},{6,22},{7,23},{8,24},{9,... | collective-permute-start | bytes 1572872 | tf_op jit(solution)/shard_map/ppermute | solution.py:291
  49.8 12.5 %collective-permute-start.14 = (bf16[128,2048]{1,0:T(8,128)(2,1)S(1)}, bf16[128,2048]{1,0:T(8,128)(2,1)S(1)}, u32[]{:S(2)}, u32[]{:S(2)}) collective-permute-start(bf16[128,2048]{1,0:T(8,128)(2,1)S(1)} %get-tuple-element.47), channel_id=1, source_target_pairs={{0,4},{1,5},{2,6},{3,7},{4,0},{5,1},{6,2},{7,3},{8,12},{9,13},{10,... | collective-permute-start | bytes 1572872 | tf_op jit(solution)/shard_map/ppermute | solution.py:291
  51.1 14.6 %collective-permute-start.12 = (bf16[128,2048]{1,0:T(8,128)(2,1)S(1)}, bf16[128,2048]{1,0:T(8,128)(2,1)S(1)}, u32[]{:S(2)}, u32[]{:S(2)}) collective-permute-start(bf16[128,2048]{1,0:T(8,128)(2,1)S(1)} %get-tuple-element.46), channel_id=1, source_target_pairs={{0,2},{1,3},{2,0},{3,1},{4,6},{5,7},{6,4},{7,5},{8,10},{9,11},{10,... | collective-permute-start | bytes 1572872 | tf_op jit(solution)/shard_map/ppermute | solution.py:291
  62.5 11.1 %collective-permute-start.15 = (bf16[64,2048]{1,0:T(8,128)(2,1)S(1)}, bf16[64,2048]{1,0:T(8,128)(2,1)S(1)}, u32[]{:S(2)}, u32[]{:S(2)}) collective-permute-start(bf16[64,2048]{1,0:T(8,128)(2,1)S(1)} %get-tuple-element.53), channel_id=1, source_target_pairs={{0,2},{1,3},{2,0},{3,1},{4,6},{5,7},{6,4},{7,5},{8,10},{9,11},{10,... | collective-permute-start | bytes 786440 | tf_op jit(solution)/shard_map/ppermute | solution.py:291
  64.1 7.1 %collective-permute-start.16 = (bf16[64,2048]{1,0:T(8,128)(2,1)S(1)}, bf16[64,2048]{1,0:T(8,128)(2,1)S(1)}, u32[]{:S(2)}, u32[]{:S(2)}) collective-permute-start(bf16[64,2048]{1,0:T(8,128)(2,1)S(1)} %get-tuple-element.55), channel_id=1, source_target_pairs={{0,16},{1,17},{2,18},{3,19},{4,20},{5,21},{6,22},{7,23},{8,24},{9,... | collective-permute-start | bytes 786440 | tf_op jit(solution)/shard_map/ppermute | solution.py:291
  65.6 19.1 %collective-permute-start.19 = (bf16[64,2048]{1,0:T(8,128)(2,1)S(1)}, bf16[64,2048]{1,0:T(8,128)(2,1)S(1)}, u32[]{:S(2)}, u32[]{:S(2)}) collective-permute-start(bf16[64,2048]{1,0:T(8,128)(2,1)S(1)} %get-tuple-element.60), channel_id=1, source_target_pairs={{0,2},{1,3},{2,0},{3,1},{4,6},{5,7},{6,4},{7,5},{8,10},{9,11},{10,... | collective-permute-start | bytes 786440 | tf_op jit(solution)/shard_map/ppermute | solution.py:291
  66.3 20.0 %collective-permute-start.21 = (bf16[64,2048]{1,0:T(8,128)(2,1)S(1)}, bf16[64,2048]{1,0:T(8,128)(2,1)S(1)}, u32[]{:S(2)}, u32[]{:S(2)}) collective-permute-start(bf16[64,2048]{1,0:T(8,128)(2,1)S(1)} %add_convert_fusion.3), channel_id=1, source_target_pairs={{0,8},{1,9},{2,10},{3,11},{4,12},{5,13},{6,14},{7,15},{8,0},{9,1},... | collective-permute-start | bytes 786440 | tf_op jit(solution)/shard_map/ppermute | solution.py:291
  71.2 7.9 %collective-permute-start.17 = (bf16[64,2048]{1,0:T(8,128)(2,1)S(1)}, bf16[64,2048]{1,0:T(8,128)(2,1)S(1)}, u32[]{:S(2)}, u32[]{:S(2)}) collective-permute-start(bf16[64,2048]{1,0:T(8,128)(2,1)S(1)} %get-tuple-element.57), channel_id=1, source_target_pairs={{0,16},{1,17},{2,18},{3,19},{4,20},{5,21},{6,22},{7,23},{8,24},{9,... | collective-permute-start | bytes 786440 | tf_op jit(solution)/shard_map/ppermute | solution.py:291
  72.8 7.9 %collective-permute-start.22 = (bf16[64,2048]{1,0:T(8,128)(2,1)S(1)}, bf16[64,2048]{1,0:T(8,128)(2,1)S(1)}, u32[]{:S(2)}, u32[]{:S(2)}) collective-permute-start(bf16[64,2048]{1,0:T(8,128)(2,1)S(1)} %add_convert_fusion.2), channel_id=1, source_target_pairs={{0,2},{1,3},{2,0},{3,1},{4,6},{5,7},{6,4},{7,5},{8,10},{9,11},{10,... | collective-permute-start | bytes 786440 | tf_op jit(solution)/shard_map/ppermute | solution.py:291
  79.2 6.4 %collective-permute-start.18 = (bf16[64,2048]{1,0:T(8,128)(2,1)S(1)}, bf16[64,2048]{1,0:T(8,128)(2,1)S(1)}, u32[]{:S(2)}, u32[]{:S(2)}) collective-permute-start(bf16[64,2048]{1,0:T(8,128)(2,1)S(1)} %add_convert_fusion.6), channel_id=1, source_target_pairs={{0,16},{1,17},{2,18},{3,19},{4,20},{5,21},{6,22},{7,23},{8,24},{9,... | collective-permute-start | bytes 786440 | tf_op jit(solution)/shard_map/ppermute | solution.py:291
  80.8 10.8 %collective-permute-start.23 = (bf16[64,2048]{1,0:T(8,128)(2,1)S(1)}, bf16[64,2048]{1,0:T(8,128)(2,1)S(1)}, u32[]{:S(2)}, u32[]{:S(2)}) collective-permute-start(bf16[64,2048]{1,0:T(8,128)(2,1)S(1)} %add_convert_fusion.1), channel_id=1, source_target_pairs={{0,12},{1,13},{2,14},{3,15},{4,8},{5,9},{6,10},{7,11},{8,4},{9,5},... | collective-permute-start | bytes 786440 | tf_op jit(solution)/shard_map/ppermute | solution.py:291
  85.6 8.7 %collective-permute-start.20 = (bf16[64,2048]{1,0:T(8,128)(2,1)S(1)}, bf16[64,2048]{1,0:T(8,128)(2,1)S(1)}, u32[]{:S(2)}, u32[]{:S(2)}) collective-permute-start(bf16[64,2048]{1,0:T(8,128)(2,1)S(1)} %add_convert_fusion.4), channel_id=1, source_target_pairs={{0,4},{1,5},{2,6},{3,7},{4,0},{5,1},{6,2},{7,3},{8,12},{9,13},{10,... | collective-permute-start | bytes 786440 | tf_op jit(solution)/shard_map/ppermute | solution.py:291

commit v5 on v3

--- a/solution.py
+++ b/solution.py
@@ -364,7 +364,7 @@
     by1 = send(after(y1, bx02, by02, bd02), y)
     bx3 = send(after(x3, bd3), x)
     by3 = send(add(y3, bd3), y)
-    bx1 = send(after(add(x1, bd1), bd3, bx3), x)
+    bx1 = send(after(add(x1, bd1), bd3), x)
     bs3 = send(add(s3, bx3, by3), z3)
     bs1 = send(add(s1, bx1, by1), z1)
     return add(s0, bx02[:rows], by02[:rows], bs1, bs2, bs3)

time: 95.4 us -> 92.9 us (0.974)
  waiting for transfers between devices: 29.8 us -> 26.8 us
    ppermute x24, waiting for transfers between devices: 29.8 us -> 26.8 us  [hop(): return lax.ppermute(value, AXES, [(i, i ^ bit) for i in range(devices)])]
  transfers between devices with their start and end apart: 24 -> 24, of which waited for: 15 -> 15; matrix products, arithmetic and copies ran while one was open for 1% -> 1% of each run, Pallas kernels for 30% -> 31%
where the time goes in v5:
time: 92.9 us; the launch traced here: 92.6 us
  starting transfers between devices  33.8 us (36%)
  Pallas kernels  30.2 us (33%)
  waiting for transfers between devices  26.8 us (29%)
  other arithmetic  1.64 us (2%)
    ppermute x24, starting transfers between devices, hop(): return lax.ppermute(value, AXES, [(i, i ^ bit) for i in range(devices)])  33.8 us
    ppermute x24, waiting for transfers between devices, hop(): return lax.ppermute(value, AXES, [(i, i ^ bit) for i in range(devices)])  26.8 us
    pallas_call x2, Pallas kernels, run_experts(): pl.pallas_call(functools.partial(expert_kernel, blocks=len(messages), pla...  18.6 us
    pallas_call x1, Pallas kernels, scale_weights(): pl.pallas_call(functools.partial(scale_kernel, pieces=pieces), in_specs=[...  5.73 us
    pallas_call x1, Pallas kernels, own_hidden(): pl.pallas_call(hidden_kernel, in_specs=[pl.BlockSpec(memory_space=pltpu.S...  4.05 us
  transfers between devices with their start and end apart: 24, of which 15 were waited for; matrix products, arithmetic and copies ran while one was open for 1% of the time, Pallas kernels for 31%

profile of v5, /device:TPU:0, one launch (start us, length us, event | category | flops | bytes accessed | tf_op | source)
XLA Modules:
  0.0 92.6 jit_solution(8186993695278158783)
XLA Ops:
  0.0 1.8 %pack.1.refs_2_ = bf16[64,2176]{1,0:T(8,128)(2,1)} custom-call(f32[8,64]{1,0:T(8,128)} %bitcast.14, s32[8,64]{1,0:T(8,128)} %bitcast.15, s32[8,64]{1,0:T(8,128)} %bitcast.16, bf16[64,2048]{1,0:T(8,128)(2,1)} %tokens_ref.1), custom_call_target="tpu_custom_call" | custom-call | flops 131072 | bytes 524288 | tf_op jit(solution)/shard_map/pack/pallas_call | solution.py:89
  1.8 4.0 %collective-permute-start.2 = (bf16[64,2176]{1,0:T(8,128)(2,1)}, bf16[64,2176]{1,0:T(8,128)(2,1)S(1)}, u32[]{:S(2)}, u32[]{:S(2)}) collective-permute-start(bf16[64,2176]{1,0:T(8,128)(2,1)} %pack.1.refs_2_), channel_id=1, source_target_pairs={{0,8},{1,9},{2,10},{3,11},{4,12},{5,13},{6,14},{7,15},{8,0},{9,1},... | collective-permute-start | bytes 835592 | tf_op jit(solution)/shard_map/ppermute | solution.py:291
  5.9 1.5 %collective-permute-start = (bf16[64,2176]{1,0:T(8,128)(2,1)}, bf16[64,2176]{1,0:T(8,128)(2,1)S(1)}, u32[]{:S(2)}, u32[]{:S(2)}) collective-permute-start(bf16[64,2176]{1,0:T(8,128)(2,1)} %pack.1.refs_2_), channel_id=1, source_target_pairs={{0,16},{1,17},{2,18},{3,19},{4,20},{5,21},{6,22},{7,23},{8,24},{9,... | collective-permute-start | bytes 835592 | tf_op jit(solution)/shard_map/ppermute | solution.py:291
  7.4 1.5 %collective-permute-start.1 = (bf16[64,2176]{1,0:T(8,128)(2,1)}, bf16[64,2176]{1,0:T(8,128)(2,1)S(1)}, u32[]{:S(2)}, u32[]{:S(2)}) collective-permute-start(bf16[64,2176]{1,0:T(8,128)(2,1)} %pack.1.refs_2_), channel_id=1, source_target_pairs={{0,2},{1,3},{2,0},{3,1},{4,6},{5,7},{6,4},{7,5},{8,10},{9,11},{10,... | collective-permute-start | bytes 835592 | tf_op jit(solution)/shard_map/ppermute | solution.py:291
  8.9 0.0 copy-start
  8.9 5.7 %scale_weights.1.refs_4_.refs_8_ = bf16[2048,1536]{1,0:T(8,128)(2,1)} custom-call(f32[4,16]{1,0:T(4,128)} %bitcast.17, f32[4,16]{1,0:T(4,128)} %bitcast.18, f32[4,16]{1,0:T(4,128)} %bitcast.19, bf16[1,2048,512]{2,1,0:T(8,128)(2,1)} %refs_3_.1, bf16[1,2048,512]{2,1,0:T(8,128)(2,1)} %refs_4_.1, bf16[1,2048,512]{2,1,0:T(8,128)(2,1)} %refs_5_.1), custom_call_target="tpu_custom_call" | custom-call | flops 3145728 | bytes 12582912 | tf_op jit(solution)/shard_map/scale_weights/pallas_call | solution.py:142
  14.6 4.1 %collective-permute-done.2.refs_3_ = bf16[64,2176]{1,0:T(8,128)(2,1)S(1)} collective-permute-done((bf16[64,2176]{1,0:T(8,128)(2,1)}, bf16[64,2176]{1,0:T(8,128)(2,1)S(1)}, u32[]{:S(2)}, u32[]{:S(2)}) %collective-permute-start.2) | collective-permute-done | bytes 278560 | tf_op jit(solution)/shard_map/ppermute | solution.py:291
  18.7 0.0 collective-permute-done.refs_0_
  18.7 0.0 collective-permute-done.1.refs_1_
  18.7 0.0 collective-permute-start.7
  18.7 0.0 copy-done
  18.8 0.9 collective-permute-start.8
  19.7 1.5 %collective-permute-start.3 = (bf16[64,2176]{1,0:T(8,128)(2,1)S(1)}, bf16[64,2176]{1,0:T(8,128)(2,1)S(1)}, u32[]{:S(2)}, u32[]{:S(2)}) collective-permute-start(bf16[64,2176]{1,0:T(8,128)(2,1)S(1)} %collective-permute-done.2.refs_3_), channel_id=1, source_target_pairs={{0,16},{1,17},{2,18},{3,19},{4,20},{5,21},{6,22},{7,23},{8,24},{9,... | collective-permute-start | bytes 835592 | tf_op jit(solution)/shard_map/ppermute | solution.py:291
  21.2 1.5 %collective-permute-start.4 = (bf16[64,2176]{1,0:T(8,128)(2,1)S(1)}, bf16[64,2176]{1,0:T(8,128)(2,1)S(1)}, u32[]{:S(2)}, u32[]{:S(2)}) collective-permute-start(bf16[64,2176]{1,0:T(8,128)(2,1)S(1)} %collective-permute-done.2.refs_3_), channel_id=1, source_target_pairs={{0,2},{1,3},{2,0},{3,1},{4,6},{5,7},{6,4},{7,5},{8,10},{9,11},{10,... | collective-permute-start | bytes 835592 | tf_op jit(solution)/shard_map/ppermute | solution.py:291
  22.7 0.1 pad_add_fusion.me_ref
  22.7 0.5 collective-permute-start.5
  23.3 4.1 %own_hidden.1.refs_10_ = bf16[256,512]{1,0:T(8,128)(2,1)S(1)} custom-call(s32[2]{0:T(128)S(1)} %pad_add_fusion.me_ref, bf16[64,2176]{1,0:T(8,128)(2,1)S(1)} %collective-permute-done.refs_0_, bf16[64,2176]{1,0:T(8,128)(2,1)S(1)} %collective-permute-done.1.refs_1_, bf16[64,2176]{1,0:T(8,128)(2,1)S(1)} %copy-done, ...), custom_call_target="tpu_custom_call" | custom-call | flops 1073741824 | bytes 5242880 | tf_op jit(solution)/shard_map/own_hidden/pallas_call | solution.py:188
  27.3 1.1 %collective-permute-done.3.refs_4_ = bf16[64,2176]{1,0:T(8,128)(2,1)S(1)} collective-permute-done((bf16[64,2176]{1,0:T(8,128)(2,1)S(1)}, bf16[64,2176]{1,0:T(8,128)(2,1)S(1)}, u32[]{:S(2)}, u32[]{:S(2)}) %collective-permute-start.3) | collective-permute-done | bytes 278560 | tf_op jit(solution)/shard_map/ppermute | solution.py:291
  28.4 2.3 %collective-permute-done.4.refs_5_ = bf16[64,2176]{1,0:T(8,128)(2,1)S(1)} collective-permute-done((bf16[64,2176]{1,0:T(8,128)(2,1)S(1)}, bf16[64,2176]{1,0:T(8,128)(2,1)S(1)}, u32[]{:S(2)}, u32[]{:S(2)}) %collective-permute-start.4) | collective-permute-done | bytes 278560 | tf_op jit(solution)/shard_map/ppermute | solution.py:291
  30.7 0.5 collective-permute-start.6
  31.2 2.6 %collective-permute-done.8.refs_3_ = bf16[128,2176]{1,0:T(8,128)(2,1)S(1)} collective-permute-done((bf16[128,2176]{1,0:T(8,128)(2,1)S(1)}, bf16[128,2176]{1,0:T(8,128)(2,1)S(1)}, u32[]{:S(2)}, u32[]{:S(2)}) %collective-permute-start.8) | collective-permute-done | bytes 557088 | tf_op jit(solution)/shard_map/ppermute | solution.py:291
  33.9 1.5 %collective-permute-start.9 = (bf16[128,2176]{1,0:T(8,128)(2,1)S(1)}, bf16[128,2176]{1,0:T(8,128)(2,1)S(1)}, u32[]{:S(2)}, u32[]{:S(2)}) collective-permute-start(bf16[128,2176]{1,0:T(8,128)(2,1)S(1)} %collective-permute-done.8.refs_3_), channel_id=1, source_target_pairs={{0,16},{1,17},{2,18},{3,19},{4,20},{5,21},{6,22},{7,23},{8,24},{9,... | collective-permute-start | bytes 1671176 | tf_op jit(solution)/shard_map/ppermute | solution.py:291
  35.4 1.5 %collective-permute-start.10 = (bf16[128,2176]{1,0:T(8,128)(2,1)S(1)}, bf16[128,2176]{1,0:T(8,128)(2,1)S(1)}, u32[]{:S(2)}, u32[]{:S(2)}) collective-permute-start(bf16[128,2176]{1,0:T(8,128)(2,1)S(1)} %collective-permute-done.8.refs_3_), channel_id=1, source_target_pairs={{0,2},{1,3},{2,0},{3,1},{4,6},{5,7},{6,4},{7,5},{8,10},{9,11},{10,... | collective-permute-start | bytes 1671176 | tf_op jit(solution)/shard_map/ppermute | solution.py:291
  36.9 0.0 collective-permute-done.5.refs_6_
  36.9 1.4 %collective-permute-done.6.refs_7_ = bf16[64,2176]{1,0:T(8,128)(2,1)S(1)} collective-permute-done((bf16[64,2176]{1,0:T(8,128)(2,1)S(1)}, bf16[64,2176]{1,0:T(8,128)(2,1)S(1)}, u32[]{:S(2)}, u32[]{:S(2)}) %collective-permute-start.6) | collective-permute-done | bytes 278560 | tf_op jit(solution)/shard_map/ppermute | solution.py:291
  38.4 1.7 %collective-permute-start.13 = (bf16[128,2176]{1,0:T(8,128)(2,1)S(1)}, bf16[128,2176]{1,0:T(8,128)(2,1)S(1)}, u32[]{:S(2)}, u32[]{:S(2)}) collective-permute-start(bf16[128,2176]{1,0:T(8,128)(2,1)S(1)} %pad_maximum_fusion.1), channel_id=1, source_target_pairs={{0,4},{1,5},{2,6},{3,7},{4,0},{5,1},{6,2},{7,3},{8,12},{9,13},{10,... | collective-permute-start | bytes 1671176 | tf_op jit(solution)/shard_map/ppermute | solution.py:291
  40.1 0.0 collective-permute-done.7.refs_9_
  40.1 9.0 %run_experts.2 = (bf16[128,2048]{1,0:T(8,128)(2,1)S(1)}, bf16[128,2048]{1,0:T(8,128)(2,1)S(1)}, bf16[128,2048]{1,0:T(8,128)(2,1)S(1)}, bf16[64,2048]{1,0:T(8,128...) custom-call(s32[2]{0:T(128)S(1)} %pad_add_fusion.me_ref, ...), custom_call_target="tpu_custom_call" | custom-call | flops 6442450944 | bytes 16777216 | tf_op jit(solution)/shard_map/run_experts/pallas_call | solution.py:268
  49.1 0.1 collective-permute-done.9.refs_1_
  49.2 0.1 collective-permute-done.10.refs_2_
  49.4 0.5 collective-permute-start.11
  49.8 1.2 %collective-permute-start.14 = (bf16[128,2048]{1,0:T(8,128)(2,1)S(1)}, bf16[128,2048]{1,0:T(8,128)(2,1)S(1)}, u32[]{:S(2)}, u32[]{:S(2)}) collective-permute-start(bf16[128,2048]{1,0:T(8,128)(2,1)S(1)} %get-tuple-element.47), channel_id=1, source_target_pairs={{0,4},{1,5},{2,6},{3,7},{4,0},{5,1},{6,2},{7,3},{8,12},{9,13},{10,... | collective-permute-start | bytes 1572872 | tf_op jit(solution)/shard_map/ppermute | solution.py:291
  51.1 0.0 collective-permute-done.13.refs_0_
  51.1 1.5 %collective-permute-start.12 = (bf16[128,2048]{1,0:T(8,128)(2,1)S(1)}, bf16[128,2048]{1,0:T(8,128)(2,1)S(1)}, u32[]{:S(2)}, u32[]{:S(2)}) collective-permute-start(bf16[128,2048]{1,0:T(8,128)(2,1)S(1)} %get-tuple-element.46), channel_id=1, source_target_pairs={{0,2},{1,3},{2,0},{3,1},{4,6},{5,7},{6,4},{7,5},{8,10},{9,11},{10,... | collective-permute-start | bytes 1572872 | tf_op jit(solution)/shard_map/ppermute | solution.py:291
  52.6 9.6 %run_experts.3 = (bf16[64,2048]{1,0:T(8,128)(2,1)S(1)}, bf16[64,2048]{1,0:T(8,128)(2,1)S(1)}, bf16[64,2048]{1,0:T(8,128)(2,1)S(1)}, bf16[64,2048]{1,0:T(8,128)(2...) custom-call(s32[2]{0:T(128)S(1)} %pad_add_fusion.me_ref, ...), custom_call_target="tpu_custom_call" | custom-call | flops 6442450944 | bytes 16777216 | tf_op jit(solution)/shard_map/run_experts/pallas_call | solution.py:268
  62.2 0.2 collective-permute-done.14
  62.4 0.1 add_convert_fusion.7
  62.5 0.0 collective-permute-done.11
  62.5 1.3 %collective-permute-done.12 = bf16[128,2048]{1,0:T(8,128)(2,1)S(1)} collective-permute-done((bf16[128,2048]{1,0:T(8,128)(2,1)S(1)}, bf16[128,2048]{1,0:T(8,128)(2,1)S(1)}, u32[]{:S(2)}, u32[]{:S(2)}) %collective-permute-start.12) | collective-permute-done | bytes 524320 | tf_op jit(solution)/shard_map/ppermute | solution.py:291
  63.8 1.5 %collective-permute-start.15 = (bf16[64,2048]{1,0:T(8,128)(2,1)S(1)}, bf16[64,2048]{1,0:T(8,128)(2,1)S(1)}, u32[]{:S(2)}, u32[]{:S(2)}) collective-permute-start(bf16[64,2048]{1,0:T(8,128)(2,1)S(1)} %get-tuple-element.53), channel_id=1, source_target_pairs={{0,2},{1,3},{2,0},{3,1},{4,6},{5,7},{6,4},{7,5},{8,10},{9,11},{10,... | collective-permute-start | bytes 786440 | tf_op jit(solution)/shard_map/ppermute | solution.py:291
  65.3 0.6 collective-permute-start.16
  65.9 0.5 collective-permute-start.18
  66.5 0.1 add_convert_fusion.3
  66.6 3.4 %collective-permute-start.20 = (bf16[64,2048]{1,0:T(8,128)(2,1)S(1)}, bf16[64,2048]{1,0:T(8,128)(2,1)S(1)}, u32[]{:S(2)}, u32[]{:S(2)}) collective-permute-start(bf16[64,2048]{1,0:T(8,128)(2,1)S(1)} %add_convert_fusion.3), channel_id=1, source_target_pairs={{0,8},{1,9},{2,10},{3,11},{4,12},{5,13},{6,14},{7,15},{8,0},{9,1},... | collective-permute-start | bytes 786440 | tf_op jit(solution)/shard_map/ppermute | solution.py:291
  69.9 2.9 %collective-permute-done.15 = bf16[64,2048]{1,0:T(8,128)(2,1)S(1)} collective-permute-done((bf16[64,2048]{1,0:T(8,128)(2,1)S(1)}, bf16[64,2048]{1,0:T(8,128)(2,1)S(1)}, u32[]{:S(2)}, u32[]{:S(2)}) %collective-permute-start.15) | collective-permute-done | bytes 262176 | tf_op jit(solution)/shard_map/ppermute | solution.py:291
  72.8 0.1 add_convert_fusion.6
  72.9 0.0 collective-permute-done.16
  72.9 0.2 collective-permute-start.17
  73.2 1.8 %collective-permute-start.21 = (bf16[64,2048]{1,0:T(8,128)(2,1)S(1)}, bf16[64,2048]{1,0:T(8,128)(2,1)S(1)}, u32[]{:S(2)}, u32[]{:S(2)}) collective-permute-start(bf16[64,2048]{1,0:T(8,128)(2,1)S(1)} %get-tuple-element.63), channel_id=1, source_target_pairs={{0,16},{1,17},{2,18},{3,19},{4,20},{5,21},{6,22},{7,23},{8,24},{9,... | collective-permute-start | bytes 786440 | tf_op jit(solution)/shard_map/ppermute | solution.py:291
  75.0 0.1 add_convert_fusion.2
  75.1 1.8 %collective-permute-start.22 = (bf16[64,2048]{1,0:T(8,128)(2,1)S(1)}, bf16[64,2048]{1,0:T(8,128)(2,1)S(1)}, u32[]{:S(2)}, u32[]{:S(2)}) collective-permute-start(bf16[64,2048]{1,0:T(8,128)(2,1)S(1)} %add_convert_fusion.2), channel_id=1, source_target_pairs={{0,2},{1,3},{2,0},{3,1},{4,6},{5,7},{6,4},{7,5},{8,10},{9,11},{10,... | collective-permute-start | bytes 786440 | tf_op jit(solution)/shard_map/ppermute | solution.py:291
  76.9 1.6 %collective-permute-done.18 = bf16[64,2048]{1,0:T(8,128)(2,1)S(1)} collective-permute-done((bf16[64,2048]{1,0:T(8,128)(2,1)S(1)}, bf16[64,2048]{1,0:T(8,128)(2,1)S(1)}, u32[]{:S(2)}, u32[]{:S(2)}) %collective-permute-start.18) | collective-permute-done | bytes 262176 | tf_op jit(solution)/shard_map/ppermute | solution.py:291
  78.5 1.7 %collective-permute-done.17 = bf16[64,2048]{1,0:T(8,128)(2,1)S(1)} collective-permute-done((bf16[64,2048]{1,0:T(8,128)(2,1)S(1)}, bf16[64,2048]{1,0:T(8,128)(2,1)S(1)}, u32[]{:S(2)}, u32[]{:S(2)}) %collective-permute-start.17) | collective-permute-done | bytes 262176 | tf_op jit(solution)/shard_map/ppermute | solution.py:291
  80.1 0.1 add_convert_fusion.4
  80.2 0.6 collective-permute-start.19
  80.8 2.1 %collective-permute-done.21 = bf16[64,2048]{1,0:T(8,128)(2,1)S(1)} collective-permute-done((bf16[64,2048]{1,0:T(8,128)(2,1)S(1)}, bf16[64,2048]{1,0:T(8,128)(2,1)S(1)}, u32[]{:S(2)}, u32[]{:S(2)}) %collective-permute-start.21) | collective-permute-done | bytes 262176 | tf_op jit(solution)/shard_map/ppermute | solution.py:291
  83.0 0.0 collective-permute-done.22
  83.0 0.1 add_convert_fusion.1
  83.1 3.3 %collective-permute-start.23 = (bf16[64,2048]{1,0:T(8,128)(2,1)S(1)}, bf16[64,2048]{1,0:T(8,128)(2,1)S(1)}, u32[]{:S(2)}, u32[]{:S(2)}) collective-permute-start(bf16[64,2048]{1,0:T(8,128)(2,1)S(1)} %add_convert_fusion.1), channel_id=1, source_target_pairs={{0,12},{1,13},{2,14},{3,15},{4,8},{5,9},{6,10},{7,11},{8,4},{9,5},... | collective-permute-start | bytes 786440 | tf_op jit(solution)/shard_map/ppermute | solution.py:291
  86.4 0.0 collective-permute-done.20
  86.4 2.5 %collective-permute-done.19 = bf16[64,2048]{1,0:T(8,128)(2,1)S(1)} collective-permute-done((bf16[64,2048]{1,0:T(8,128)(2,1)S(1)}, bf16[64,2048]{1,0:T(8,128)(2,1)S(1)}, u32[]{:S(2)}, u32[]{:S(2)}) %collective-permute-start.19) | collective-permute-done | bytes 262176 | tf_op jit(solution)/shard_map/ppermute | solution.py:291
  88.8 2.8 %collective-permute-done.23 = bf16[64,2048]{1,0:T(8,128)(2,1)S(1)} collective-permute-done((bf16[64,2048]{1,0:T(8,128)(2,1)S(1)}, bf16[64,2048]{1,0:T(8,128)(2,1)S(1)}, u32[]{:S(2)}, u32[]{:S(2)}) %collective-permute-start.23) | collective-permute-done | bytes 262176 | tf_op jit(solution)/shard_map/ppermute | solution.py:291
  91.7 0.9 %add_convert_fusion = bf16[64,2048]{1,0:T(8,128)(2,1)} fusion(bf16[64,2048]{1,0:T(8,128)(2,1)S(1)} %collective-permute-done.23, bf16[64,2048]{1,0:T(8,128)(2,1)S(1)} %collective-permute-done.20, bf16[64,2048]{1,0:T(8,128)(2,1)S(1)} %collective-permute-done.19, bf16[64,2048]{1,0:T(8,128)(2,1)S(1)} %get-tuple-element.40, ...), kind=kLoop, calls=%fused_computation.2 | loop fusion | flops 1572864 | bytes 1835008 | tf_op jit(solution)/shard_map/convert_element_type | solution.py:302
  (2 shorter events, 0.1 us)
Async XLA Ops:
  1.8 16.9 %collective-permute-start.2 = (bf16[64,2176]{1,0:T(8,128)(2,1)}, bf16[64,2176]{1,0:T(8,128)(2,1)S(1)}, u32[]{:S(2)}, u32[]{:S(2)}) collective-permute-start(bf16[64,2176]{1,0:T(8,128)(2,1)} %pack.1.refs_2_), channel_id=1, source_target_pairs={{0,8},{1,9},{2,10},{3,11},{4,12},{5,13},{6,14},{7,15},{8,0},{9,1},... | collective-permute-start | bytes 835592 | tf_op jit(solution)/shard_map/ppermute | solution.py:291
  5.9 12.8 %collective-permute-start = (bf16[64,2176]{1,0:T(8,128)(2,1)}, bf16[64,2176]{1,0:T(8,128)(2,1)S(1)}, u32[]{:S(2)}, u32[]{:S(2)}) collective-permute-start(bf16[64,2176]{1,0:T(8,128)(2,1)} %pack.1.refs_2_), channel_id=1, source_target_pairs={{0,16},{1,17},{2,18},{3,19},{4,20},{5,21},{6,22},{7,23},{8,24},{9,... | collective-permute-start | bytes 835592 | tf_op jit(solution)/shard_map/ppermute | solution.py:291
  7.4 11.3 %collective-permute-start.1 = (bf16[64,2176]{1,0:T(8,128)(2,1)}, bf16[64,2176]{1,0:T(8,128)(2,1)S(1)}, u32[]{:S(2)}, u32[]{:S(2)}) collective-permute-start(bf16[64,2176]{1,0:T(8,128)(2,1)} %pack.1.refs_2_), channel_id=1, source_target_pairs={{0,2},{1,3},{2,0},{3,1},{4,6},{5,7},{6,4},{7,5},{8,10},{9,11},{10,... | collective-permute-start | bytes 835592 | tf_op jit(solution)/shard_map/ppermute | solution.py:291
  8.9 9.8 %copy-start = (bf16[64,2176]{1,0:T(8,128)(2,1)S(1)}, bf16[64,2176]{1,0:T(8,128)(2,1)}, u32[]{:S(2)}) copy-start(bf16[64,2176]{1,0:T(8,128)(2,1)} %pack.1.refs_2_) | copy-start | bytes 835588
  18.7 21.4 %collective-permute-start.7 = (bf16[2048,1536]{1,0:T(8,128)(2,1)}, bf16[2048,1536]{1,0:T(8,128)(2,1)}, u32[]{:S(2)}, u32[]{:S(2)}) collective-permute-start(bf16[2048,1536]{1,0:T(8,128)(2,1)} %scale_weights.1.refs_4_.refs_8_), channel_id=1, source_target_pairs={{0,1},{1,0},{2,3},{3,2},{4,5},{5,4},{6,7},{7,6},{8,9},{9,8},{10,11... | collective-permute-start | bytes 18874376 | tf_op jit(solution)/shard_map/ppermute | solution.py:291
  18.8 15.1 %collective-permute-start.8 = (bf16[128,2176]{1,0:T(8,128)(2,1)S(1)}, bf16[128,2176]{1,0:T(8,128)(2,1)S(1)}, u32[]{:S(2)}, u32[]{:S(2)}) collective-permute-start(bf16[128,2176]{1,0:T(8,128)(2,1)S(1)} %pad_maximum_fusion), channel_id=1, source_target_pairs={{0,4},{1,5},{2,6},{3,7},{4,0},{5,1},{6,2},{7,3},{8,12},{9,13},{10,... | collective-permute-start | bytes 1671176 | tf_op jit(solution)/shard_map/ppermute | solution.py:291
  19.7 8.8 %collective-permute-start.3 = (bf16[64,2176]{1,0:T(8,128)(2,1)S(1)}, bf16[64,2176]{1,0:T(8,128)(2,1)S(1)}, u32[]{:S(2)}, u32[]{:S(2)}) collective-permute-start(bf16[64,2176]{1,0:T(8,128)(2,1)S(1)} %collective-permute-done.2.refs_3_), channel_id=1, source_target_pairs={{0,16},{1,17},{2,18},{3,19},{4,20},{5,21},{6,22},{7,23},{8,24},{9,... | collective-permute-start | bytes 835592 | tf_op jit(solution)/shard_map/ppermute | solution.py:291
  21.2 9.5 %collective-permute-start.4 = (bf16[64,2176]{1,0:T(8,128)(2,1)S(1)}, bf16[64,2176]{1,0:T(8,128)(2,1)S(1)}, u32[]{:S(2)}, u32[]{:S(2)}) collective-permute-start(bf16[64,2176]{1,0:T(8,128)(2,1)S(1)} %collective-permute-done.2.refs_3_), channel_id=1, source_target_pairs={{0,2},{1,3},{2,0},{3,1},{4,6},{5,7},{6,4},{7,5},{8,10},{9,11},{10,... | collective-permute-start | bytes 835592 | tf_op jit(solution)/shard_map/ppermute | solution.py:291
  22.7 14.2 %collective-permute-start.5 = (bf16[64,2176]{1,0:T(8,128)(2,1)S(1)}, bf16[64,2176]{1,0:T(8,128)(2,1)S(1)}, u32[]{:S(2)}, u32[]{:S(2)}) collective-permute-start(bf16[64,2176]{1,0:T(8,128)(2,1)S(1)} %collective-permute-done.refs_0_), channel_id=1, source_target_pairs={{0,2},{1,3},{2,0},{3,1},{4,6},{5,7},{6,4},{7,5},{8,10},{9,11},{10,... | collective-permute-start | bytes 835592 | tf_op jit(solution)/shard_map/ppermute | solution.py:291
  30.7 7.6 %collective-permute-start.6 = (bf16[64,2176]{1,0:T(8,128)(2,1)S(1)}, bf16[64,2176]{1,0:T(8,128)(2,1)S(1)}, u32[]{:S(2)}, u32[]{:S(2)}) collective-permute-start(bf16[64,2176]{1,0:T(8,128)(2,1)S(1)} %collective-permute-done.4.refs_5_), channel_id=1, source_target_pairs={{0,16},{1,17},{2,18},{3,19},{4,20},{5,21},{6,22},{7,23},{8,24},{9,... | collective-permute-start | bytes 835592 | tf_op jit(solution)/shard_map/ppermute | solution.py:291
  33.9 15.4 %collective-permute-start.9 = (bf16[128,2176]{1,0:T(8,128)(2,1)S(1)}, bf16[128,2176]{1,0:T(8,128)(2,1)S(1)}, u32[]{:S(2)}, u32[]{:S(2)}) collective-permute-start(bf16[128,2176]{1,0:T(8,128)(2,1)S(1)} %collective-permute-done.8.refs_3_), channel_id=1, source_target_pairs={{0,16},{1,17},{2,18},{3,19},{4,20},{5,21},{6,22},{7,23},{8,24},{9,... | collective-permute-start | bytes 1671176 | tf_op jit(solution)/shard_map/ppermute | solution.py:291
  35.4 14.0 %collective-permute-start.10 = (bf16[128,2176]{1,0:T(8,128)(2,1)S(1)}, bf16[128,2176]{1,0:T(8,128)(2,1)S(1)}, u32[]{:S(2)}, u32[]{:S(2)}) collective-permute-start(bf16[128,2176]{1,0:T(8,128)(2,1)S(1)} %collective-permute-done.8.refs_3_), channel_id=1, source_target_pairs={{0,2},{1,3},{2,0},{3,1},{4,6},{5,7},{6,4},{7,5},{8,10},{9,11},{10,... | collective-permute-start | bytes 1671176 | tf_op jit(solution)/shard_map/ppermute | solution.py:291
  38.4 12.7 %collective-permute-start.13 = (bf16[128,2176]{1,0:T(8,128)(2,1)S(1)}, bf16[128,2176]{1,0:T(8,128)(2,1)S(1)}, u32[]{:S(2)}, u32[]{:S(2)}) collective-permute-start(bf16[128,2176]{1,0:T(8,128)(2,1)S(1)} %pad_maximum_fusion.1), channel_id=1, source_target_pairs={{0,4},{1,5},{2,6},{3,7},{4,0},{5,1},{6,2},{7,3},{8,12},{9,13},{10,... | collective-permute-start | bytes 1671176 | tf_op jit(solution)/shard_map/ppermute | solution.py:291
  49.4 13.2 %collective-permute-start.11 = (bf16[128,2048]{1,0:T(8,128)(2,1)S(1)}, bf16[128,2048]{1,0:T(8,128)(2,1)S(1)}, u32[]{:S(2)}, u32[]{:S(2)}) collective-permute-start(bf16[128,2048]{1,0:T(8,128)(2,1)S(1)} %get-tuple-element.44), channel_id=1, source_target_pairs={{0,16},{1,17},{2,18},{3,19},{4,20},{5,21},{6,22},{7,23},{8,24},{9,... | collective-permute-start | bytes 1572872 | tf_op jit(solution)/shard_map/ppermute | solution.py:291
  49.8 12.5 %collective-permute-start.14 = (bf16[128,2048]{1,0:T(8,128)(2,1)S(1)}, bf16[128,2048]{1,0:T(8,128)(2,1)S(1)}, u32[]{:S(2)}, u32[]{:S(2)}) collective-permute-start(bf16[128,2048]{1,0:T(8,128)(2,1)S(1)} %get-tuple-element.47), channel_id=1, source_target_pairs={{0,4},{1,5},{2,6},{3,7},{4,0},{5,1},{6,2},{7,3},{8,12},{9,13},{10,... | collective-permute-start | bytes 1572872 | tf_op jit(solution)/shard_map/ppermute | solution.py:291
  51.1 12.7 %collective-permute-start.12 = (bf16[128,2048]{1,0:T(8,128)(2,1)S(1)}, bf16[128,2048]{1,0:T(8,128)(2,1)S(1)}, u32[]{:S(2)}, u32[]{:S(2)}) collective-permute-start(bf16[128,2048]{1,0:T(8,128)(2,1)S(1)} %get-tuple-element.46), channel_id=1, source_target_pairs={{0,2},{1,3},{2,0},{3,1},{4,6},{5,7},{6,4},{7,5},{8,10},{9,11},{10,... | collective-permute-start | bytes 1572872 | tf_op jit(solution)/shard_map/ppermute | solution.py:291
  63.8 9.0 %collective-permute-start.15 = (bf16[64,2048]{1,0:T(8,128)(2,1)S(1)}, bf16[64,2048]{1,0:T(8,128)(2,1)S(1)}, u32[]{:S(2)}, u32[]{:S(2)}) collective-permute-start(bf16[64,2048]{1,0:T(8,128)(2,1)S(1)} %get-tuple-element.53), channel_id=1, source_target_pairs={{0,2},{1,3},{2,0},{3,1},{4,6},{5,7},{6,4},{7,5},{8,10},{9,11},{10,... | collective-permute-start | bytes 786440 | tf_op jit(solution)/shard_map/ppermute | solution.py:291
  65.3 7.6 %collective-permute-start.16 = (bf16[64,2048]{1,0:T(8,128)(2,1)S(1)}, bf16[64,2048]{1,0:T(8,128)(2,1)S(1)}, u32[]{:S(2)}, u32[]{:S(2)}) collective-permute-start(bf16[64,2048]{1,0:T(8,128)(2,1)S(1)} %get-tuple-element.55), channel_id=1, source_target_pairs={{0,16},{1,17},{2,18},{3,19},{4,20},{5,21},{6,22},{7,23},{8,24},{9,... | collective-permute-start | bytes 786440 | tf_op jit(solution)/shard_map/ppermute | solution.py:291
  65.9 12.5 %collective-permute-start.18 = (bf16[64,2048]{1,0:T(8,128)(2,1)S(1)}, bf16[64,2048]{1,0:T(8,128)(2,1)S(1)}, u32[]{:S(2)}, u32[]{:S(2)}) collective-permute-start(bf16[64,2048]{1,0:T(8,128)(2,1)S(1)} %get-tuple-element.58), channel_id=1, source_target_pairs={{0,2},{1,3},{2,0},{3,1},{4,6},{5,7},{6,4},{7,5},{8,10},{9,11},{10,... | collective-permute-start | bytes 786440 | tf_op jit(solution)/shard_map/ppermute | solution.py:291
  66.6 19.8 %collective-permute-start.20 = (bf16[64,2048]{1,0:T(8,128)(2,1)S(1)}, bf16[64,2048]{1,0:T(8,128)(2,1)S(1)}, u32[]{:S(2)}, u32[]{:S(2)}) collective-permute-start(bf16[64,2048]{1,0:T(8,128)(2,1)S(1)} %add_convert_fusion.3), channel_id=1, source_target_pairs={{0,8},{1,9},{2,10},{3,11},{4,12},{5,13},{6,14},{7,15},{8,0},{9,1},... | collective-permute-start | bytes 786440 | tf_op jit(solution)/shard_map/ppermute | solution.py:291
  72.9 7.2 %collective-permute-start.17 = (bf16[64,2048]{1,0:T(8,128)(2,1)S(1)}, bf16[64,2048]{1,0:T(8,128)(2,1)S(1)}, u32[]{:S(2)}, u32[]{:S(2)}) collective-permute-start(bf16[64,2048]{1,0:T(8,128)(2,1)S(1)} %add_convert_fusion.6), channel_id=1, source_target_pairs={{0,16},{1,17},{2,18},{3,19},{4,20},{5,21},{6,22},{7,23},{8,24},{9,... | collective-permute-start | bytes 786440 | tf_op jit(solution)/shard_map/ppermute | solution.py:291
  73.2 9.8 %collective-permute-start.21 = (bf16[64,2048]{1,0:T(8,128)(2,1)S(1)}, bf16[64,2048]{1,0:T(8,128)(2,1)S(1)}, u32[]{:S(2)}, u32[]{:S(2)}) collective-permute-start(bf16[64,2048]{1,0:T(8,128)(2,1)S(1)} %get-tuple-element.63), channel_id=1, source_target_pairs={{0,16},{1,17},{2,18},{3,19},{4,20},{5,21},{6,22},{7,23},{8,24},{9,... | collective-permute-start | bytes 786440 | tf_op jit(solution)/shard_map/ppermute | solution.py:291
  75.1 7.9 %collective-permute-start.22 = (bf16[64,2048]{1,0:T(8,128)(2,1)S(1)}, bf16[64,2048]{1,0:T(8,128)(2,1)S(1)}, u32[]{:S(2)}, u32[]{:S(2)}) collective-permute-start(bf16[64,2048]{1,0:T(8,128)(2,1)S(1)} %add_convert_fusion.2), channel_id=1, source_target_pairs={{0,2},{1,3},{2,0},{3,1},{4,6},{5,7},{6,4},{7,5},{8,10},{9,11},{10,... | collective-permute-start | bytes 786440 | tf_op jit(solution)/shard_map/ppermute | solution.py:291
  80.2 8.6 %collective-permute-start.19 = (bf16[64,2048]{1,0:T(8,128)(2,1)S(1)}, bf16[64,2048]{1,0:T(8,128)(2,1)S(1)}, u32[]{:S(2)}, u32[]{:S(2)}) collective-permute-start(bf16[64,2048]{1,0:T(8,128)(2,1)S(1)} %add_convert_fusion.4), channel_id=1, source_target_pairs={{0,4},{1,5},{2,6},{3,7},{4,0},{5,1},{6,2},{7,3},{8,12},{9,13},{10,... | collective-permute-start | bytes 786440 | tf_op jit(solution)/shard_map/ppermute | solution.py:291
  83.1 8.6 %collective-permute-start.23 = (bf16[64,2048]{1,0:T(8,128)(2,1)S(1)}, bf16[64,2048]{1,0:T(8,128)(2,1)S(1)}, u32[]{:S(2)}, u32[]{:S(2)}) collective-permute-start(bf16[64,2048]{1,0:T(8,128)(2,1)S(1)} %add_convert_fusion.1), channel_id=1, source_target_pairs={{0,12},{1,13},{2,14},{3,15},{4,8},{5,9},{6,10},{7,11},{8,4},{9,5},... | collective-permute-start | bytes 786440 | tf_op jit(solution)/shard_map/ppermute | solution.py:291

commit v6 on v4

--- a/solution.py
+++ b/solution.py
@@ -364,7 +364,7 @@
     by1 = send(after(y1, bx02, by02, bd02), y)
     bx3 = send(after(x3, bd3), x)
     by3 = send(add(y3, bd3), y)
-    bx1 = send(after(add(x1, bd1), bd3, bx3), x)
+    bx1 = send(after(add(x1, bd1), bd3), x)
     bs3 = send(add(s3, bx3, by3), z3)
     bs1 = send(add(s1, bx1, by1), z1)
     return add(s0, bx02[:rows], by02[:rows], bs1, bs2, bs3)

time: 95.5 us -> 92.5 us (0.969)
  waiting for transfers between devices: 28.3 us -> 24.8 us
    ppermute x24, waiting for transfers between devices: 28.3 us -> 24.8 us  [hop(): return lax.ppermute(value, AXES, [(i, i ^ bit) for i in range(devices)])]
  transfers between devices with their start and end apart: 24 -> 24, of which waited for: 14 -> 14; matrix products, arithmetic and copies ran while one was open for 1% -> 1% of each run, Pallas kernels for 30% -> 31%
where the time goes in v6:
time: 92.5 us; the launch traced here: 92.2 us
  starting transfers between devices  35.4 us (38%)
  Pallas kernels  30.2 us (33%)
  waiting for transfers between devices  24.8 us (27%)
  other arithmetic  1.64 us (2%)
    ppermute x24, starting transfers between devices, hop(): return lax.ppermute(value, AXES, [(i, i ^ bit) for i in range(devices)])  35.4 us
    ppermute x24, waiting for transfers between devices, hop(): return lax.ppermute(value, AXES, [(i, i ^ bit) for i in range(devices)])  24.8 us
    pallas_call x2, Pallas kernels, run_experts(): pl.pallas_call(functools.partial(expert_kernel, blocks=len(messages), pla...  18.6 us
    pallas_call x1, Pallas kernels, scale_weights(): pl.pallas_call(functools.partial(scale_kernel, pieces=pieces), in_specs=[...  5.73 us
    pallas_call x1, Pallas kernels, own_hidden(): pl.pallas_call(hidden_kernel, in_specs=[pl.BlockSpec(memory_space=pltpu.S...  4.05 us
  transfers between devices with their start and end apart: 24, of which 14 were waited for; matrix products, arithmetic and copies ran while one was open for 1% of the time, Pallas kernels for 31%

profile of v6, /device:TPU:0, one launch (start us, length us, event | category | flops | bytes accessed | tf_op | source)
XLA Modules:
  0.0 92.2 jit_solution(5784640941762144453)
XLA Ops:
  0.0 1.8 %pack.1.refs_2_ = bf16[64,2176]{1,0:T(8,128)(2,1)} custom-call(f32[8,64]{1,0:T(8,128)} %bitcast.14, s32[8,64]{1,0:T(8,128)} %bitcast.15, s32[8,64]{1,0:T(8,128)} %bitcast.16, bf16[64,2048]{1,0:T(8,128)(2,1)} %tokens_ref.1), custom_call_target="tpu_custom_call" | custom-call | flops 131072 | bytes 524288 | tf_op jit(solution)/shard_map/pack/pallas_call | solution.py:89
  1.8 4.0 %collective-permute-start.2 = (bf16[64,2176]{1,0:T(8,128)(2,1)}, bf16[64,2176]{1,0:T(8,128)(2,1)S(1)}, u32[]{:S(2)}, u32[]{:S(2)}) collective-permute-start(bf16[64,2176]{1,0:T(8,128)(2,1)} %pack.1.refs_2_), channel_id=1, source_target_pairs={{0,8},{1,9},{2,10},{3,11},{4,12},{5,13},{6,14},{7,15},{8,0},{9,1},... | collective-permute-start | bytes 835592 | tf_op jit(solution)/shard_map/ppermute | solution.py:291
  5.9 1.5 %collective-permute-start = (bf16[64,2176]{1,0:T(8,128)(2,1)}, bf16[64,2176]{1,0:T(8,128)(2,1)S(1)}, u32[]{:S(2)}, u32[]{:S(2)}) collective-permute-start(bf16[64,2176]{1,0:T(8,128)(2,1)} %pack.1.refs_2_), channel_id=1, source_target_pairs={{0,16},{1,17},{2,18},{3,19},{4,20},{5,21},{6,22},{7,23},{8,24},{9,... | collective-permute-start | bytes 835592 | tf_op jit(solution)/shard_map/ppermute | solution.py:291
  7.4 1.5 %collective-permute-start.1 = (bf16[64,2176]{1,0:T(8,128)(2,1)}, bf16[64,2176]{1,0:T(8,128)(2,1)S(1)}, u32[]{:S(2)}, u32[]{:S(2)}) collective-permute-start(bf16[64,2176]{1,0:T(8,128)(2,1)} %pack.1.refs_2_), channel_id=1, source_target_pairs={{0,2},{1,3},{2,0},{3,1},{4,6},{5,7},{6,4},{7,5},{8,10},{9,11},{10,... | collective-permute-start | bytes 835592 | tf_op jit(solution)/shard_map/ppermute | solution.py:291
  8.9 0.0 copy-start
  8.9 5.7 %scale_weights.1.refs_4_.refs_8_ = bf16[2048,1536]{1,0:T(8,128)(2,1)} custom-call(f32[4,16]{1,0:T(4,128)} %bitcast.17, f32[4,16]{1,0:T(4,128)} %bitcast.18, f32[4,16]{1,0:T(4,128)} %bitcast.19, bf16[1,2048,512]{2,1,0:T(8,128)(2,1)} %refs_3_.1, bf16[1,2048,512]{2,1,0:T(8,128)(2,1)} %refs_4_.1, bf16[1,2048,512]{2,1,0:T(8,128)(2,1)} %refs_5_.1), custom_call_target="tpu_custom_call" | custom-call | flops 3145728 | bytes 12582912 | tf_op jit(solution)/shard_map/scale_weights/pallas_call | solution.py:142
  14.6 4.1 %collective-permute-done.2.refs_3_ = bf16[64,2176]{1,0:T(8,128)(2,1)S(1)} collective-permute-done((bf16[64,2176]{1,0:T(8,128)(2,1)}, bf16[64,2176]{1,0:T(8,128)(2,1)S(1)}, u32[]{:S(2)}, u32[]{:S(2)}) %collective-permute-start.2) | collective-permute-done | bytes 278560 | tf_op jit(solution)/shard_map/ppermute | solution.py:291
  18.7 0.0 collective-permute-done.refs_0_
  18.7 0.0 collective-permute-done.1.refs_1_
  18.7 0.0 collective-permute-start.7
  18.7 0.0 copy-done
  18.8 0.9 collective-permute-start.8
  19.7 1.5 %collective-permute-start.3 = (bf16[64,2176]{1,0:T(8,128)(2,1)S(1)}, bf16[64,2176]{1,0:T(8,128)(2,1)S(1)}, u32[]{:S(2)}, u32[]{:S(2)}) collective-permute-start(bf16[64,2176]{1,0:T(8,128)(2,1)S(1)} %collective-permute-done.2.refs_3_), channel_id=1, source_target_pairs={{0,16},{1,17},{2,18},{3,19},{4,20},{5,21},{6,22},{7,23},{8,24},{9,... | collective-permute-start | bytes 835592 | tf_op jit(solution)/shard_map/ppermute | solution.py:291
  21.2 1.5 %collective-permute-start.4 = (bf16[64,2176]{1,0:T(8,128)(2,1)S(1)}, bf16[64,2176]{1,0:T(8,128)(2,1)S(1)}, u32[]{:S(2)}, u32[]{:S(2)}) collective-permute-start(bf16[64,2176]{1,0:T(8,128)(2,1)S(1)} %collective-permute-done.2.refs_3_), channel_id=1, source_target_pairs={{0,2},{1,3},{2,0},{3,1},{4,6},{5,7},{6,4},{7,5},{8,10},{9,11},{10,... | collective-permute-start | bytes 835592 | tf_op jit(solution)/shard_map/ppermute | solution.py:291
  22.7 0.1 pad_add_fusion.me_ref
  22.7 0.5 collective-permute-start.5
  23.3 4.1 %own_hidden.1.refs_10_ = bf16[256,512]{1,0:T(8,128)(2,1)S(1)} custom-call(s32[2]{0:T(128)S(1)} %pad_add_fusion.me_ref, bf16[64,2176]{1,0:T(8,128)(2,1)S(1)} %collective-permute-done.refs_0_, bf16[64,2176]{1,0:T(8,128)(2,1)S(1)} %collective-permute-done.1.refs_1_, bf16[64,2176]{1,0:T(8,128)(2,1)S(1)} %copy-done, ...), custom_call_target="tpu_custom_call" | custom-call | flops 1073741824 | bytes 5242880 | tf_op jit(solution)/shard_map/own_hidden/pallas_call | solution.py:188
  27.3 1.1 %collective-permute-done.3.refs_4_ = bf16[64,2176]{1,0:T(8,128)(2,1)S(1)} collective-permute-done((bf16[64,2176]{1,0:T(8,128)(2,1)S(1)}, bf16[64,2176]{1,0:T(8,128)(2,1)S(1)}, u32[]{:S(2)}, u32[]{:S(2)}) %collective-permute-start.3) | collective-permute-done | bytes 278560 | tf_op jit(solution)/shard_map/ppermute | solution.py:291
  28.4 2.3 %collective-permute-done.4.refs_5_ = bf16[64,2176]{1,0:T(8,128)(2,1)S(1)} collective-permute-done((bf16[64,2176]{1,0:T(8,128)(2,1)S(1)}, bf16[64,2176]{1,0:T(8,128)(2,1)S(1)}, u32[]{:S(2)}, u32[]{:S(2)}) %collective-permute-start.4) | collective-permute-done | bytes 278560 | tf_op jit(solution)/shard_map/ppermute | solution.py:291
  30.7 0.5 collective-permute-start.6
  31.2 2.6 %collective-permute-done.8.refs_3_ = bf16[128,2176]{1,0:T(8,128)(2,1)S(1)} collective-permute-done((bf16[128,2176]{1,0:T(8,128)(2,1)S(1)}, bf16[128,2176]{1,0:T(8,128)(2,1)S(1)}, u32[]{:S(2)}, u32[]{:S(2)}) %collective-permute-start.8) | collective-permute-done | bytes 557088 | tf_op jit(solution)/shard_map/ppermute | solution.py:291
  33.9 1.5 %collective-permute-start.9 = (bf16[128,2176]{1,0:T(8,128)(2,1)S(1)}, bf16[128,2176]{1,0:T(8,128)(2,1)S(1)}, u32[]{:S(2)}, u32[]{:S(2)}) collective-permute-start(bf16[128,2176]{1,0:T(8,128)(2,1)S(1)} %collective-permute-done.8.refs_3_), channel_id=1, source_target_pairs={{0,16},{1,17},{2,18},{3,19},{4,20},{5,21},{6,22},{7,23},{8,24},{9,... | collective-permute-start | bytes 1671176 | tf_op jit(solution)/shard_map/ppermute | solution.py:291
  35.4 1.5 %collective-permute-start.10 = (bf16[128,2176]{1,0:T(8,128)(2,1)S(1)}, bf16[128,2176]{1,0:T(8,128)(2,1)S(1)}, u32[]{:S(2)}, u32[]{:S(2)}) collective-permute-start(bf16[128,2176]{1,0:T(8,128)(2,1)S(1)} %collective-permute-done.8.refs_3_), channel_id=1, source_target_pairs={{0,2},{1,3},{2,0},{3,1},{4,6},{5,7},{6,4},{7,5},{8,10},{9,11},{10,... | collective-permute-start | bytes 1671176 | tf_op jit(solution)/shard_map/ppermute | solution.py:291
  36.9 0.0 collective-permute-done.5.refs_6_
  36.9 1.4 %collective-permute-done.6.refs_7_ = bf16[64,2176]{1,0:T(8,128)(2,1)S(1)} collective-permute-done((bf16[64,2176]{1,0:T(8,128)(2,1)S(1)}, bf16[64,2176]{1,0:T(8,128)(2,1)S(1)}, u32[]{:S(2)}, u32[]{:S(2)}) %collective-permute-start.6) | collective-permute-done | bytes 278560 | tf_op jit(solution)/shard_map/ppermute | solution.py:291
  38.4 1.7 %collective-permute-start.13 = (bf16[128,2176]{1,0:T(8,128)(2,1)S(1)}, bf16[128,2176]{1,0:T(8,128)(2,1)S(1)}, u32[]{:S(2)}, u32[]{:S(2)}) collective-permute-start(bf16[128,2176]{1,0:T(8,128)(2,1)S(1)} %pad_maximum_fusion.1), channel_id=1, source_target_pairs={{0,4},{1,5},{2,6},{3,7},{4,0},{5,1},{6,2},{7,3},{8,12},{9,13},{10,... | collective-permute-start | bytes 1671176 | tf_op jit(solution)/shard_map/ppermute | solution.py:291
  40.1 0.0 collective-permute-done.7.refs_9_
  40.1 9.0 %run_experts.2 = (bf16[128,2048]{1,0:T(8,128)(2,1)S(1)}, bf16[128,2048]{1,0:T(8,128)(2,1)S(1)}, bf16[128,2048]{1,0:T(8,128)(2,1)S(1)}, bf16[64,2048]{1,0:T(8,128...) custom-call(s32[2]{0:T(128)S(1)} %pad_add_fusion.me_ref, ...), custom_call_target="tpu_custom_call" | custom-call | flops 6442450944 | bytes 16777216 | tf_op jit(solution)/shard_map/run_experts/pallas_call | solution.py:268
  49.1 0.1 collective-permute-done.9.refs_1_
  49.2 0.1 collective-permute-done.10.refs_2_
  49.4 0.5 collective-permute-start.11
  49.8 1.2 %collective-permute-start.14 = (bf16[128,2048]{1,0:T(8,128)(2,1)S(1)}, bf16[128,2048]{1,0:T(8,128)(2,1)S(1)}, u32[]{:S(2)}, u32[]{:S(2)}) collective-permute-start(bf16[128,2048]{1,0:T(8,128)(2,1)S(1)} %get-tuple-element.47), channel_id=1, source_target_pairs={{0,4},{1,5},{2,6},{3,7},{4,0},{5,1},{6,2},{7,3},{8,12},{9,13},{10,... | collective-permute-start | bytes 1572872 | tf_op jit(solution)/shard_map/ppermute | solution.py:291
  51.1 0.0 collective-permute-done.13.refs_0_
  51.1 1.5 %collective-permute-start.12 = (bf16[128,2048]{1,0:T(8,128)(2,1)S(1)}, bf16[128,2048]{1,0:T(8,128)(2,1)S(1)}, u32[]{:S(2)}, u32[]{:S(2)}) collective-permute-start(bf16[128,2048]{1,0:T(8,128)(2,1)S(1)} %get-tuple-element.46), channel_id=1, source_target_pairs={{0,2},{1,3},{2,0},{3,1},{4,6},{5,7},{6,4},{7,5},{8,10},{9,11},{10,... | collective-permute-start | bytes 1572872 | tf_op jit(solution)/shard_map/ppermute | solution.py:291
  52.6 9.6 %run_experts.3 = (bf16[64,2048]{1,0:T(8,128)(2,1)S(1)}, bf16[64,2048]{1,0:T(8,128)(2,1)S(1)}, bf16[64,2048]{1,0:T(8,128)(2,1)S(1)}, bf16[64,2048]{1,0:T(8,128)(2...) custom-call(s32[2]{0:T(128)S(1)} %pad_add_fusion.me_ref, ...), custom_call_target="tpu_custom_call" | custom-call | flops 6442450944 | bytes 16777216 | tf_op jit(solution)/shard_map/run_experts/pallas_call | solution.py:268
  62.2 0.2 collective-permute-done.14
  62.4 0.1 add_convert_fusion.7
  62.5 0.0 collective-permute-done.11
  62.5 1.6 %collective-permute-start.15 = (bf16[64,2048]{1,0:T(8,128)(2,1)S(1)}, bf16[64,2048]{1,0:T(8,128)(2,1)S(1)}, u32[]{:S(2)}, u32[]{:S(2)}) collective-permute-start(bf16[64,2048]{1,0:T(8,128)(2,1)S(1)} %get-tuple-element.53), channel_id=1, source_target_pairs={{0,2},{1,3},{2,0},{3,1},{4,6},{5,7},{6,4},{7,5},{8,10},{9,11},{10,... | collective-permute-start | bytes 786440 | tf_op jit(solution)/shard_map/ppermute | solution.py:291
  64.1 1.5 %collective-permute-start.16 = (bf16[64,2048]{1,0:T(8,128)(2,1)S(1)}, bf16[64,2048]{1,0:T(8,128)(2,1)S(1)}, u32[]{:S(2)}, u32[]{:S(2)}) collective-permute-start(bf16[64,2048]{1,0:T(8,128)(2,1)S(1)} %get-tuple-element.55), channel_id=1, source_target_pairs={{0,16},{1,17},{2,18},{3,19},{4,20},{5,21},{6,22},{7,23},{8,24},{9,... | collective-permute-start | bytes 786440 | tf_op jit(solution)/shard_map/ppermute | solution.py:291
  65.6 0.0 collective-permute-done.12
  65.6 0.6 collective-permute-start.18
  66.2 0.1 add_convert_fusion.3
  66.3 2.9 %collective-permute-start.20 = (bf16[64,2048]{1,0:T(8,128)(2,1)S(1)}, bf16[64,2048]{1,0:T(8,128)(2,1)S(1)}, u32[]{:S(2)}, u32[]{:S(2)}) collective-permute-start(bf16[64,2048]{1,0:T(8,128)(2,1)S(1)} %add_convert_fusion.3), channel_id=1, source_target_pairs={{0,8},{1,9},{2,10},{3,11},{4,12},{5,13},{6,14},{7,15},{8,0},{9,1},... | collective-permute-start | bytes 786440 | tf_op jit(solution)/shard_map/ppermute | solution.py:291
  69.2 2.6 %collective-permute-done.15 = bf16[64,2048]{1,0:T(8,128)(2,1)S(1)} collective-permute-done((bf16[64,2048]{1,0:T(8,128)(2,1)S(1)}, bf16[64,2048]{1,0:T(8,128)(2,1)S(1)}, u32[]{:S(2)}, u32[]{:S(2)}) %collective-permute-start.15) | collective-permute-done | bytes 262176 | tf_op jit(solution)/shard_map/ppermute | solution.py:291
  71.8 0.1 add_convert_fusion.6
  71.9 0.0 collective-permute-done.16
  71.9 1.1 %collective-permute-start.17 = (bf16[64,2048]{1,0:T(8,128)(2,1)S(1)}, bf16[64,2048]{1,0:T(8,128)(2,1)S(1)}, u32[]{:S(2)}, u32[]{:S(2)}) collective-permute-start(bf16[64,2048]{1,0:T(8,128)(2,1)S(1)} %add_convert_fusion.6), channel_id=1, source_target_pairs={{0,16},{1,17},{2,18},{3,19},{4,20},{5,21},{6,22},{7,23},{8,24},{9,... | collective-permute-start | bytes 786440 | tf_op jit(solution)/shard_map/ppermute | solution.py:291
  73.0 1.0 %collective-permute-start.21 = (bf16[64,2048]{1,0:T(8,128)(2,1)S(1)}, bf16[64,2048]{1,0:T(8,128)(2,1)S(1)}, u32[]{:S(2)}, u32[]{:S(2)}) collective-permute-start(bf16[64,2048]{1,0:T(8,128)(2,1)S(1)} %get-tuple-element.63), channel_id=1, source_target_pairs={{0,16},{1,17},{2,18},{3,19},{4,20},{5,21},{6,22},{7,23},{8,24},{9,... | collective-permute-start | bytes 786440 | tf_op jit(solution)/shard_map/ppermute | solution.py:291
  74.0 0.1 add_convert_fusion.2
  74.1 1.6 %collective-permute-start.22 = (bf16[64,2048]{1,0:T(8,128)(2,1)S(1)}, bf16[64,2048]{1,0:T(8,128)(2,1)S(1)}, u32[]{:S(2)}, u32[]{:S(2)}) collective-permute-start(bf16[64,2048]{1,0:T(8,128)(2,1)S(1)} %add_convert_fusion.2), channel_id=1, source_target_pairs={{0,2},{1,3},{2,0},{3,1},{4,6},{5,7},{6,4},{7,5},{8,10},{9,11},{10,... | collective-permute-start | bytes 786440 | tf_op jit(solution)/shard_map/ppermute | solution.py:291
  75.6 1.8 %collective-permute-done.18 = bf16[64,2048]{1,0:T(8,128)(2,1)S(1)} collective-permute-done((bf16[64,2048]{1,0:T(8,128)(2,1)S(1)}, bf16[64,2048]{1,0:T(8,128)(2,1)S(1)}, u32[]{:S(2)}, u32[]{:S(2)}) %collective-permute-start.18) | collective-permute-done | bytes 262176 | tf_op jit(solution)/shard_map/ppermute | solution.py:291
  77.4 1.5 %collective-permute-done.17 = bf16[64,2048]{1,0:T(8,128)(2,1)S(1)} collective-permute-done((bf16[64,2048]{1,0:T(8,128)(2,1)S(1)}, bf16[64,2048]{1,0:T(8,128)(2,1)S(1)}, u32[]{:S(2)}, u32[]{:S(2)}) %collective-permute-start.17) | collective-permute-done | bytes 262176 | tf_op jit(solution)/shard_map/ppermute | solution.py:291
  78.9 0.1 add_convert_fusion.4
  79.0 1.8 %collective-permute-start.19 = (bf16[64,2048]{1,0:T(8,128)(2,1)S(1)}, bf16[64,2048]{1,0:T(8,128)(2,1)S(1)}, u32[]{:S(2)}, u32[]{:S(2)}) collective-permute-start(bf16[64,2048]{1,0:T(8,128)(2,1)S(1)} %add_convert_fusion.4), channel_id=1, source_target_pairs={{0,4},{1,5},{2,6},{3,7},{4,0},{5,1},{6,2},{7,3},{8,12},{9,13},{10,... | collective-permute-start | bytes 786440 | tf_op jit(solution)/shard_map/ppermute | solution.py:291
  80.8 0.9 collective-permute-done.21
  81.7 0.0 collective-permute-done.22
  81.7 0.1 add_convert_fusion.1
  81.8 3.4 %collective-permute-start.23 = (bf16[64,2048]{1,0:T(8,128)(2,1)S(1)}, bf16[64,2048]{1,0:T(8,128)(2,1)S(1)}, u32[]{:S(2)}, u32[]{:S(2)}) collective-permute-start(bf16[64,2048]{1,0:T(8,128)(2,1)S(1)} %add_convert_fusion.1), channel_id=1, source_target_pairs={{0,12},{1,13},{2,14},{3,15},{4,8},{5,9},{6,10},{7,11},{8,4},{9,5},... | collective-permute-start | bytes 786440 | tf_op jit(solution)/shard_map/ppermute | solution.py:291
  85.2 0.0 collective-permute-done.20
  85.2 3.1 %collective-permute-done.19 = bf16[64,2048]{1,0:T(8,128)(2,1)S(1)} collective-permute-done((bf16[64,2048]{1,0:T(8,128)(2,1)S(1)}, bf16[64,2048]{1,0:T(8,128)(2,1)S(1)}, u32[]{:S(2)}, u32[]{:S(2)}) %collective-permute-start.19) | collective-permute-done | bytes 262176 | tf_op jit(solution)/shard_map/ppermute | solution.py:291
  88.3 3.1 %collective-permute-done.23 = bf16[64,2048]{1,0:T(8,128)(2,1)S(1)} collective-permute-done((bf16[64,2048]{1,0:T(8,128)(2,1)S(1)}, bf16[64,2048]{1,0:T(8,128)(2,1)S(1)}, u32[]{:S(2)}, u32[]{:S(2)}) %collective-permute-start.23) | collective-permute-done | bytes 262176 | tf_op jit(solution)/shard_map/ppermute | solution.py:291
  91.3 0.9 %add_convert_fusion = bf16[64,2048]{1,0:T(8,128)(2,1)} fusion(bf16[64,2048]{1,0:T(8,128)(2,1)S(1)} %collective-permute-done.23, bf16[64,2048]{1,0:T(8,128)(2,1)S(1)} %collective-permute-done.20, bf16[64,2048]{1,0:T(8,128)(2,1)S(1)} %collective-permute-done.19, bf16[64,2048]{1,0:T(8,128)(2,1)S(1)} %get-tuple-element.40, ...), kind=kLoop, calls=%fused_computation.2 | loop fusion | flops 1572864 | bytes 1835008 | tf_op jit(solution)/shard_map/convert_element_type | solution.py:302
  (2 shorter events, 0.1 us)
Async XLA Ops:
  1.8 16.9 %collective-permute-start.2 = (bf16[64,2176]{1,0:T(8,128)(2,1)}, bf16[64,2176]{1,0:T(8,128)(2,1)S(1)}, u32[]{:S(2)}, u32[]{:S(2)}) collective-permute-start(bf16[64,2176]{1,0:T(8,128)(2,1)} %pack.1.refs_2_), channel_id=1, source_target_pairs={{0,8},{1,9},{2,10},{3,11},{4,12},{5,13},{6,14},{7,15},{8,0},{9,1},... | collective-permute-start | bytes 835592 | tf_op jit(solution)/shard_map/ppermute | solution.py:291
  5.9 12.8 %collective-permute-start = (bf16[64,2176]{1,0:T(8,128)(2,1)}, bf16[64,2176]{1,0:T(8,128)(2,1)S(1)}, u32[]{:S(2)}, u32[]{:S(2)}) collective-permute-start(bf16[64,2176]{1,0:T(8,128)(2,1)} %pack.1.refs_2_), channel_id=1, source_target_pairs={{0,16},{1,17},{2,18},{3,19},{4,20},{5,21},{6,22},{7,23},{8,24},{9,... | collective-permute-start | bytes 835592 | tf_op jit(solution)/shard_map/ppermute | solution.py:291
  7.4 11.3 %collective-permute-start.1 = (bf16[64,2176]{1,0:T(8,128)(2,1)}, bf16[64,2176]{1,0:T(8,128)(2,1)S(1)}, u32[]{:S(2)}, u32[]{:S(2)}) collective-permute-start(bf16[64,2176]{1,0:T(8,128)(2,1)} %pack.1.refs_2_), channel_id=1, source_target_pairs={{0,2},{1,3},{2,0},{3,1},{4,6},{5,7},{6,4},{7,5},{8,10},{9,11},{10,... | collective-permute-start | bytes 835592 | tf_op jit(solution)/shard_map/ppermute | solution.py:291
  8.9 9.8 %copy-start = (bf16[64,2176]{1,0:T(8,128)(2,1)S(1)}, bf16[64,2176]{1,0:T(8,128)(2,1)}, u32[]{:S(2)}) copy-start(bf16[64,2176]{1,0:T(8,128)(2,1)} %pack.1.refs_2_) | copy-start | bytes 835588
  18.7 21.4 %collective-permute-start.7 = (bf16[2048,1536]{1,0:T(8,128)(2,1)}, bf16[2048,1536]{1,0:T(8,128)(2,1)}, u32[]{:S(2)}, u32[]{:S(2)}) collective-permute-start(bf16[2048,1536]{1,0:T(8,128)(2,1)} %scale_weights.1.refs_4_.refs_8_), channel_id=1, source_target_pairs={{0,1},{1,0},{2,3},{3,2},{4,5},{5,4},{6,7},{7,6},{8,9},{9,8},{10,11... | collective-permute-start | bytes 18874376 | tf_op jit(solution)/shard_map/ppermute | solution.py:291
  18.8 15.1 %collective-permute-start.8 = (bf16[128,2176]{1,0:T(8,128)(2,1)S(1)}, bf16[128,2176]{1,0:T(8,128)(2,1)S(1)}, u32[]{:S(2)}, u32[]{:S(2)}) collective-permute-start(bf16[128,2176]{1,0:T(8,128)(2,1)S(1)} %pad_maximum_fusion), channel_id=1, source_target_pairs={{0,4},{1,5},{2,6},{3,7},{4,0},{5,1},{6,2},{7,3},{8,12},{9,13},{10,... | collective-permute-start | bytes 1671176 | tf_op jit(solution)/shard_map/ppermute | solution.py:291
  19.7 8.8 %collective-permute-start.3 = (bf16[64,2176]{1,0:T(8,128)(2,1)S(1)}, bf16[64,2176]{1,0:T(8,128)(2,1)S(1)}, u32[]{:S(2)}, u32[]{:S(2)}) collective-permute-start(bf16[64,2176]{1,0:T(8,128)(2,1)S(1)} %collective-permute-done.2.refs_3_), channel_id=1, source_target_pairs={{0,16},{1,17},{2,18},{3,19},{4,20},{5,21},{6,22},{7,23},{8,24},{9,... | collective-permute-start | bytes 835592 | tf_op jit(solution)/shard_map/ppermute | solution.py:291
  21.2 9.5 %collective-permute-start.4 = (bf16[64,2176]{1,0:T(8,128)(2,1)S(1)}, bf16[64,2176]{1,0:T(8,128)(2,1)S(1)}, u32[]{:S(2)}, u32[]{:S(2)}) collective-permute-start(bf16[64,2176]{1,0:T(8,128)(2,1)S(1)} %collective-permute-done.2.refs_3_), channel_id=1, source_target_pairs={{0,2},{1,3},{2,0},{3,1},{4,6},{5,7},{6,4},{7,5},{8,10},{9,11},{10,... | collective-permute-start | bytes 835592 | tf_op jit(solution)/shard_map/ppermute | solution.py:291
  22.7 14.2 %collective-permute-start.5 = (bf16[64,2176]{1,0:T(8,128)(2,1)S(1)}, bf16[64,2176]{1,0:T(8,128)(2,1)S(1)}, u32[]{:S(2)}, u32[]{:S(2)}) collective-permute-start(bf16[64,2176]{1,0:T(8,128)(2,1)S(1)} %collective-permute-done.refs_0_), channel_id=1, source_target_pairs={{0,2},{1,3},{2,0},{3,1},{4,6},{5,7},{6,4},{7,5},{8,10},{9,11},{10,... | collective-permute-start | bytes 835592 | tf_op jit(solution)/shard_map/ppermute | solution.py:291
  30.7 7.6 %collective-permute-start.6 = (bf16[64,2176]{1,0:T(8,128)(2,1)S(1)}, bf16[64,2176]{1,0:T(8,128)(2,1)S(1)}, u32[]{:S(2)}, u32[]{:S(2)}) collective-permute-start(bf16[64,2176]{1,0:T(8,128)(2,1)S(1)} %collective-permute-done.4.refs_5_), channel_id=1, source_target_pairs={{0,16},{1,17},{2,18},{3,19},{4,20},{5,21},{6,22},{7,23},{8,24},{9,... | collective-permute-start | bytes 835592 | tf_op jit(solution)/shard_map/ppermute | solution.py:291
  33.9 15.4 %collective-permute-start.9 = (bf16[128,2176]{1,0:T(8,128)(2,1)S(1)}, bf16[128,2176]{1,0:T(8,128)(2,1)S(1)}, u32[]{:S(2)}, u32[]{:S(2)}) collective-permute-start(bf16[128,2176]{1,0:T(8,128)(2,1)S(1)} %collective-permute-done.8.refs_3_), channel_id=1, source_target_pairs={{0,16},{1,17},{2,18},{3,19},{4,20},{5,21},{6,22},{7,23},{8,24},{9,... | collective-permute-start | bytes 1671176 | tf_op jit(solution)/shard_map/ppermute | solution.py:291
  35.4 14.0 %collective-permute-start.10 = (bf16[128,2176]{1,0:T(8,128)(2,1)S(1)}, bf16[128,2176]{1,0:T(8,128)(2,1)S(1)}, u32[]{:S(2)}, u32[]{:S(2)}) collective-permute-start(bf16[128,2176]{1,0:T(8,128)(2,1)S(1)} %collective-permute-done.8.refs_3_), channel_id=1, source_target_pairs={{0,2},{1,3},{2,0},{3,1},{4,6},{5,7},{6,4},{7,5},{8,10},{9,11},{10,... | collective-permute-start | bytes 1671176 | tf_op jit(solution)/shard_map/ppermute | solution.py:291
  38.4 12.7 %collective-permute-start.13 = (bf16[128,2176]{1,0:T(8,128)(2,1)S(1)}, bf16[128,2176]{1,0:T(8,128)(2,1)S(1)}, u32[]{:S(2)}, u32[]{:S(2)}) collective-permute-start(bf16[128,2176]{1,0:T(8,128)(2,1)S(1)} %pad_maximum_fusion.1), channel_id=1, source_target_pairs={{0,4},{1,5},{2,6},{3,7},{4,0},{5,1},{6,2},{7,3},{8,12},{9,13},{10,... | collective-permute-start | bytes 1671176 | tf_op jit(solution)/shard_map/ppermute | solution.py:291
  49.4 13.2 %collective-permute-start.11 = (bf16[128,2048]{1,0:T(8,128)(2,1)S(1)}, bf16[128,2048]{1,0:T(8,128)(2,1)S(1)}, u32[]{:S(2)}, u32[]{:S(2)}) collective-permute-start(bf16[128,2048]{1,0:T(8,128)(2,1)S(1)} %get-tuple-element.44), channel_id=1, source_target_pairs={{0,16},{1,17},{2,18},{3,19},{4,20},{5,21},{6,22},{7,23},{8,24},{9,... | collective-permute-start | bytes 1572872 | tf_op jit(solution)/shard_map/ppermute | solution.py:291
  49.8 12.5 %collective-permute-start.14 = (bf16[128,2048]{1,0:T(8,128)(2,1)S(1)}, bf16[128,2048]{1,0:T(8,128)(2,1)S(1)}, u32[]{:S(2)}, u32[]{:S(2)}) collective-permute-start(bf16[128,2048]{1,0:T(8,128)(2,1)S(1)} %get-tuple-element.47), channel_id=1, source_target_pairs={{0,4},{1,5},{2,6},{3,7},{4,0},{5,1},{6,2},{7,3},{8,12},{9,13},{10,... | collective-permute-start | bytes 1572872 | tf_op jit(solution)/shard_map/ppermute | solution.py:291
  51.1 14.6 %collective-permute-start.12 = (bf16[128,2048]{1,0:T(8,128)(2,1)S(1)}, bf16[128,2048]{1,0:T(8,128)(2,1)S(1)}, u32[]{:S(2)}, u32[]{:S(2)}) collective-permute-start(bf16[128,2048]{1,0:T(8,128)(2,1)S(1)} %get-tuple-element.46), channel_id=1, source_target_pairs={{0,2},{1,3},{2,0},{3,1},{4,6},{5,7},{6,4},{7,5},{8,10},{9,11},{10,... | collective-permute-start | bytes 1572872 | tf_op jit(solution)/shard_map/ppermute | solution.py:291
  62.5 9.3 %collective-permute-start.15 = (bf16[64,2048]{1,0:T(8,128)(2,1)S(1)}, bf16[64,2048]{1,0:T(8,128)(2,1)S(1)}, u32[]{:S(2)}, u32[]{:S(2)}) collective-permute-start(bf16[64,2048]{1,0:T(8,128)(2,1)S(1)} %get-tuple-element.53), channel_id=1, source_target_pairs={{0,2},{1,3},{2,0},{3,1},{4,6},{5,7},{6,4},{7,5},{8,10},{9,11},{10,... | collective-permute-start | bytes 786440 | tf_op jit(solution)/shard_map/ppermute | solution.py:291
  64.1 7.8 %collective-permute-start.16 = (bf16[64,2048]{1,0:T(8,128)(2,1)S(1)}, bf16[64,2048]{1,0:T(8,128)(2,1)S(1)}, u32[]{:S(2)}, u32[]{:S(2)}) collective-permute-start(bf16[64,2048]{1,0:T(8,128)(2,1)S(1)} %get-tuple-element.55), channel_id=1, source_target_pairs={{0,16},{1,17},{2,18},{3,19},{4,20},{5,21},{6,22},{7,23},{8,24},{9,... | collective-permute-start | bytes 786440 | tf_op jit(solution)/shard_map/ppermute | solution.py:291
  65.6 11.8 %collective-permute-start.18 = (bf16[64,2048]{1,0:T(8,128)(2,1)S(1)}, bf16[64,2048]{1,0:T(8,128)(2,1)S(1)}, u32[]{:S(2)}, u32[]{:S(2)}) collective-permute-start(bf16[64,2048]{1,0:T(8,128)(2,1)S(1)} %get-tuple-element.58), channel_id=1, source_target_pairs={{0,2},{1,3},{2,0},{3,1},{4,6},{5,7},{6,4},{7,5},{8,10},{9,11},{10,... | collective-permute-start | bytes 786440 | tf_op jit(solution)/shard_map/ppermute | solution.py:291
  66.3 18.9 %collective-permute-start.20 = (bf16[64,2048]{1,0:T(8,128)(2,1)S(1)}, bf16[64,2048]{1,0:T(8,128)(2,1)S(1)}, u32[]{:S(2)}, u32[]{:S(2)}) collective-permute-start(bf16[64,2048]{1,0:T(8,128)(2,1)S(1)} %add_convert_fusion.3), channel_id=1, source_target_pairs={{0,8},{1,9},{2,10},{3,11},{4,12},{5,13},{6,14},{7,15},{8,0},{9,1},... | collective-permute-start | bytes 786440 | tf_op jit(solution)/shard_map/ppermute | solution.py:291
  71.9 7.0 %collective-permute-start.17 = (bf16[64,2048]{1,0:T(8,128)(2,1)S(1)}, bf16[64,2048]{1,0:T(8,128)(2,1)S(1)}, u32[]{:S(2)}, u32[]{:S(2)}) collective-permute-start(bf16[64,2048]{1,0:T(8,128)(2,1)S(1)} %add_convert_fusion.6), channel_id=1, source_target_pairs={{0,16},{1,17},{2,18},{3,19},{4,20},{5,21},{6,22},{7,23},{8,24},{9,... | collective-permute-start | bytes 786440 | tf_op jit(solution)/shard_map/ppermute | solution.py:291
  73.0 8.7 %collective-permute-start.21 = (bf16[64,2048]{1,0:T(8,128)(2,1)S(1)}, bf16[64,2048]{1,0:T(8,128)(2,1)S(1)}, u32[]{:S(2)}, u32[]{:S(2)}) collective-permute-start(bf16[64,2048]{1,0:T(8,128)(2,1)S(1)} %get-tuple-element.63), channel_id=1, source_target_pairs={{0,16},{1,17},{2,18},{3,19},{4,20},{5,21},{6,22},{7,23},{8,24},{9,... | collective-permute-start | bytes 786440 | tf_op jit(solution)/shard_map/ppermute | solution.py:291
  74.1 7.7 %collective-permute-start.22 = (bf16[64,2048]{1,0:T(8,128)(2,1)S(1)}, bf16[64,2048]{1,0:T(8,128)(2,1)S(1)}, u32[]{:S(2)}, u32[]{:S(2)}) collective-permute-start(bf16[64,2048]{1,0:T(8,128)(2,1)S(1)} %add_convert_fusion.2), channel_id=1, source_target_pairs={{0,2},{1,3},{2,0},{3,1},{4,6},{5,7},{6,4},{7,5},{8,10},{9,11},{10,... | collective-permute-start | bytes 786440 | tf_op jit(solution)/shard_map/ppermute | solution.py:291
  79.0 9.2 %collective-permute-start.19 = (bf16[64,2048]{1,0:T(8,128)(2,1)S(1)}, bf16[64,2048]{1,0:T(8,128)(2,1)S(1)}, u32[]{:S(2)}, u32[]{:S(2)}) collective-permute-start(bf16[64,2048]{1,0:T(8,128)(2,1)S(1)} %add_convert_fusion.4), channel_id=1, source_target_pairs={{0,4},{1,5},{2,6},{3,7},{4,0},{5,1},{6,2},{7,3},{8,12},{9,13},{10,... | collective-permute-start | bytes 786440 | tf_op jit(solution)/shard_map/ppermute | solution.py:291
  81.8 9.5 %collective-permute-start.23 = (bf16[64,2048]{1,0:T(8,128)(2,1)S(1)}, bf16[64,2048]{1,0:T(8,128)(2,1)S(1)}, u32[]{:S(2)}, u32[]{:S(2)}) collective-permute-start(bf16[64,2048]{1,0:T(8,128)(2,1)S(1)} %add_convert_fusion.1), channel_id=1, source_target_pairs={{0,12},{1,13},{2,14},{3,15},{4,8},{5,9},{6,10},{7,11},{8,4},{9,5},... | collective-permute-start | bytes 786440 | tf_op jit(solution)/shard_map/ppermute | solution.py:291
